TPU v7x, 32 devices: a whole 2x2x4 slice. The times are simulated.
32 devices in a mesh: groups: 2 (over x), seq: 16 (over z, y, core).
Axes of the slice: x: 2, y: 2, z: 4, core: 2. Of those that a mesh axis runs over, the one named last changes fastest.
Arguments:
- query_rows: bfloat16 [4096, 2048], P(('groups', 'seq')), parts along dimension 0, may hold values from -150 to 150
- key_rows: bfloat16 [4096, 256], P(('groups', 'seq')), parts along dimension 0, may hold values from -4.1 to 4.1
- value_rows: bfloat16 [4096, 256], P(('groups', 'seq')), parts along dimension 0, may hold values from -6 to 6
- sink_positions: int32 [32], P('groups'), parts along dimension 0, may hold values from 0 to 2047
- residual: bfloat16 [4096, 2880], P(('groups', 'seq')), parts along dimension 0, may hold values from -6 to 6
- out_proj: bfloat16 [2048, 2880], replicated, may hold values from -0.125 to 0.125
- norm_gain: float32 [2880], replicated, may hold values from 0.5 to 1.5
- expert_ids: int32 [4096, 4], P(('groups', 'seq')), parts along dimension 0, may hold values from 0 to 7, all different within a row; in each aligned block of 128 rows (0 to 127, 128 to 255, ...) at most 128 rows name the same one
- route_weights: float32 [4096, 4], P(('groups', 'seq')), parts along dimension 0, may hold values from 0.05 to 1
- gate_up: bfloat16 [16, 2880, 1440], P('seq'), may hold values from -0.109375 to 0.109375
- down_proj: bfloat16 [16, 720, 2880], P('seq'), may hold values from -0.15625 to 0.15625
Outputs:
- layer_out: bfloat16 [4096, 2880], P(('groups', 'seq')), parts along dimension 0
There are 2 independent parts, one for each index of `groups`. A program takes and returns all parts, laid end to end along the dimension named above; an argument that names none is the same for every part. Nothing has to cross between parts.
Inputs may be any that keep to these rules, and one draw needn't show every extreme that they name: `expert_ids`: each row names 4 different experts; in the rows of one index of seq no expert is named by more than 128 rows, a bound that some block reaches. `sink_positions`: positions may repeat.
All inputs are finite; a program needn't handle non-finite values.
Results may differ from a plain program's by a relative error of at most 0.013.
Values may be sent and summed in bfloat16 or wider, within the bound.
No kernel may reach another device: no remote copies, remote signals or barrier semaphores. Data moves between devices by JAX's collectives and lax.ppermute only.
A program may use at most 192 MiB of HBM per device.

v0:
```python
import functools

import jax
import jax.numpy as jnp
from jax import lax
from jax.experimental import pallas as pl
from jax.experimental.pallas import tpu as pltpu
from jax.sharding import PartitionSpec as P

Q_HEADS = 32
KV_HEADS = 4
HEAD_DIM = 64
WINDOW = 128
TOPK = 4
PLANE = 4
NEVER = -1e30
VMEM_BYTES = 56 * 1024 * 1024
HIDDEN_PART = 240
OUT_PART = 1024


def window_allowed(query_pos, key_pos):
    return (
        (key_pos[:, None] >= 0)
        & (key_pos[:, None] <= query_pos[None, :])
        & (key_pos[:, None] > query_pos[None, :] - WINDOW)
    )


def sink_allowed(sink_positions, query_pos):
    order = jnp.arange(sink_positions.shape[0], dtype=jnp.int32)
    repeated = jnp.any(
        (sink_positions[:, None] == sink_positions[None, :]) & (order[:, None] > order[None, :]),
        axis=1,
    )
    return (~repeated)[:, None] & (sink_positions[:, None] <= query_pos[None, :] - WINDOW)


def after(block, *earlier):
    return lax.optimization_barrier((block, earlier))[0]


def summed(block, axis, halo, later):
    shards = lax.axis_size(axis)
    step = 1
    while step < shards:
        reach = min(4, shards // step)
        parts = [
            lax.ppermute(block, axis, [(i, i ^ (step * m)) for i in range(shards)])
            for m in range(1, reach)
        ]
        for part in parts:
            block = block + part
        if step == 1:
            block, halo, later = lax.optimization_barrier((block, halo, later))
        step *= reach
    return block, halo, later


def even_rows(rows, most):
    return max(r for r in range(16, most + 1, 16) if rows % r == 0)


def attention_kernel(
    experts,
    query_t,
    keys,
    values,
    sinks,
    bias,
    residual_t,
    gain,
    ids_t,
    route_t,
    out_proj_t,
    hidden_ref,
    rows_ref,
    proj_v,
    att_v,
    sems,
):
    parts, part, heads_width = proj_v.shape
    width = parts * part
    tokens = query_t.shape[1]

    def proj_copy(r):
        at = pl.ds(pl.multiple_of(r * part, 16), part)
        return pltpu.make_async_copy(out_proj_t.at[at], proj_v.at[r], sems.at[r])

    for r in range(parts):
        proj_copy(r).start()
    group = Q_HEADS // KV_HEADS
    near = keys.shape[0]
    wide_bias = jnp.concatenate([bias[:, :]] * group, 1)
    scale = HEAD_DIM ** (-0.5)
    for g in range(KV_HEADS):
        lanes = slice(g * HEAD_DIM, (g + 1) * HEAD_DIM)
        value_lanes = slice((KV_HEADS + g) * HEAD_DIM, (KV_HEADS + g + 1) * HEAD_DIM)
        first = g * group * HEAD_DIM
        query = jnp.concatenate(
            [
                query_t[first + h * HEAD_DIM : first + (h + 1) * HEAD_DIM, :]
                for h in range(group)
            ],
            1,
        )
        near_scores = (
            jnp.dot(keys[:, lanes], query, preferred_element_type=jnp.float32) * scale
            + wide_bias[:near]
        )
        sink_scores = (
            jnp.dot(sinks[:, lanes], query, preferred_element_type=jnp.float32) * scale
            + wide_bias[near:]
        )
        largest = jnp.maximum(
            jnp.max(near_scores, axis=0, keepdims=True),
            jnp.max(sink_scores, axis=0, keepdims=True),
        )
        near_terms = jnp.exp(near_scores - largest)
        sink_terms = jnp.exp(sink_scores - largest)
        total = jnp.sum(near_terms, axis=0, keepdims=True) + jnp.sum(
            sink_terms, axis=0, keepdims=True
        )
        down = (((0,), (0,)), ((), ()))
        gathered = lax.dot_general(
            values[:, lanes],
            near_terms.astype(jnp.bfloat16),
            down,
            preferred_element_type=jnp.float32,
        ) + lax.dot_general(
            sinks[:, value_lanes],
            sink_terms.astype(jnp.bfloat16),
            down,
            preferred_element_type=jnp.float32,
        )
        gathered = (gathered / total).astype(jnp.bfloat16)
        for h in range(group):
            att_v[first + h * HEAD_DIM : first + (h + 1) * HEAD_DIM, :] = gathered[
                :, h * tokens : (h + 1) * tokens
            ]

    def project(r, squares):
        proj_copy(r).wait()
        rows = pl.ds(pl.multiple_of(r * part, 16), part)
        state = (
            jnp.dot(proj_v[r], att_v[:, :], preferred_element_type=jnp.float32)
            + residual_t[rows, :].astype(jnp.float32)
        ).astype(jnp.bfloat16)
        hidden_ref[rows, :] = state
        state = state.astype(jnp.float32)
        return squares + jnp.sum(state * state, axis=0, keepdims=True)

    squares = lax.fori_loop(0, parts, project, jnp.zeros((1, tokens), jnp.float32))
    inverse = lax.rsqrt(squares / width + 1e-05)
    for r in range(parts):
        rows = slice(r * part, (r + 1) * part)
        rows_ref[rows, :] = (
            hidden_ref[rows, :].astype(jnp.float32) * inverse * gain[rows, :]
        ).astype(jnp.bfloat16)
    expert = lax.broadcasted_iota(jnp.int32, (experts, tokens), 0)
    weight = jnp.zeros((experts, tokens), jnp.float32)
    for k in range(TOPK):
        weight = weight + jnp.where(ids_t[k : k + 1, :] == expert, route_t[k : k + 1, :], 0.0)
    high = weight.astype(jnp.bfloat16).astype(jnp.float32)
    rows_ref[width:, :] = jnp.concatenate([high, weight - high], 0).astype(jnp.bfloat16)


def attended_rows(
    query_t, keys, values, sinks, bias, residual_t, gain, ids_t, route_t, out_proj_t, experts
):
    width, heads_width = out_proj_t.shape
    tokens = query_t.shape[1]
    part = even_rows(width, 480)
    parts = width // part
    vmem = pl.BlockSpec(memory_space=pltpu.VMEM)
    return pl.pallas_call(
        functools.partial(attention_kernel, experts),
        out_shape=(
            jax.ShapeDtypeStruct((width, tokens), jnp.bfloat16),
            jax.ShapeDtypeStruct((width + 2 * experts, tokens), jnp.bfloat16),
        ),
        in_specs=[vmem] * 9 + [pl.BlockSpec(memory_space=pl.ANY)],
        out_specs=(vmem, vmem),
        scratch_shapes=[
            pltpu.VMEM((parts, part, heads_width), jnp.bfloat16),
            pltpu.VMEM((heads_width, tokens), jnp.bfloat16),
            pltpu.SemaphoreType.DMA((parts,)),
        ],
        compiler_params=pltpu.CompilerParams(vmem_limit_bytes=VMEM_BYTES),
        cost_estimate=pl.CostEstimate(
            flops=2 * tokens * width * heads_width,
            bytes_accessed=2 * width * heads_width,
            transcendentals=tokens * Q_HEADS * bias.shape[0],
        ),
    )(query_t, keys, values, sinks, bias, residual_t, gain, ids_t, route_t, out_proj_t)


def expert_kernel(experts, me_ref, x_ref, y_ref, gu0, gu1, dn0, dn1, *refs):
    *out_refs, rows, units, gu_v, dn_v, gu_sems, dn_sems = refs
    hidden = units.shape[1]
    width = gu_v.shape[4]
    tokens = x_ref.shape[1]
    parts, part = gu_v.shape[2:4]

    def gate_up_copy(half, side, k):
        source = (gu0, gu1)[half].at[pl.ds(pl.multiple_of(side * hidden + k * part, 16), part)]
        return pltpu.make_async_copy(source, gu_v.at[half, side, k], gu_sems.at[half, side, k])

    def down_copy(half, k):
        at = pl.ds(pl.multiple_of(k * part, 16), part)
        source = (dn0, dn1)[half].at[at]
        return pltpu.make_async_copy(source, dn_v.at[half, at], dn_sems.at[half, k])

    for k in range(parts):
        gate_up_copy(0, 0, k).start()
        gate_up_copy(0, 1, k).start()
    rows[:, :tokens] = x_ref[:, :]
    rows[:, tokens:] = y_ref[:, :]

    def step(half, k):
        gate_up_copy(half, 0, k).wait()
        gate_up_copy(half, 1, k).wait()
        if half == 0:
            gate_up_copy(1, 0, k).start()
            gate_up_copy(1, 1, k).start()
            down_copy(0, k).start()
        else:
            down_copy(1, k).start()
        gate, up = (
            jnp.dot(gu_v[half, side, k], rows[:width, :], preferred_element_type=jnp.float32)
            for side in range(2)
        )
        units[half, pl.ds(pl.multiple_of(k * part, 16), part), :] = (
            gate / (1.0 + jnp.exp(-gate)) * up
        ).astype(jnp.bfloat16)

    for half in range(2):
        pl.loop(0, parts)(functools.partial(step, half))
    extra = rows[width:, :].astype(jnp.float32)
    place = lax.broadcasted_iota(jnp.int32, extra.shape, 0)
    mine = (place == me_ref[0]) | (place == experts + me_ref[0])
    weight = jnp.sum(jnp.where(mine, extra, 0.0), axis=0, keepdims=True)
    for half in range(2):
        for k in range(parts):
            down_copy(half, k).wait()
    for first in range(0, width, OUT_PART):
        at = slice(first, min(first + OUT_PART, width))
        total = (product(dn_v[0, :, at], units[0]) + product(dn_v[1, :, at], units[1])) * weight
        out_refs[0][at, :] = total[:, :tokens].astype(out_refs[0].dtype)
        out_refs[1][at, :] = total[:, tokens:].astype(out_refs[1].dtype)


def product(down, units):
    return lax.dot_general(
        down, units, (((0,), (0,)), ((), ())), preferred_element_type=jnp.float32
    )


def expert_rows(me, x, y, weights, experts, kinds):
    gu0, gu1, dn0, dn1 = weights
    tokens = x.shape[1]
    hidden, width = gu0.shape[0] // 2, gu0.shape[1]
    part = even_rows(hidden, HIDDEN_PART)
    parts = hidden // part
    vmem = pl.BlockSpec(memory_space=pltpu.VMEM)
    hbm = pl.BlockSpec(memory_space=pl.ANY)
    return pl.pallas_call(
        functools.partial(expert_kernel, experts),
        out_shape=[jax.ShapeDtypeStruct((width, tokens), kind) for kind in kinds],
        in_specs=[pl.BlockSpec(memory_space=pltpu.SMEM), vmem, vmem, hbm, hbm, hbm, hbm],
        out_specs=[vmem] * len(kinds),
        scratch_shapes=[
            pltpu.VMEM((x.shape[0], 2 * tokens), jnp.bfloat16),
            pltpu.VMEM((2, hidden, 2 * tokens), jnp.bfloat16),
            pltpu.VMEM((2, 2, parts, part, width), jnp.bfloat16),
            pltpu.VMEM((2,) + dn0.shape, jnp.bfloat16),
            pltpu.SemaphoreType.DMA((2, 2, parts)),
            pltpu.SemaphoreType.DMA((2, parts)),
        ],
        compiler_params=pltpu.CompilerParams(vmem_limit_bytes=VMEM_BYTES),
        cost_estimate=pl.CostEstimate(
            flops=2 * 2 * tokens * 2 * 3 * width * hidden,
            bytes_accessed=2 * 2 * (gu0.size + dn0.size),
            transcendentals=4 * tokens * hidden,
        ),
    )(me, x, y, gu0, gu1, dn0, dn1)


def line_pairs(moves):
    return [(PLANE * p + r, PLANE * q + r) for p, q in moves for r in range(PLANE)]


def column_pairs(planes):
    return [(PLANE * p + r, (PLANE * p + r) ^ 2) for p in range(planes) for r in range(PLANE)]


def sources(planes):
    return [
        sorted(
            (q for q in range(planes) if q != p),
            key=lambda q: (abs(q - p), -(planes - p if q > p else p)),
        )
        for p in range(planes)
    ]


def rounds(moves):
    lists = []
    for p, q in moves:
        for held in lists:
            if all(q != to for _, to in held):
                held.append((p, q))
                break
        else:
            lists.append([(p, q)])
    return lists


def next_blocks(held, distance, planes):
    up = [(p, p + 1) for p in range(distance - 1, planes - 1)]
    down = [(p, p - 1) for p in range(1, planes - distance + 1)]
    if len(held) == 1 and distance > 1:
        return [lax.ppermute(held[0], "seq", line_pairs(up + down))]
    below, above = held if len(held) == 2 else held * 2
    return [
        lax.ppermute(below, "seq", line_pairs(up)),
        lax.ppermute(above, "seq", line_pairs(down)),
    ]


def slot_block(arrivals, plane, origins):
    chosen = {}
    for p, q in enumerate(origins):
        blocks = arrivals[abs(q - p)]
        block = blocks[0] if len(blocks) == 1 or q < p else blocks[1]
        chosen.setdefault(id(block), (block, []))[1].append(p)
    (result, _), *others = chosen.values()
    for block, holders in others:
        here = functools.reduce(jnp.logical_or, [plane == p for p in holders])
        result = jnp.where(here, block, result)
    return result


def on_device(
    query_rows,
    key_rows,
    value_rows,
    sink_positions,
    residual,
    out_proj,
    norm_gain,
    expert_ids,
    route_weights,
    gate_up,
    down_proj,
):
    rows_dev = query_rows.shape[0]
    width = residual.shape[1]
    shards = lax.axis_size("seq")
    planes = shards // PLANE
    experts = shards // 2
    my_index = lax.axis_index("seq")
    plane = my_index // PLANE
    first_pos = my_index * rows_dev
    own_pos = first_pos + jnp.arange(rows_dev, dtype=jnp.int32)

    local_rows = jnp.concatenate([key_rows, value_rows], 1)
    halo_rows = lax.ppermute(local_rows, "seq", [(i, i + 1) for i in range(shards - 1)])
    pick_rows = (sink_positions[:, None] == own_pos[None, :]).astype(jnp.bfloat16)
    sink_rows = jnp.dot(pick_rows, local_rows, preferred_element_type=jnp.float32)
    later = (query_rows, norm_gain, sink_positions)
    sink_rows, halo_rows, later = summed(
        sink_rows.astype(jnp.bfloat16), "seq", halo_rows, later
    )
    query_rows, norm_gain, sink_positions = later

    to_core = [(i, i ^ 1) for i in range(shards)]
    gu_own = jnp.swapaxes(gate_up[0], 0, 1)
    dn_own = down_proj[0]
    gu_other = lax.ppermute(gu_own, "seq", to_core)
    dn_other = lax.ppermute(dn_own, "seq", to_core)
    weights = (gu_own, gu_other, dn_own, dn_other)

    joined = jnp.concatenate([halo_rows, local_rows], 0)
    keys_joined = joined[:, : key_rows.shape[1]]
    values_joined = joined[:, key_rows.shape[1] :]
    key_pos = first_pos - WINDOW + jnp.arange(rows_dev + WINDOW, dtype=jnp.int32)
    allowed = jnp.concatenate(
        [window_allowed(own_pos, key_pos), sink_allowed(sink_positions, own_pos)], 0
    )
    bias = jnp.where(allowed, 0.0, NEVER).astype(jnp.float32)
    hidden_state, own = attended_rows(
        query_rows.T,
        keys_joined,
        values_joined,
        sink_rows,
        bias,
        residual.T,
        norm_gain[:, None],
        expert_ids.T,
        route_weights.T,
        out_proj.T,
        experts,
    )

    me = (my_index // 2).reshape(1)
    across = column_pairs(planes)
    order = sources(planes)
    expert = functools.partial(expert_rows, me)
    half = jnp.bfloat16

    held = next_blocks([own], 1, planes)
    arrivals = {1: held}
    cross = lax.ppermute(own, "seq", across)
    block, ready = own, (cross, *held)
    sums = []
    for j in range(1, planes):
        nearer = [after(x, *ready) for x in arrivals[j]]
        next_block = after(slot_block(arrivals, plane, [o[j - 1] for o in order]), *ready)
        next_cross = lax.ppermute(next_block, "seq", across)
        if j + 1 < planes:
            held = next_blocks(nearer, j + 1, planes)
        else:
            held = []
        flows = []
        if j == 1:
            mine, theirs = expert(block, cross, weights, experts, (jnp.float32, jnp.float32))
            column_sum = hidden_state.astype(jnp.float32) + mine
            cross_sum = theirs
            done = mine
        elif j == 2:
            near = expert(block, cross, weights, experts, (half, half))
            done = near[0]
        else:
            if j == 3:
                flows = [(0, near[0])]
            elif j == 4:
                flows = [(1, near[1])]
            sums.append((j - 1, expert(block, cross, weights, experts, (jnp.float32, half))))
            done = sums[-1][1][1]
        backs = []
        for side, part in flows:
            part = after(part, *ready)
            for moves in rounds([(p, o[0]) for p, o in enumerate(order)]):
                backs.append((side, lax.ppermute(part, "seq", line_pairs(moves))))
        for side, back in backs:
            if side == 0:
                column_sum = column_sum + back.astype(jnp.float32)
            else:
                cross_sum = cross_sum + back.astype(jnp.float32)
        block, cross = next_block, next_cross
        ready = (next_cross, done, *held, *[back for _, back in backs])
        if held:
            held = [after(x, *ready) for x in held]
            if len(held) == 2 and 2 * (j + 1) >= planes:
                held = [jnp.where(plane >= j + 1, held[0], held[1])]
            arrivals[j + 1] = held
    last = planes - 1
    parts = expert(block, cross, weights, experts, (jnp.float32, half))
    sums.append((last, parts))
    pending = None
    for n, (j, (mine, theirs)) in enumerate(sums):
        theirs = after(theirs, *ready)
        returned = lax.ppermute(theirs, "seq", across)
        backs = []
        if n == 0 and planes <= 4:
            part = after(near[1], *ready)
            for moves in rounds([(p, o[0]) for p, o in enumerate(order)]):
                back = lax.ppermute(part, "seq", line_pairs(moves))
                cross_sum = cross_sum + back.astype(jnp.float32)
                backs.append(back)
        if pending is not None:
            k, both = pending
            for moves in rounds([(p, o[k - 1]) for p, o in enumerate(order)]):
                back = lax.ppermute(both, "seq", line_pairs(moves))
                column_sum = column_sum + back.astype(jnp.float32)
        pending = (j, (mine + returned.astype(jnp.float32)).astype(half))
        ready = (returned, *backs)
    crossing = lax.ppermute(after(cross_sum.astype(half), *ready), "seq", across)
    k, both = pending
    for moves in rounds([(p, o[k - 1]) for p, o in enumerate(order)]):
        back = lax.ppermute(both, "seq", line_pairs(moves))
        column_sum = column_sum + back.astype(jnp.float32)
    return (column_sum + crossing.astype(jnp.float32)).astype(half).T


def solution(mesh):
    in_specs = (
        P(("groups", "seq"), None),
        P(("groups", "seq"), None),
        P(("groups", "seq"), None),
        P("groups"),
        P(("groups", "seq"), None),
        P(),
        P(),
        P(("groups", "seq"), None),
        P(("groups", "seq"), None),
        P("seq", None, None),
        P("seq", None, None),
    )
    out_specs = P(("groups", "seq"), None)
    return jax.shard_map(
        on_device, mesh=mesh, in_specs=in_specs, out_specs=out_specs, check_vma=False
    )
```

profile of v0, /device:TPU:0, one launch (start us, length us, event | category | flops | bytes accessed | tf_op | source)
XLA Modules:
  0.0 192.1 jit_solution(9279879341654561631)
XLA Ops:
  0.5 0.8 constant_dynamic-update-slice_fusion.1
  1.4 0.8 constant_dynamic-update-slice_fusion
  2.2 0.8 convolution_convert_fusion
  3.1 2.6 %collective-permute-start.2 = (bf16[16,512]{1,0:T(8,128)(2,1)S(1)}, bf16[16,512]{1,0:T(8,128)(2,1)S(1)}, u32[]{:S(2)}, u32[]{:S(2)}) collective-permute-start(bf16[16,512]{1,0:T(8,128)(2,1)S(1)} %convolution_convert_fusion), channel_id=1, source_target_pairs={{0,3},{1,2},{2,1},{3,0},{4,7},{5,6},{6,5},{7,4},{8,11},{9,10},{10,... | collective-permute-start | bytes 49160 | tf_op jit(solution)/shard_map/ppermute | solution.py:49
  6.3 0.8 collective-permute-done.2
  7.1 2.3 %collective-permute-start.3 = (bf16[128,512]{1,0:T(8,128)(2,1)S(1)}, bf16[128,512]{1,0:T(8,128)(2,1)S(1)}, u32[]{:S(2)}, u32[]{:S(2)}) collective-permute-start(bf16[128,512]{1,0:T(8,128)(2,1)S(1)} %constant_dynamic-update-slice_fusion), channel_id=1, source_target_pairs={{0,1},{1,2},{2,3},{3,4},{4,5},{5,6},{6,7},{7,8},{8,9},{9,10},{10,1... | collective-permute-start | bytes 393224 | tf_op jit(solution)/shard_map/ppermute | solution.py:368
  9.5 3.9 %collective-permute-done = bf16[16,512]{1,0:T(8,128)(2,1)S(1)} collective-permute-done((bf16[16,512]{1,0:T(8,128)(2,1)S(1)}, bf16[16,512]{1,0:T(8,128)(2,1)S(1)}, u32[]{:S(2)}, u32[]{:S(2)}) %collective-permute-start) | collective-permute-done | bytes 16416 | tf_op jit(solution)/shard_map/ppermute | solution.py:49
  13.8 4.7 %collective-permute-start.6 = (bf16[16,512]{1,0:T(8,128)(2,1)S(1)}, bf16[16,512]{1,0:T(8,128)(2,1)S(1)}, u32[]{:S(2)}, u32[]{:S(2)}) collective-permute-start(bf16[16,512]{1,0:T(8,128)(2,1)S(1)} %add_add_fusion.1), channel_id=1, source_target_pairs={{0,12},{1,13},{2,14},{3,15},{4,8},{5,9},{6,10},{7,11},{8,4},{9,5},... | collective-permute-start | bytes 49160 | tf_op jit(solution)/shard_map/ppermute | solution.py:49
  18.5 0.6 collective-permute-start.4
  19.1 0.9 fusion.3
  20.0 0.7 pad_maximum_fusion
  20.8 0.7 compare_and_fusion.1
  21.5 0.7 add_select_fusion.bias
  22.2 1.0 copy.15
  23.2 1.5 broadcast_in_dim.11.gain
  24.7 0.6 add_add_fusion.sinks
  25.3 9.7 %shard_map.109 = (bf16[2880,128]{1,0:T(8,128)(2,1)}, bf16[2896,128]{1,0:T(8,128)(2,1)}) custom-call(bf16[2048,128]{1,0:T(8,128)(2,1)} %bitcast.24, bf16[256,256]{1,0:T(8,128)(2,1)} %get-tuple-element.66.keys, bf16[256,256]{1,0:T(8,128)(2,1)} %get-tuple-element.65.values, bf16[16,512]{1,0:T(8,128)(2,1)} %add_add_fusion.sinks, ...), custom_call_target="tpu_custom_call" | custom-call | flops 1509949440 | bytes 11796480 | tf_op jit(solution)/shard_map/pallas_call | solution.py:176
  35.0 3.3 %collective-permute-start.10 = (bf16[2896,128]{1,0:T(8,128)(2,1)}, bf16[2896,128]{1,0:T(8,128)(2,1)S(1)}, u32[]{:S(2)}, u32[]{:S(2)}) collective-permute-start(bf16[2896,128]{1,0:T(8,128)(2,1)} %get-tuple-element.40.x_ref), channel_id=1, source_target_pairs={{0,4},{1,5},{2,6},{3,7},{4,8},{5,9},{6,10},{7,11},{8,12},{9,13},{1... | collective-permute-start | bytes 2224136 | tf_op jit(solution)/shard_map/ppermute | solution.py:326
  38.4 1.3 collective-permute-start.11
  39.7 1.6 collective-permute-start.7
  41.3 13.1 %collective-permute-done.10 = bf16[2896,128]{1,0:T(8,128)(2,1)S(1)} collective-permute-done((bf16[2896,128]{1,0:T(8,128)(2,1)}, bf16[2896,128]{1,0:T(8,128)(2,1)S(1)}, u32[]{:S(2)}, u32[]{:S(2)}) %collective-permute-start.10) | collective-permute-done | bytes 741408 | tf_op jit(solution)/shard_map/ppermute | solution.py:326
  54.4 4.1 %collective-permute-done.11 = bf16[2896,128]{1,0:T(8,128)(2,1)S(1)} collective-permute-done((bf16[2896,128]{1,0:T(8,128)(2,1)}, bf16[2896,128]{1,0:T(8,128)(2,1)S(1)}, u32[]{:S(2)}, u32[]{:S(2)}) %collective-permute-start.11) | collective-permute-done | bytes 741408 | tf_op jit(solution)/shard_map/ppermute | solution.py:327
  58.5 1.6 collective-permute-start.12
  60.1 1.5 collective-permute-start.13
  61.7 1.3 collective-permute-start.14
  63.0 14.2 %shard_map.110 = (f32[2880,128]{1,0:T(8,128)}, f32[2880,128]{1,0:T(8,128)}) custom-call(s32[1]{0:T(128)} %bitcast.5.me_ref, bf16[2896,128]{1,0:T(8,128)(2,1)} %get-tuple-element.40.x_ref, bf16[2896,128]{1,0:T(8,128)(2,1)} %copy-done.7, bf16[1440,2880]{1,0:T(8,128)(2,1)} %bitcast.14, bf16[1440,2880]{1,0:T(8,128)(2,1)} %collective-permute-done.8.gu1, ...), custom_call_target="tpu_custom_call" | custom-call | flops 6370099200 | bytes 24883200 | tf_op jit(solution)/shard_map/pallas_call | solution.py:267
  77.2 5.3 %collective-permute-done.14 = bf16[2896,128]{1,0:T(8,128)(2,1)} collective-permute-done((bf16[2896,128]{1,0:T(8,128)(2,1)S(1)}, bf16[2896,128]{1,0:T(8,128)(2,1)}, u32[]{:S(2)}, u32[]{:S(2)}) %collective-permute-start.14) | collective-permute-done | bytes 741408 | tf_op jit(solution)/shard_map/ppermute | solution.py:327
  82.5 1.4 select_select_fusion
  83.9 1.5 collective-permute-start.16
  86.0 13.7 %shard_map.111 = (bf16[2880,128]{1,0:T(8,128)(2,1)}, bf16[2880,128]{1,0:T(8,128)(2,1)}) custom-call(s32[1]{0:T(128)} %bitcast.5.me_ref, bf16[2896,128]{1,0:T(8,128)(2,1)} %copy-done, bf16[2896,128]{1,0:T(8,128)(2,1)} %collective-permute-done.12.y_ref, bf16[1440,2880]{1,0:T(8,128)(2,1)} %bitcast.15, bf16[1440,2880]{1,0:T(8,128)(2,1)} %collective-permute-done.8.gu1, ...), custom_call_target="tpu_custom_call" | custom-call | flops 6370099200 | bytes 24883200 | tf_op jit(solution)/shard_map/pallas_call | solution.py:267
  99.7 1.6 collective-permute-done.16
  102.3 4.7 %collective-permute-start.17 = (bf16[2880,128]{1,0:T(8,128)(2,1)S(1)}, bf16[2880,128]{1,0:T(8,128)(2,1)S(1)}, u32[]{:S(2)}, u32[]{:S(2)}) collective-permute-start(bf16[2880,128]{1,0:T(8,128)(2,1)S(1)} %copy-done.14), channel_id=1, source_target_pairs={{0,4},{1,5},{2,6},{3,7},{4,8},{5,9},{6,10},{7,11},{16,20},{17,21},... | collective-permute-start | bytes 2211848 | tf_op jit(solution)/shard_map/ppermute | solution.py:445
  107.0 0.7 collective-permute-start.18
  107.7 13.9 %shard_map.112 = (f32[2880,128]{1,0:T(8,128)}, bf16[2880,128]{1,0:T(8,128)(2,1)}) custom-call(s32[1]{0:T(128)} %bitcast.5.me_ref, bf16[2896,128]{1,0:T(8,128)(2,1)} %copy-done.2, bf16[2896,128]{1,0:T(8,128)(2,1)} %copy-done.9, bf16[1440,2880]{1,0:T(8,128)(2,1)} %bitcast.16, bf16[1440,2880]{1,0:T(8,128)(2,1)} %collective-permute-done.8.gu1, ...), custom_call_target="tpu_custom_call" | custom-call | flops 6370099200 | bytes 24883200 | tf_op jit(solution)/shard_map/pallas_call | solution.py:267
  121.7 0.8 collective-permute-start.23
  122.6 4.1 %collective-permute-start.22 = (bf16[2880,128]{1,0:T(8,128)(2,1)S(1)}, bf16[2880,128]{1,0:T(8,128)(2,1)S(1)}, u32[]{:S(2)}, u32[]{:S(2)}) collective-permute-start(bf16[2880,128]{1,0:T(8,128)(2,1)S(1)} %copy-done.13), channel_id=1, source_target_pairs={{0,4},{1,5},{2,6},{3,7},{4,8},{5,9},{6,10},{7,11},{16,20},{17,21},... | collective-permute-start | bytes 2211848 | tf_op jit(solution)/shard_map/ppermute | solution.py:469
  126.7 1.5 collective-permute-start.20
  128.2 14.0 %shard_map.113 = (f32[2880,128]{1,0:T(8,128)}, bf16[2880,128]{1,0:T(8,128)(2,1)}) custom-call(s32[1]{0:T(128)} %bitcast.5.me_ref, bf16[2896,128]{1,0:T(8,128)(2,1)} %copy-done.1, bf16[2896,128]{1,0:T(8,128)(2,1)} %copy-done.8, bf16[1440,2880]{1,0:T(8,128)(2,1)} %bitcast.17, bf16[1440,2880]{1,0:T(8,128)(2,1)} %collective-permute-done.8.gu1, ...), custom_call_target="tpu_custom_call" | custom-call | flops 6370099200 | bytes 24883200 | tf_op jit(solution)/shard_map/pallas_call | solution.py:267
  142.2 0.7 collective-permute-start.24
  143.1 2.1 %collective-permute-start.21 = (bf16[2880,128]{1,0:T(8,128)(2,1)S(1)}, bf16[2880,128]{1,0:T(8,128)(2,1)S(1)}, u32[]{:S(2)}, u32[]{:S(2)}) collective-permute-start(bf16[2880,128]{1,0:T(8,128)(2,1)S(1)} %add_convert_fusion.3), channel_id=1, source_target_pairs={{0,8},{1,9},{2,10},{3,11},{4,0},{5,1},{6,2},{7,3},{8,12},{9,13},{1... | collective-permute-start | bytes 2211848 | tf_op jit(solution)/shard_map/ppermute | solution.py:475
  145.5 13.1 %collective-permute-done.24 = bf16[2880,128]{1,0:T(8,128)(2,1)S(1)} collective-permute-done((bf16[2880,128]{1,0:T(8,128)(2,1)}, bf16[2880,128]{1,0:T(8,128)(2,1)S(1)}, u32[]{:S(2)}, u32[]{:S(2)}) %collective-permute-start.24) | collective-permute-done | bytes 737312 | tf_op jit(solution)/shard_map/ppermute | solution.py:464
  158.6 1.2 collective-permute-start.27
  159.9 1.4 collective-permute-start.26
  161.3 6.3 %collective-permute-start.25 = (bf16[2880,128]{1,0:T(8,128)(2,1)S(1)}, bf16[2880,128]{1,0:T(8,128)(2,1)S(1)}, u32[]{:S(2)}, u32[]{:S(2)}) collective-permute-start(bf16[2880,128]{1,0:T(8,128)(2,1)S(1)} %add_convert_fusion.2), channel_id=1, source_target_pairs={{0,12},{1,13},{2,14},{3,15},{8,0},{9,1},{10,2},{11,3},{16,28},{17,... | collective-permute-start | bytes 2211848 | tf_op jit(solution)/shard_map/ppermute | solution.py:482
  167.7 4.0 %collective-permute-done.27 = bf16[2880,128]{1,0:T(8,128)(2,1)S(1)} collective-permute-done((bf16[2880,128]{1,0:T(8,128)(2,1)S(1)}, bf16[2880,128]{1,0:T(8,128)(2,1)S(1)}, u32[]{:S(2)}, u32[]{:S(2)}) %collective-permute-start.27) | collective-permute-done | bytes 737312 | tf_op jit(solution)/shard_map/ppermute | solution.py:479
  171.7 3.5 %collective-permute-done.26 = bf16[2880,128]{1,0:T(8,128)(2,1)S(1)} collective-permute-done((bf16[2880,128]{1,0:T(8,128)(2,1)S(1)}, bf16[2880,128]{1,0:T(8,128)(2,1)S(1)}, u32[]{:S(2)}, u32[]{:S(2)}) %collective-permute-start.26) | collective-permute-done | bytes 737312 | tf_op jit(solution)/shard_map/ppermute | solution.py:482
  175.2 15.3 %collective-permute-done.25 = bf16[2880,128]{1,0:T(8,128)(2,1)S(1)} collective-permute-done((bf16[2880,128]{1,0:T(8,128)(2,1)S(1)}, bf16[2880,128]{1,0:T(8,128)(2,1)S(1)}, u32[]{:S(2)}, u32[]{:S(2)}) %collective-permute-start.25) | collective-permute-done | bytes 737312 | tf_op jit(solution)/shard_map/ppermute | solution.py:482
  190.5 1.6 fusion
  (67 shorter events, 3.8 us)
Async XLA Ops:
  0.0 22.2 %copy-start.11 = (bf16[128,2048]{1,0:T(8,128)(2,1)S(1)}, bf16[128,2048]{1,0:T(8,128)(2,1)}, u32[]{:S(2)}) copy-start(bf16[128,2048]{1,0:T(8,128)(2,1)} %param.11) | copy-start | bytes 1572868
  0.0 23.2 %copy-start.12 = (f32[2880]{0:T(1024)S(1)}, f32[2880]{0:T(1024)}, u32[]{:S(2)}) copy-start(f32[2880]{0:T(1024)} %param.17) | copy-start | bytes 34564
  0.0 63.0 %collective-permute-start.8 = (bf16[1440,2880]{1,0:T(8,128)(2,1)}, bf16[1440,2880]{1,0:T(8,128)(2,1)}, u32[]{:S(2)}, u32[]{:S(2)}) collective-permute-start(bf16[1440,2880]{1,0:T(8,128)(2,1)} %bitcast.13), channel_id=1, source_target_pairs={{0,1},{1,0},{2,3},{3,2},{4,5},{5,4},{6,7},{7,6},{8,9},{9,8},{10,11... | collective-permute-start | bytes 24883208 | tf_op jit(solution)/shard_map/ppermute | solution.py:380
  0.5 62.5 %collective-permute-start.9 = (bf16[720,2880]{1,0:T(8,128)(2,1)}, bf16[720,2880]{1,0:T(8,128)(2,1)}, u32[]{:S(2)}, u32[]{:S(2)}) collective-permute-start(bf16[720,2880]{1,0:T(8,128)(2,1)} %bitcast.18), channel_id=1, source_target_pairs={{0,1},{1,0},{2,3},{3,2},{4,5},{5,4},{6,7},{7,6},{8,9},{9,8},{10,11... | collective-permute-start | bytes 12441608 | tf_op jit(solution)/shard_map/ppermute | solution.py:381
  3.1 4.1 %collective-permute-start.2 = (bf16[16,512]{1,0:T(8,128)(2,1)S(1)}, bf16[16,512]{1,0:T(8,128)(2,1)S(1)}, u32[]{:S(2)}, u32[]{:S(2)}) collective-permute-start(bf16[16,512]{1,0:T(8,128)(2,1)S(1)} %convolution_convert_fusion), channel_id=1, source_target_pairs={{0,3},{1,2},{2,1},{3,0},{4,7},{5,6},{6,5},{7,4},{8,11},{9,10},{10,... | collective-permute-start | bytes 49160 | tf_op jit(solution)/shard_map/ppermute | solution.py:49
  5.7 3.8 %collective-permute-start.1 = (bf16[16,512]{1,0:T(8,128)(2,1)S(1)}, bf16[16,512]{1,0:T(8,128)(2,1)S(1)}, u32[]{:S(2)}, u32[]{:S(2)}) collective-permute-start(bf16[16,512]{1,0:T(8,128)(2,1)S(1)} %convolution_convert_fusion), channel_id=1, source_target_pairs={{0,2},{1,3},{2,0},{3,1},{4,6},{5,7},{6,4},{7,5},{8,10},{9,11},{10,... | collective-permute-start | bytes 49160 | tf_op jit(solution)/shard_map/ppermute | solution.py:49
  6.1 7.3 %collective-permute-start = (bf16[16,512]{1,0:T(8,128)(2,1)S(1)}, bf16[16,512]{1,0:T(8,128)(2,1)S(1)}, u32[]{:S(2)}, u32[]{:S(2)}) collective-permute-start(bf16[16,512]{1,0:T(8,128)(2,1)S(1)} %convolution_convert_fusion), channel_id=1, source_target_pairs={{0,1},{1,0},{2,3},{3,2},{4,5},{5,4},{6,7},{7,6},{8,9},{9,8},{10,11... | collective-permute-start | bytes 49160 | tf_op jit(solution)/shard_map/ppermute | solution.py:49
  7.1 6.6 %collective-permute-start.3 = (bf16[128,512]{1,0:T(8,128)(2,1)S(1)}, bf16[128,512]{1,0:T(8,128)(2,1)S(1)}, u32[]{:S(2)}, u32[]{:S(2)}) collective-permute-start(bf16[128,512]{1,0:T(8,128)(2,1)S(1)} %constant_dynamic-update-slice_fusion), channel_id=1, source_target_pairs={{0,1},{1,2},{2,3},{3,4},{4,5},{5,6},{6,7},{7,8},{8,9},{9,10},{10,1... | collective-permute-start | bytes 393224 | tf_op jit(solution)/shard_map/ppermute | solution.py:368
  13.8 10.9 %collective-permute-start.6 = (bf16[16,512]{1,0:T(8,128)(2,1)S(1)}, bf16[16,512]{1,0:T(8,128)(2,1)S(1)}, u32[]{:S(2)}, u32[]{:S(2)}) collective-permute-start(bf16[16,512]{1,0:T(8,128)(2,1)S(1)} %add_add_fusion.1), channel_id=1, source_target_pairs={{0,12},{1,13},{2,14},{3,15},{4,8},{5,9},{6,10},{7,11},{8,4},{9,5},... | collective-permute-start | bytes 49160 | tf_op jit(solution)/shard_map/ppermute | solution.py:49
  18.5 6.2 %collective-permute-start.5 = (bf16[16,512]{1,0:T(8,128)(2,1)S(1)}, bf16[16,512]{1,0:T(8,128)(2,1)S(1)}, u32[]{:S(2)}, u32[]{:S(2)}) collective-permute-start(bf16[16,512]{1,0:T(8,128)(2,1)S(1)} %add_add_fusion.1), channel_id=1, source_target_pairs={{0,8},{1,9},{2,10},{3,11},{4,12},{5,13},{6,14},{7,15},{8,0},{9,1},... | collective-permute-start | bytes 49160 | tf_op jit(solution)/shard_map/ppermute | solution.py:49
  18.5 6.2 %collective-permute-start.4 = (bf16[16,512]{1,0:T(8,128)(2,1)S(1)}, bf16[16,512]{1,0:T(8,128)(2,1)S(1)}, u32[]{:S(2)}, u32[]{:S(2)}) collective-permute-start(bf16[16,512]{1,0:T(8,128)(2,1)S(1)} %add_add_fusion.1), channel_id=1, source_target_pairs={{0,4},{1,5},{2,6},{3,7},{4,0},{5,1},{6,2},{7,3},{8,12},{9,13},{10,... | collective-permute-start | bytes 49160 | tf_op jit(solution)/shard_map/ppermute | solution.py:49
  35.0 19.3 %collective-permute-start.10 = (bf16[2896,128]{1,0:T(8,128)(2,1)}, bf16[2896,128]{1,0:T(8,128)(2,1)S(1)}, u32[]{:S(2)}, u32[]{:S(2)}) collective-permute-start(bf16[2896,128]{1,0:T(8,128)(2,1)} %get-tuple-element.40.x_ref), channel_id=1, source_target_pairs={{0,4},{1,5},{2,6},{3,7},{4,8},{5,9},{6,10},{7,11},{8,12},{9,13},{1... | collective-permute-start | bytes 2224136 | tf_op jit(solution)/shard_map/ppermute | solution.py:326
  38.4 20.0 %collective-permute-start.11 = (bf16[2896,128]{1,0:T(8,128)(2,1)}, bf16[2896,128]{1,0:T(8,128)(2,1)S(1)}, u32[]{:S(2)}, u32[]{:S(2)}) collective-permute-start(bf16[2896,128]{1,0:T(8,128)(2,1)} %get-tuple-element.40.x_ref), channel_id=1, source_target_pairs={{4,0},{5,1},{6,2},{7,3},{8,4},{9,5},{10,6},{11,7},{12,8},{13,9},{1... | collective-permute-start | bytes 2224136 | tf_op jit(solution)/shard_map/ppermute | solution.py:327
  39.7 18.9 %collective-permute-start.7 = (bf16[2896,128]{1,0:T(8,128)(2,1)}, bf16[2896,128]{1,0:T(8,128)(2,1)S(1)}, u32[]{:S(2)}, u32[]{:S(2)}) collective-permute-start(bf16[2896,128]{1,0:T(8,128)(2,1)} %get-tuple-element.40.x_ref), channel_id=1, source_target_pairs={{0,2},{1,3},{2,0},{3,1},{4,6},{5,7},{6,4},{7,5},{8,10},{9,11},{10,... | collective-permute-start | bytes 2224136 | tf_op jit(solution)/shard_map/ppermute | solution.py:414
  58.5 18.7 %copy-start = (bf16[2896,128]{1,0:T(8,128)(2,1)}, bf16[2896,128]{1,0:T(8,128)(2,1)S(1)}, u32[]{:S(2)}) copy-start(bf16[2896,128]{1,0:T(8,128)(2,1)S(1)} %broadcast_select_fusion.2.x_ref) | copy-start | bytes 2224132
  58.5 4.5 %copy-start.7 = (bf16[2896,128]{1,0:T(8,128)(2,1)}, bf16[2896,128]{1,0:T(8,128)(2,1)S(1)}, u32[]{:S(2)}) copy-start(bf16[2896,128]{1,0:T(8,128)(2,1)S(1)} %collective-permute-done.7.y_ref) | copy-start | bytes 2224132
  58.5 18.7 %collective-permute-start.12 = (bf16[2896,128]{1,0:T(8,128)(2,1)S(1)}, bf16[2896,128]{1,0:T(8,128)(2,1)}, u32[]{:S(2)}, u32[]{:S(2)}) collective-permute-start(bf16[2896,128]{1,0:T(8,128)(2,1)S(1)} %broadcast_select_fusion.2.x_ref), channel_id=1, source_target_pairs={{0,2},{1,3},{2,0},{3,1},{4,6},{5,7},{6,4},{7,5},{8,10},{9,11},{10,... | collective-permute-start | bytes 2224136 | tf_op jit(solution)/shard_map/ppermute | solution.py:420
  60.1 17.1 %collective-permute-start.13 = (bf16[2896,128]{1,0:T(8,128)(2,1)S(1)}, bf16[2896,128]{1,0:T(8,128)(2,1)}, u32[]{:S(2)}, u32[]{:S(2)}) collective-permute-start(bf16[2896,128]{1,0:T(8,128)(2,1)S(1)} %collective-permute-done.10), channel_id=1, source_target_pairs={{4,8},{5,9},{6,10},{7,11},{8,12},{9,13},{10,14},{11,15},{20,24},{2... | collective-permute-start | bytes 2224136 | tf_op jit(solution)/shard_map/ppermute | solution.py:326
  61.7 20.8 %collective-permute-start.14 = (bf16[2896,128]{1,0:T(8,128)(2,1)S(1)}, bf16[2896,128]{1,0:T(8,128)(2,1)}, u32[]{:S(2)}, u32[]{:S(2)}) collective-permute-start(bf16[2896,128]{1,0:T(8,128)(2,1)S(1)} %collective-permute-done.11), channel_id=1, source_target_pairs={{4,0},{5,1},{6,2},{7,3},{8,4},{9,5},{10,6},{11,7},{20,16},{21,17},... | collective-permute-start | bytes 2224136 | tf_op jit(solution)/shard_map/ppermute | solution.py:327
  83.9 15.8 %copy-start.2 = (bf16[2896,128]{1,0:T(8,128)(2,1)}, bf16[2896,128]{1,0:T(8,128)(2,1)S(1)}, u32[]{:S(2)}) copy-start(bf16[2896,128]{1,0:T(8,128)(2,1)S(1)} %get-tuple-element.48.x_ref) | copy-start | bytes 2224132
  83.9 17.4 %collective-permute-start.16 = (bf16[2896,128]{1,0:T(8,128)(2,1)S(1)}, bf16[2896,128]{1,0:T(8,128)(2,1)S(1)}, u32[]{:S(2)}, u32[]{:S(2)}) collective-permute-start(bf16[2896,128]{1,0:T(8,128)(2,1)S(1)} %get-tuple-element.49), channel_id=1, source_target_pairs={{8,12},{9,13},{10,14},{11,15},{4,0},{5,1},{6,2},{7,3},{24,28},{25,... | collective-permute-start | bytes 2224136 | tf_op jit(solution)/shard_map/ppermute | solution.py:323
  85.4 16.3 %collective-permute-start.15 = (bf16[2896,128]{1,0:T(8,128)(2,1)S(1)}, bf16[2896,128]{1,0:T(8,128)(2,1)S(1)}, u32[]{:S(2)}, u32[]{:S(2)}) collective-permute-start(bf16[2896,128]{1,0:T(8,128)(2,1)S(1)} %get-tuple-element.48.x_ref), channel_id=1, source_target_pairs={{0,2},{1,3},{2,0},{3,1},{4,6},{5,7},{6,4},{7,5},{8,10},{9,11},{10,... | collective-permute-start | bytes 2224136 | tf_op jit(solution)/shard_map/ppermute | solution.py:420
  99.7 2.6 %copy-start.14 = (bf16[2880,128]{1,0:T(8,128)(2,1)S(1)}, bf16[2880,128]{1,0:T(8,128)(2,1)}, u32[]{:S(2)}) copy-start(bf16[2880,128]{1,0:T(8,128)(2,1)} %get-tuple-element.50) | copy-start | bytes 2211844
  101.7 6.0 %copy-start.9 = (bf16[2896,128]{1,0:T(8,128)(2,1)}, bf16[2896,128]{1,0:T(8,128)(2,1)S(1)}, u32[]{:S(2)}) copy-start(bf16[2896,128]{1,0:T(8,128)(2,1)S(1)} %collective-permute-done.15.y_ref) | copy-start | bytes 2224132
  101.8 19.9 %copy-start.1 = (bf16[2896,128]{1,0:T(8,128)(2,1)}, bf16[2896,128]{1,0:T(8,128)(2,1)S(1)}, u32[]{:S(2)}) copy-start(bf16[2896,128]{1,0:T(8,128)(2,1)S(1)} %broadcast_select_fusion.x_ref) | copy-start | bytes 2224132
  101.8 19.9 %copy-start.13 = (bf16[2880,128]{1,0:T(8,128)(2,1)S(1)}, bf16[2880,128]{1,0:T(8,128)(2,1)}, u32[]{:S(2)}) copy-start(bf16[2880,128]{1,0:T(8,128)(2,1)} %get-tuple-element.59) | copy-start | bytes 2211844
  101.8 19.9 %collective-permute-start.19 = (bf16[2896,128]{1,0:T(8,128)(2,1)S(1)}, bf16[2896,128]{1,0:T(8,128)(2,1)S(1)}, u32[]{:S(2)}, u32[]{:S(2)}) collective-permute-start(bf16[2896,128]{1,0:T(8,128)(2,1)S(1)} %broadcast_select_fusion.x_ref), channel_id=1, source_target_pairs={{0,2},{1,3},{2,0},{3,1},{4,6},{5,7},{6,4},{7,5},{8,10},{9,11},{10,... | collective-permute-start | bytes 2224136 | tf_op jit(solution)/shard_map/ppermute | solution.py:420
  102.3 19.4 %collective-permute-start.17 = (bf16[2880,128]{1,0:T(8,128)(2,1)S(1)}, bf16[2880,128]{1,0:T(8,128)(2,1)S(1)}, u32[]{:S(2)}, u32[]{:S(2)}) collective-permute-start(bf16[2880,128]{1,0:T(8,128)(2,1)S(1)} %copy-done.14), channel_id=1, source_target_pairs={{0,4},{1,5},{2,6},{3,7},{4,8},{5,9},{6,10},{7,11},{16,20},{17,21},... | collective-permute-start | bytes 2211848 | tf_op jit(solution)/shard_map/ppermute | solution.py:445
  107.0 14.7 %collective-permute-start.18 = (bf16[2880,128]{1,0:T(8,128)(2,1)S(1)}, bf16[2880,128]{1,0:T(8,128)(2,1)S(1)}, u32[]{:S(2)}, u32[]{:S(2)}) collective-permute-start(bf16[2880,128]{1,0:T(8,128)(2,1)S(1)} %copy-done.14), channel_id=1, source_target_pairs={{8,4},{9,5},{10,6},{11,7},{12,8},{13,9},{14,10},{15,11},{24,20},{2... | collective-permute-start | bytes 2211848 | tf_op jit(solution)/shard_map/ppermute | solution.py:445
  121.7 6.5 %copy-start.8 = (bf16[2896,128]{1,0:T(8,128)(2,1)}, bf16[2896,128]{1,0:T(8,128)(2,1)S(1)}, u32[]{:S(2)}) copy-start(bf16[2896,128]{1,0:T(8,128)(2,1)S(1)} %collective-permute-done.19.y_ref) | copy-start | bytes 2224132
  121.7 21.2 %copy-start.5 = (f32[2880,128]{1,0:T(8,128)S(1)}, f32[2880,128]{1,0:T(8,128)}, u32[]{:S(2)}) copy-start(f32[2880,128]{1,0:T(8,128)} %get-tuple-element.51) | copy-start | bytes 4423684
  121.7 20.4 %collective-permute-start.23 = (bf16[2880,128]{1,0:T(8,128)(2,1)S(1)}, bf16[2880,128]{1,0:T(8,128)(2,1)S(1)}, u32[]{:S(2)}, u32[]{:S(2)}) collective-permute-start(bf16[2880,128]{1,0:T(8,128)(2,1)S(1)} %copy-done.13), channel_id=1, source_target_pairs={{8,4},{9,5},{10,6},{11,7},{12,8},{13,9},{14,10},{15,11},{24,20},{2... | collective-permute-start | bytes 2211848 | tf_op jit(solution)/shard_map/ppermute | solution.py:469
  122.6 19.6 %collective-permute-start.22 = (bf16[2880,128]{1,0:T(8,128)(2,1)S(1)}, bf16[2880,128]{1,0:T(8,128)(2,1)S(1)}, u32[]{:S(2)}, u32[]{:S(2)}) collective-permute-start(bf16[2880,128]{1,0:T(8,128)(2,1)S(1)} %copy-done.13), channel_id=1, source_target_pairs={{0,4},{1,5},{2,6},{3,7},{4,8},{5,9},{6,10},{7,11},{16,20},{17,21},... | collective-permute-start | bytes 2211848 | tf_op jit(solution)/shard_map/ppermute | solution.py:469
  126.7 15.5 %collective-permute-start.20 = (bf16[2880,128]{1,0:T(8,128)(2,1)}, bf16[2880,128]{1,0:T(8,128)(2,1)S(1)}, u32[]{:S(2)}, u32[]{:S(2)}) collective-permute-start(bf16[2880,128]{1,0:T(8,128)(2,1)} %get-tuple-element.55), channel_id=1, source_target_pairs={{0,2},{1,3},{2,0},{3,1},{4,6},{5,7},{6,4},{7,5},{8,10},{9,11},{10,... | collective-permute-start | bytes 2211848 | tf_op jit(solution)/shard_map/ppermute | solution.py:464
  142.2 16.4 %collective-permute-start.24 = (bf16[2880,128]{1,0:T(8,128)(2,1)}, bf16[2880,128]{1,0:T(8,128)(2,1)S(1)}, u32[]{:S(2)}, u32[]{:S(2)}) collective-permute-start(bf16[2880,128]{1,0:T(8,128)(2,1)} %get-tuple-element.60), channel_id=1, source_target_pairs={{0,2},{1,3},{2,0},{3,1},{4,6},{5,7},{6,4},{7,5},{8,10},{9,11},{10,... | collective-permute-start | bytes 2211848 | tf_op jit(solution)/shard_map/ppermute | solution.py:464
  142.9 2.3 %copy-start.4 = (f32[2880,128]{1,0:T(8,128)S(1)}, f32[2880,128]{1,0:T(8,128)}, u32[]{:S(2)}) copy-start(f32[2880,128]{1,0:T(8,128)} %get-tuple-element.61) | copy-start | bytes 4423684
  143.1 24.6 %collective-permute-start.21 = (bf16[2880,128]{1,0:T(8,128)(2,1)S(1)}, bf16[2880,128]{1,0:T(8,128)(2,1)S(1)}, u32[]{:S(2)}, u32[]{:S(2)}) collective-permute-start(bf16[2880,128]{1,0:T(8,128)(2,1)S(1)} %add_convert_fusion.3), channel_id=1, source_target_pairs={{0,8},{1,9},{2,10},{3,11},{4,0},{5,1},{6,2},{7,3},{8,12},{9,13},{1... | collective-permute-start | bytes 2211848 | tf_op jit(solution)/shard_map/ppermute | solution.py:475
  145.2 14.5 %copy-start.6 = (f32[2880,128]{1,0:T(8,128)S(1)}, f32[2880,128]{1,0:T(8,128)}, u32[]{:S(2)}) copy-start(f32[2880,128]{1,0:T(8,128)} %get-tuple-element.56) | copy-start | bytes 4423684
  158.6 13.1 %collective-permute-start.27 = (bf16[2880,128]{1,0:T(8,128)(2,1)S(1)}, bf16[2880,128]{1,0:T(8,128)(2,1)S(1)}, u32[]{:S(2)}, u32[]{:S(2)}) collective-permute-start(bf16[2880,128]{1,0:T(8,128)(2,1)S(1)} %add_convert_fusion.1), channel_id=1, source_target_pairs={{0,2},{1,3},{2,0},{3,1},{4,6},{5,7},{6,4},{7,5},{8,10},{9,11},{10,... | collective-permute-start | bytes 2211848 | tf_op jit(solution)/shard_map/ppermute | solution.py:479
  159.8 30.8 %copy-start.3 = (f32[2880,128]{1,0:T(8,128)S(1)}, f32[2880,128]{1,0:T(8,128)}, u32[]{:S(2)}) copy-start(f32[2880,128]{1,0:T(8,128)} %get-tuple-element.41) | copy-start | bytes 4423684
  159.8 30.8 %copy-start.10 = (bf16[2880,128]{1,0:T(8,128)(2,1)S(1)}, bf16[2880,128]{1,0:T(8,128)(2,1)}, u32[]{:S(2)}) copy-start(bf16[2880,128]{1,0:T(8,128)(2,1)} %get-tuple-element.39) | copy-start | bytes 2211844
  159.9 15.3 %collective-permute-start.26 = (bf16[2880,128]{1,0:T(8,128)(2,1)S(1)}, bf16[2880,128]{1,0:T(8,128)(2,1)S(1)}, u32[]{:S(2)}, u32[]{:S(2)}) collective-permute-start(bf16[2880,128]{1,0:T(8,128)(2,1)S(1)} %add_convert_fusion.2), channel_id=1, source_target_pairs={{4,12},{5,13},{6,14},{7,15},{12,0},{13,1},{14,2},{15,3},{20,28},{2... | collective-permute-start | bytes 2211848 | tf_op jit(solution)/shard_map/ppermute | solution.py:482
  161.3 29.2 %collective-permute-start.25 = (bf16[2880,128]{1,0:T(8,128)(2,1)S(1)}, bf16[2880,128]{1,0:T(8,128)(2,1)S(1)}, u32[]{:S(2)}, u32[]{:S(2)}) collective-permute-start(bf16[2880,128]{1,0:T(8,128)(2,1)S(1)} %add_convert_fusion.2), channel_id=1, source_target_pairs={{0,12},{1,13},{2,14},{3,15},{8,0},{9,1},{10,2},{11,3},{16,28},{17,... | collective-permute-start | bytes 2211848 | tf_op jit(solution)/shard_map/ppermute | solution.py:482
where the time goes:
time: 193 us; the launch traced here: 192 us
  waiting for transfers between devices  65.5 us (34%)
  Pallas kernels  65.5 us (34%)
  starting transfers between devices  48 us (25%)
  other arithmetic  7.59 us (4%)
  local copies, waits for them, and re-layouts  4.29 us (2%)
    pallas_call x4, Pallas kernels, expert_rows(): pl.pallas_call(functools.partial(expert_kernel, experts), out_shape=[jax....  55.8 us
    ppermute x3, waiting for transfers between devices, on_device(): back = lax.ppermute(both, 'seq', line_pairs(moves))  18.9 us
    ppermute x2, waiting for transfers between devices, on_device(): returned = lax.ppermute(theirs, 'seq', across)  13.1 us
    ppermute x2, waiting for transfers between devices, next_blocks(): lax.ppermute(below, 'seq', line_pairs(up))  13.1 us
    ppermute x3, starting transfers between devices, on_device(): back = lax.ppermute(both, 'seq', line_pairs(moves))  9.89 us
    pallas_call x1, Pallas kernels, attended_rows(): pl.pallas_call(functools.partial(attention_kernel, experts), out_shape=(j...  9.7 us
    ppermute x2, waiting for transfers between devices, next_blocks(): lax.ppermute(above, 'seq', line_pairs(down))  9.33 us
    ppermute x6, starting transfers between devices, summed(): lax.ppermute(block, axis, [(i, i ^ step * m) for i in range(shards)])  8.38 us
  transfers between devices with their start and end apart: 28, of which 12 were waited for; matrix products, arithmetic and copies ran while one was open for 5% of the time, Pallas kernels for 34%

commit v1 on v0

--- a/solution.py
+++ b/solution.py
@@ -19,21 +19,49 @@
 OUT_PART = 1024
 
 
-def window_allowed(query_pos, key_pos):
-    return (
-        (key_pos[:, None] >= 0)
-        & (key_pos[:, None] <= query_pos[None, :])
-        & (key_pos[:, None] > query_pos[None, :] - WINDOW)
-    )
-
-
-def sink_allowed(sink_positions, query_pos):
-    order = jnp.arange(sink_positions.shape[0], dtype=jnp.int32)
-    repeated = jnp.any(
-        (sink_positions[:, None] == sink_positions[None, :]) & (order[:, None] > order[None, :]),
-        axis=1,
-    )
-    return (~repeated)[:, None] & (sink_positions[:, None] <= query_pos[None, :] - WINDOW)
+def prepare_kernel(index_ref, sinks_ref, keys, values, joined_ref, picked_ref, bias_ref):
+    tokens, key_width = keys.shape
+    count = sinks_ref.shape[0]
+    first_pos = index_ref[0] * tokens
+    slot = lax.broadcasted_iota(jnp.int32, (count, tokens), 0)
+    lane = lax.broadcasted_iota(jnp.int32, (count, tokens), 1)
+    place = jnp.zeros((count, tokens), jnp.int32)
+    seen = jnp.zeros((count, tokens), jnp.int32)
+    for i in range(count):
+        repeated = jnp.int32(0)
+        for k in range(i):
+            repeated = jnp.where(sinks_ref[i] == sinks_ref[k], jnp.int32(1), repeated)
+        place = jnp.where(slot == i, sinks_ref[i], place)
+        seen = jnp.where(slot == i, repeated, seen)
+    pick = jnp.where(place == first_pos + lane, 1.0, 0.0).astype(jnp.bfloat16)
+    for at, rows in ((slice(0, key_width), keys), (slice(key_width, None), values)):
+        joined_ref[:, at] = rows[:, :]
+        picked_ref[:, at] = jnp.dot(
+            pick, rows[:, :], preferred_element_type=jnp.float32
+        ).astype(jnp.bfloat16)
+    near = bias_ref.shape[0] - count
+    key_pos = first_pos - WINDOW + lax.broadcasted_iota(jnp.int32, (near, tokens), 0)
+    query_pos = first_pos + lax.broadcasted_iota(jnp.int32, (near, tokens), 1)
+    allowed = (key_pos >= 0) & (key_pos <= query_pos) & (key_pos > query_pos - WINDOW)
+    bias_ref[:near, :] = jnp.where(allowed, 0.0, NEVER)
+    allowed = (seen == 0) & (place <= first_pos + lane - WINDOW)
+    bias_ref[near:, :] = jnp.where(allowed, 0.0, NEVER)
+
+
+def prepared(index, sink_positions, key_rows, value_rows):
+    tokens, key_width = key_rows.shape
+    count = sink_positions.shape[0]
+    smem, vmem = (pl.BlockSpec(memory_space=space) for space in (pltpu.SMEM, pltpu.VMEM))
+    return pl.pallas_call(
+        prepare_kernel,
+        out_shape=(
+            jax.ShapeDtypeStruct((tokens, 2 * key_width), jnp.bfloat16),
+            jax.ShapeDtypeStruct((count, 2 * key_width), jnp.bfloat16),
+            jax.ShapeDtypeStruct((WINDOW + tokens + count, tokens), jnp.float32),
+        ),
+        in_specs=[smem, smem, vmem, vmem],
+        out_specs=(vmem, vmem, vmem),
+    )(index, sink_positions, key_rows, value_rows)
 
 
 def after(block, *earlier):
@@ -64,8 +92,8 @@
 def attention_kernel(
     experts,
     query_t,
-    keys,
-    values,
+    halo,
+    local,
     sinks,
     bias,
     residual_t,
@@ -90,7 +118,7 @@
     for r in range(parts):
         proj_copy(r).start()
     group = Q_HEADS // KV_HEADS
-    near = keys.shape[0]
+    near = halo.shape[0] + local.shape[0]
     wide_bias = jnp.concatenate([bias[:, :]] * group, 1)
     scale = HEAD_DIM ** (-0.5)
     for g in range(KV_HEADS):
@@ -105,7 +133,12 @@
             1,
         )
         near_scores = (
-            jnp.dot(keys[:, lanes], query, preferred_element_type=jnp.float32) * scale
+            jnp.dot(
+                jnp.concatenate([halo[:, lanes], local[:, lanes]], 0),
+                query,
+                preferred_element_type=jnp.float32,
+            )
+            * scale
             + wide_bias[:near]
         )
         sink_scores = (
@@ -123,7 +156,7 @@
         )
         down = (((0,), (0,)), ((), ()))
         gathered = lax.dot_general(
-            values[:, lanes],
+            jnp.concatenate([halo[:, value_lanes], local[:, value_lanes]], 0),
             near_terms.astype(jnp.bfloat16),
             down,
             preferred_element_type=jnp.float32,
@@ -166,7 +199,7 @@
 
 
 def attended_rows(
-    query_t, keys, values, sinks, bias, residual_t, gain, ids_t, route_t, out_proj_t, experts
+    query_t, halo, local, sinks, bias, residual_t, gain, ids_t, route_t, out_proj_t, experts
 ):
     width, heads_width = out_proj_t.shape
     tokens = query_t.shape[1]
@@ -192,7 +225,7 @@
             bytes_accessed=2 * width * heads_width,
             transcendentals=tokens * Q_HEADS * bias.shape[0],
         ),
-    )(query_t, keys, values, sinks, bias, residual_t, gain, ids_t, route_t, out_proj_t)
+    )(query_t, halo, local, sinks, bias, residual_t, gain, ids_t, route_t, out_proj_t)
 
 
 def expert_kernel(experts, me_ref, x_ref, y_ref, gu0, gu1, dn0, dn1, *refs):
@@ -361,18 +394,12 @@
     experts = shards // 2
     my_index = lax.axis_index("seq")
     plane = my_index // PLANE
-    first_pos = my_index * rows_dev
-    own_pos = first_pos + jnp.arange(rows_dev, dtype=jnp.int32)
-
-    local_rows = jnp.concatenate([key_rows, value_rows], 1)
+    local_rows, sink_rows, bias = prepared(
+        my_index.reshape(1), sink_positions, key_rows, value_rows
+    )
     halo_rows = lax.ppermute(local_rows, "seq", [(i, i + 1) for i in range(shards - 1)])
-    pick_rows = (sink_positions[:, None] == own_pos[None, :]).astype(jnp.bfloat16)
-    sink_rows = jnp.dot(pick_rows, local_rows, preferred_element_type=jnp.float32)
-    later = (query_rows, norm_gain, sink_positions)
-    sink_rows, halo_rows, later = summed(
-        sink_rows.astype(jnp.bfloat16), "seq", halo_rows, later
-    )
-    query_rows, norm_gain, sink_positions = later
+    sink_rows, halo_rows, later = summed(sink_rows, "seq", halo_rows, (query_rows, norm_gain))
+    query_rows, norm_gain = later
 
     to_core = [(i, i ^ 1) for i in range(shards)]
     gu_own = jnp.swapaxes(gate_up[0], 0, 1)
@@ -381,18 +408,10 @@
     dn_other = lax.ppermute(dn_own, "seq", to_core)
     weights = (gu_own, gu_other, dn_own, dn_other)
 
-    joined = jnp.concatenate([halo_rows, local_rows], 0)
-    keys_joined = joined[:, : key_rows.shape[1]]
-    values_joined = joined[:, key_rows.shape[1] :]
-    key_pos = first_pos - WINDOW + jnp.arange(rows_dev + WINDOW, dtype=jnp.int32)
-    allowed = jnp.concatenate(
-        [window_allowed(own_pos, key_pos), sink_allowed(sink_positions, own_pos)], 0
-    )
-    bias = jnp.where(allowed, 0.0, NEVER).astype(jnp.float32)
     hidden_state, own = attended_rows(
         query_rows.T,
-        keys_joined,
-        values_joined,
+        halo_rows,
+        local_rows,
         sink_rows,
         bias,
         residual.T,

time: 193 us -> 192 us (level)
  other arithmetic: 7.59 us -> 5.11 us
  transfers between devices with their start and end apart: 28 -> 28, of which waited for: 12 -> 11; matrix products, arithmetic and copies ran while one was open for 5% -> 3% of each run, Pallas kernels for 34% -> 35%
where the time goes in v1:
time: 192 us; the launch traced here: 191 us
  Pallas kernels  67.2 us (35%)
  waiting for transfers between devices  65.9 us (34%)
  starting transfers between devices  48.4 us (25%)
  other arithmetic  5.11 us (3%)
  local copies, waits for them, and re-layouts  4.33 us (2%)
    pallas_call x4, Pallas kernels, expert_rows(): pl.pallas_call(functools.partial(expert_kernel, experts), out_shape=[jax....  55.8 us
    ppermute x3, waiting for transfers between devices, on_device(): back = lax.ppermute(both, 'seq', line_pairs(moves))  18.9 us
    ppermute x2, waiting for transfers between devices, on_device(): returned = lax.ppermute(theirs, 'seq', across)  13.1 us
    ppermute x2, waiting for transfers between devices, next_blocks(): lax.ppermute(below, 'seq', line_pairs(up))  12.9 us
    ppermute x3, starting transfers between devices, on_device(): back = lax.ppermute(both, 'seq', line_pairs(moves))  9.87 us
    pallas_call x1, Pallas kernels, attended_rows(): pl.pallas_call(functools.partial(attention_kernel, experts), out_shape=(j...  9.68 us
    ppermute x2, waiting for transfers between devices, next_blocks(): lax.ppermute(above, 'seq', line_pairs(down))  9.16 us
    ppermute x6, starting transfers between devices, summed(): lax.ppermute(block, axis, [(i, i ^ step * m) for i in range(shards)])  8.76 us
  transfers between devices with their start and end apart: 28, of which 11 were waited for; matrix products, arithmetic and copies ran while one was open for 3% of the time, Pallas kernels for 35%

profile of v1, /device:TPU:0, one launch (start us, length us, event | category | flops | bytes accessed | tf_op | source)
XLA Modules:
  0.0 191.4 jit_solution(2191011700339416819)
XLA Ops:
  0.0 0.5 collective-permute-start.8
  0.5 1.7 shard_map.109
  2.2 2.6 %collective-permute-start.2 = (bf16[16,512]{1,0:T(8,128)(2,1)}, bf16[16,512]{1,0:T(8,128)(2,1)S(1)}, u32[]{:S(2)}, u32[]{:S(2)}) collective-permute-start(bf16[16,512]{1,0:T(8,128)(2,1)} %get-tuple-element.36), channel_id=1, source_target_pairs={{0,3},{1,2},{2,1},{3,0},{4,7},{5,6},{6,5},{7,4},{8,11},{9,10},{10,... | collective-permute-start | bytes 49160 | tf_op jit(solution)/shard_map/ppermute | solution.py:77
  4.8 0.4 collective-permute-start.1
  5.3 1.1 collective-permute-done.2
  6.4 2.4 %collective-permute-start.3 = (bf16[128,512]{1,0:T(8,128)(2,1)}, bf16[128,512]{1,0:T(8,128)(2,1)S(1)}, u32[]{:S(2)}, u32[]{:S(2)}) collective-permute-start(bf16[128,512]{1,0:T(8,128)(2,1)} %get-tuple-element.37.local), channel_id=1, source_target_pairs={{0,1},{1,2},{2,3},{3,4},{4,5},{5,6},{6,7},{7,8},{8,9},{9,10},{10,1... | collective-permute-start | bytes 393224 | tf_op jit(solution)/shard_map/ppermute | solution.py:400
  8.9 4.8 %collective-permute-done = bf16[16,512]{1,0:T(8,128)(2,1)S(1)} collective-permute-done((bf16[16,512]{1,0:T(8,128)(2,1)}, bf16[16,512]{1,0:T(8,128)(2,1)S(1)}, u32[]{:S(2)}, u32[]{:S(2)}) %collective-permute-start) | collective-permute-done | bytes 16416 | tf_op jit(solution)/shard_map/ppermute | solution.py:77
  13.6 0.7 add_add_fusion.1
  14.4 5.0 %collective-permute-start.6 = (bf16[16,512]{1,0:T(8,128)(2,1)S(1)}, bf16[16,512]{1,0:T(8,128)(2,1)S(1)}, u32[]{:S(2)}, u32[]{:S(2)}) collective-permute-start(bf16[16,512]{1,0:T(8,128)(2,1)S(1)} %add_add_fusion.1), channel_id=1, source_target_pairs={{0,12},{1,13},{2,14},{3,15},{4,8},{5,9},{6,10},{7,11},{8,4},{9,5},... | collective-permute-start | bytes 49160 | tf_op jit(solution)/shard_map/ppermute | solution.py:77
  19.4 0.6 collective-permute-start.4
  20.0 2.0 %copy.13 = bf16[128,2048]{0,1:T(8,128)(2,1)} copy(bf16[128,2048]{1,0:T(8,128)(2,1)} %param.11) | data formatting | bytes 1048576 | tf_op jit(solution)/shard_map/optimization_barrier | solution.py:83
  22.1 2.2 %broadcast_in_dim.4.gain = f32[2880,1]{1,0:T(8,128)} reshape(f32[2880]{0:T(1024)} %param.17) | data formatting | bytes 23040 | tf_op jit(solution)/shard_map/broadcast_in_dim | solution.py:418
  24.3 0.6 add_add_fusion.sinks
  24.9 9.7 %shard_map.110 = (bf16[2880,128]{1,0:T(8,128)(2,1)}, bf16[2896,128]{1,0:T(8,128)(2,1)}) custom-call(bf16[2048,128]{1,0:T(8,128)(2,1)} %bitcast.24, bf16[128,512]{1,0:T(8,128)(2,1)} %copy-done.11, bf16[128,512]{1,0:T(8,128)(2,1)} %get-tuple-element.37.local, bf16[16,512]{1,0:T(8,128)(2,1)} %add_add_fusion.sinks, f32[272,128]{1,0:T(8,128)} %get-tuple-element.41.bias, ...), custom_call_target="tpu_custom_call" | custom-call | flops 1509949440 | bytes 11796480 | tf_op jit(solution)/shard_map/pallas_call | solution.py:209
  34.6 3.3 %collective-permute-start.10 = (bf16[2896,128]{1,0:T(8,128)(2,1)}, bf16[2896,128]{1,0:T(8,128)(2,1)S(1)}, u32[]{:S(2)}, u32[]{:S(2)}) collective-permute-start(bf16[2896,128]{1,0:T(8,128)(2,1)} %get-tuple-element.44.x_ref), channel_id=1, source_target_pairs={{0,4},{1,5},{2,6},{3,7},{4,8},{5,9},{6,10},{7,11},{8,12},{9,13},{1... | collective-permute-start | bytes 2224136 | tf_op jit(solution)/shard_map/ppermute | solution.py:359
  38.0 1.3 collective-permute-start.11
  39.3 1.6 collective-permute-start.7
  40.9 12.9 %collective-permute-done.10 = bf16[2896,128]{1,0:T(8,128)(2,1)S(1)} collective-permute-done((bf16[2896,128]{1,0:T(8,128)(2,1)}, bf16[2896,128]{1,0:T(8,128)(2,1)S(1)}, u32[]{:S(2)}, u32[]{:S(2)}) %collective-permute-start.10) | collective-permute-done | bytes 741408 | tf_op jit(solution)/shard_map/ppermute | solution.py:359
  53.8 4.1 %collective-permute-done.11 = bf16[2896,128]{1,0:T(8,128)(2,1)S(1)} collective-permute-done((bf16[2896,128]{1,0:T(8,128)(2,1)}, bf16[2896,128]{1,0:T(8,128)(2,1)S(1)}, u32[]{:S(2)}, u32[]{:S(2)}) %collective-permute-start.11) | collective-permute-done | bytes 741408 | tf_op jit(solution)/shard_map/ppermute | solution.py:360
  58.0 1.6 collective-permute-start.12
  59.6 1.5 collective-permute-start.13
  61.1 1.3 collective-permute-start.14
  62.5 14.2 %shard_map.111 = (f32[2880,128]{1,0:T(8,128)}, f32[2880,128]{1,0:T(8,128)}) custom-call(s32[1]{0:T(128)} %bitcast.6.me_ref, bf16[2896,128]{1,0:T(8,128)(2,1)} %get-tuple-element.44.x_ref, bf16[2896,128]{1,0:T(8,128)(2,1)} %copy-done.7, bf16[1440,2880]{1,0:T(8,128)(2,1)} %bitcast.14, bf16[1440,2880]{1,0:T(8,128)(2,1)} %collective-permute-done.8.gu1, ...), custom_call_target="tpu_custom_call" | custom-call | flops 6370099200 | bytes 24883200 | tf_op jit(solution)/shard_map/pallas_call | solution.py:300
  76.7 5.1 %collective-permute-done.14 = bf16[2896,128]{1,0:T(8,128)(2,1)} collective-permute-done((bf16[2896,128]{1,0:T(8,128)(2,1)S(1)}, bf16[2896,128]{1,0:T(8,128)(2,1)}, u32[]{:S(2)}, u32[]{:S(2)}) %collective-permute-start.14) | collective-permute-done | bytes 741408 | tf_op jit(solution)/shard_map/ppermute | solution.py:360
  81.8 1.4 select_select_fusion
  83.2 1.5 collective-permute-start.16
  84.7 0.6 collective-permute-start.15
  85.3 13.7 %shard_map.112 = (bf16[2880,128]{1,0:T(8,128)(2,1)}, bf16[2880,128]{1,0:T(8,128)(2,1)}) custom-call(s32[1]{0:T(128)} %bitcast.6.me_ref, bf16[2896,128]{1,0:T(8,128)(2,1)} %copy-done, bf16[2896,128]{1,0:T(8,128)(2,1)} %collective-permute-done.12.y_ref, bf16[1440,2880]{1,0:T(8,128)(2,1)} %bitcast.15, bf16[1440,2880]{1,0:T(8,128)(2,1)} %collective-permute-done.8.gu1, ...), custom_call_target="tpu_custom_call" | custom-call | flops 6370099200 | bytes 24883200 | tf_op jit(solution)/shard_map/pallas_call | solution.py:300
  99.0 1.5 collective-permute-done.16
  100.5 0.5 collective-permute-done.15.y_ref
  101.1 0.3 collective-permute-start.19
  101.4 4.9 %collective-permute-start.17 = (bf16[2880,128]{1,0:T(8,128)(2,1)S(1)}, bf16[2880,128]{1,0:T(8,128)(2,1)S(1)}, u32[]{:S(2)}, u32[]{:S(2)}) collective-permute-start(bf16[2880,128]{1,0:T(8,128)(2,1)S(1)} %copy-done.13), channel_id=1, source_target_pairs={{0,4},{1,5},{2,6},{3,7},{4,8},{5,9},{6,10},{7,11},{16,20},{17,21},... | collective-permute-start | bytes 2211848 | tf_op jit(solution)/shard_map/ppermute | solution.py:464
  106.3 0.7 collective-permute-start.18
  107.0 13.9 %shard_map.113 = (f32[2880,128]{1,0:T(8,128)}, bf16[2880,128]{1,0:T(8,128)(2,1)}) custom-call(s32[1]{0:T(128)} %bitcast.6.me_ref, bf16[2896,128]{1,0:T(8,128)(2,1)} %copy-done.2, bf16[2896,128]{1,0:T(8,128)(2,1)} %copy-done.9, bf16[1440,2880]{1,0:T(8,128)(2,1)} %bitcast.16, bf16[1440,2880]{1,0:T(8,128)(2,1)} %collective-permute-done.8.gu1, ...), custom_call_target="tpu_custom_call" | custom-call | flops 6370099200 | bytes 24883200 | tf_op jit(solution)/shard_map/pallas_call | solution.py:300
  121.0 0.8 collective-permute-start.23
  121.9 4.1 %collective-permute-start.22 = (bf16[2880,128]{1,0:T(8,128)(2,1)S(1)}, bf16[2880,128]{1,0:T(8,128)(2,1)S(1)}, u32[]{:S(2)}, u32[]{:S(2)}) collective-permute-start(bf16[2880,128]{1,0:T(8,128)(2,1)S(1)} %copy-done.12), channel_id=1, source_target_pairs={{0,4},{1,5},{2,6},{3,7},{4,8},{5,9},{6,10},{7,11},{16,20},{17,21},... | collective-permute-start | bytes 2211848 | tf_op jit(solution)/shard_map/ppermute | solution.py:488
  126.0 1.5 collective-permute-start.20
  127.5 14.0 %shard_map.114 = (f32[2880,128]{1,0:T(8,128)}, bf16[2880,128]{1,0:T(8,128)(2,1)}) custom-call(s32[1]{0:T(128)} %bitcast.6.me_ref, bf16[2896,128]{1,0:T(8,128)(2,1)} %copy-done.1, bf16[2896,128]{1,0:T(8,128)(2,1)} %copy-done.8, bf16[1440,2880]{1,0:T(8,128)(2,1)} %bitcast.17, bf16[1440,2880]{1,0:T(8,128)(2,1)} %collective-permute-done.8.gu1, ...), custom_call_target="tpu_custom_call" | custom-call | flops 6370099200 | bytes 24883200 | tf_op jit(solution)/shard_map/pallas_call | solution.py:300
  141.5 0.7 collective-permute-start.24
  142.4 2.1 %collective-permute-start.21 = (bf16[2880,128]{1,0:T(8,128)(2,1)S(1)}, bf16[2880,128]{1,0:T(8,128)(2,1)S(1)}, u32[]{:S(2)}, u32[]{:S(2)}) collective-permute-start(bf16[2880,128]{1,0:T(8,128)(2,1)S(1)} %add_convert_fusion.3), channel_id=1, source_target_pairs={{0,8},{1,9},{2,10},{3,11},{4,0},{5,1},{6,2},{7,3},{8,12},{9,13},{1... | collective-permute-start | bytes 2211848 | tf_op jit(solution)/shard_map/ppermute | solution.py:494
  144.7 13.1 %collective-permute-done.24 = bf16[2880,128]{1,0:T(8,128)(2,1)S(1)} collective-permute-done((bf16[2880,128]{1,0:T(8,128)(2,1)}, bf16[2880,128]{1,0:T(8,128)(2,1)S(1)}, u32[]{:S(2)}, u32[]{:S(2)}) %collective-permute-start.24) | collective-permute-done | bytes 737312 | tf_op jit(solution)/shard_map/ppermute | solution.py:483
  157.9 1.2 collective-permute-start.27
  159.2 1.4 collective-permute-start.26
  160.7 6.3 %collective-permute-start.25 = (bf16[2880,128]{1,0:T(8,128)(2,1)S(1)}, bf16[2880,128]{1,0:T(8,128)(2,1)S(1)}, u32[]{:S(2)}, u32[]{:S(2)}) collective-permute-start(bf16[2880,128]{1,0:T(8,128)(2,1)S(1)} %add_convert_fusion.2), channel_id=1, source_target_pairs={{0,12},{1,13},{2,14},{3,15},{8,0},{9,1},{10,2},{11,3},{16,28},{17,... | collective-permute-start | bytes 2211848 | tf_op jit(solution)/shard_map/ppermute | solution.py:501
  167.0 3.9 %collective-permute-done.27 = bf16[2880,128]{1,0:T(8,128)(2,1)S(1)} collective-permute-done((bf16[2880,128]{1,0:T(8,128)(2,1)S(1)}, bf16[2880,128]{1,0:T(8,128)(2,1)S(1)}, u32[]{:S(2)}, u32[]{:S(2)}) %collective-permute-start.27) | collective-permute-done | bytes 737312 | tf_op jit(solution)/shard_map/ppermute | solution.py:498
  170.9 3.6 %collective-permute-done.26 = bf16[2880,128]{1,0:T(8,128)(2,1)S(1)} collective-permute-done((bf16[2880,128]{1,0:T(8,128)(2,1)S(1)}, bf16[2880,128]{1,0:T(8,128)(2,1)S(1)}, u32[]{:S(2)}, u32[]{:S(2)}) %collective-permute-start.26) | collective-permute-done | bytes 737312 | tf_op jit(solution)/shard_map/ppermute | solution.py:501
  174.5 15.3 %collective-permute-done.25 = bf16[2880,128]{1,0:T(8,128)(2,1)S(1)} collective-permute-done((bf16[2880,128]{1,0:T(8,128)(2,1)S(1)}, bf16[2880,128]{1,0:T(8,128)(2,1)S(1)}, u32[]{:S(2)}, u32[]{:S(2)}) %collective-permute-start.25) | collective-permute-done | bytes 737312 | tf_op jit(solution)/shard_map/ppermute | solution.py:501
  189.8 1.6 fusion
  (53 shorter events, 1.0 us)
Async XLA Ops:
  0.0 62.4 %collective-permute-start.8 = (bf16[1440,2880]{1,0:T(8,128)(2,1)}, bf16[1440,2880]{1,0:T(8,128)(2,1)}, u32[]{:S(2)}, u32[]{:S(2)}) collective-permute-start(bf16[1440,2880]{1,0:T(8,128)(2,1)} %bitcast.13), channel_id=1, source_target_pairs={{0,1},{1,0},{2,3},{3,2},{4,5},{5,4},{6,7},{7,6},{8,9},{9,8},{10,11... | collective-permute-start | bytes 24883208 | tf_op jit(solution)/shard_map/ppermute | solution.py:407
  0.5 62.0 %collective-permute-start.9 = (bf16[720,2880]{1,0:T(8,128)(2,1)}, bf16[720,2880]{1,0:T(8,128)(2,1)}, u32[]{:S(2)}, u32[]{:S(2)}) collective-permute-start(bf16[720,2880]{1,0:T(8,128)(2,1)} %bitcast.18), channel_id=1, source_target_pairs={{0,1},{1,0},{2,3},{3,2},{4,5},{5,4},{6,7},{7,6},{8,9},{9,8},{10,11... | collective-permute-start | bytes 12441608 | tf_op jit(solution)/shard_map/ppermute | solution.py:408
  2.2 4.2 %collective-permute-start.2 = (bf16[16,512]{1,0:T(8,128)(2,1)}, bf16[16,512]{1,0:T(8,128)(2,1)S(1)}, u32[]{:S(2)}, u32[]{:S(2)}) collective-permute-start(bf16[16,512]{1,0:T(8,128)(2,1)} %get-tuple-element.36), channel_id=1, source_target_pairs={{0,3},{1,2},{2,1},{3,0},{4,7},{5,6},{6,5},{7,4},{8,11},{9,10},{10,... | collective-permute-start | bytes 49160 | tf_op jit(solution)/shard_map/ppermute | solution.py:77
  4.8 4.0 %collective-permute-start.1 = (bf16[16,512]{1,0:T(8,128)(2,1)}, bf16[16,512]{1,0:T(8,128)(2,1)S(1)}, u32[]{:S(2)}, u32[]{:S(2)}) collective-permute-start(bf16[16,512]{1,0:T(8,128)(2,1)} %get-tuple-element.36), channel_id=1, source_target_pairs={{0,2},{1,3},{2,0},{3,1},{4,6},{5,7},{6,4},{7,5},{8,10},{9,11},{10,... | collective-permute-start | bytes 49160 | tf_op jit(solution)/shard_map/ppermute | solution.py:77
  5.2 8.4 %collective-permute-start = (bf16[16,512]{1,0:T(8,128)(2,1)}, bf16[16,512]{1,0:T(8,128)(2,1)S(1)}, u32[]{:S(2)}, u32[]{:S(2)}) collective-permute-start(bf16[16,512]{1,0:T(8,128)(2,1)} %get-tuple-element.36), channel_id=1, source_target_pairs={{0,1},{1,0},{2,3},{3,2},{4,5},{5,4},{6,7},{7,6},{8,9},{9,8},{10,11... | collective-permute-start | bytes 49160 | tf_op jit(solution)/shard_map/ppermute | solution.py:77
  6.4 7.9 %collective-permute-start.3 = (bf16[128,512]{1,0:T(8,128)(2,1)}, bf16[128,512]{1,0:T(8,128)(2,1)S(1)}, u32[]{:S(2)}, u32[]{:S(2)}) collective-permute-start(bf16[128,512]{1,0:T(8,128)(2,1)} %get-tuple-element.37.local), channel_id=1, source_target_pairs={{0,1},{1,2},{2,3},{3,4},{4,5},{5,6},{6,7},{7,8},{8,9},{9,10},{10,1... | collective-permute-start | bytes 393224 | tf_op jit(solution)/shard_map/ppermute | solution.py:400
  14.4 10.6 %copy-start.11 = (bf16[128,512]{1,0:T(8,128)(2,1)}, bf16[128,512]{1,0:T(8,128)(2,1)S(1)}, u32[]{:S(2)}) copy-start(bf16[128,512]{1,0:T(8,128)(2,1)S(1)} %collective-permute-done.3.halo) | copy-start | bytes 393220
  14.4 10.0 %collective-permute-start.6 = (bf16[16,512]{1,0:T(8,128)(2,1)S(1)}, bf16[16,512]{1,0:T(8,128)(2,1)S(1)}, u32[]{:S(2)}, u32[]{:S(2)}) collective-permute-start(bf16[16,512]{1,0:T(8,128)(2,1)S(1)} %add_add_fusion.1), channel_id=1, source_target_pairs={{0,12},{1,13},{2,14},{3,15},{4,8},{5,9},{6,10},{7,11},{8,4},{9,5},... | collective-permute-start | bytes 49160 | tf_op jit(solution)/shard_map/ppermute | solution.py:77
  19.4 4.9 %collective-permute-start.5 = (bf16[16,512]{1,0:T(8,128)(2,1)S(1)}, bf16[16,512]{1,0:T(8,128)(2,1)S(1)}, u32[]{:S(2)}, u32[]{:S(2)}) collective-permute-start(bf16[16,512]{1,0:T(8,128)(2,1)S(1)} %add_add_fusion.1), channel_id=1, source_target_pairs={{0,8},{1,9},{2,10},{3,11},{4,12},{5,13},{6,14},{7,15},{8,0},{9,1},... | collective-permute-start | bytes 49160 | tf_op jit(solution)/shard_map/ppermute | solution.py:77
  19.4 4.9 %collective-permute-start.4 = (bf16[16,512]{1,0:T(8,128)(2,1)S(1)}, bf16[16,512]{1,0:T(8,128)(2,1)S(1)}, u32[]{:S(2)}, u32[]{:S(2)}) collective-permute-start(bf16[16,512]{1,0:T(8,128)(2,1)S(1)} %add_add_fusion.1), channel_id=1, source_target_pairs={{0,4},{1,5},{2,6},{3,7},{4,0},{5,1},{6,2},{7,3},{8,12},{9,13},{10,... | collective-permute-start | bytes 49160 | tf_op jit(solution)/shard_map/ppermute | solution.py:77
  34.6 19.2 %collective-permute-start.10 = (bf16[2896,128]{1,0:T(8,128)(2,1)}, bf16[2896,128]{1,0:T(8,128)(2,1)S(1)}, u32[]{:S(2)}, u32[]{:S(2)}) collective-permute-start(bf16[2896,128]{1,0:T(8,128)(2,1)} %get-tuple-element.44.x_ref), channel_id=1, source_target_pairs={{0,4},{1,5},{2,6},{3,7},{4,8},{5,9},{6,10},{7,11},{8,12},{9,13},{1... | collective-permute-start | bytes 2224136 | tf_op jit(solution)/shard_map/ppermute | solution.py:359
  38.0 19.9 %collective-permute-start.11 = (bf16[2896,128]{1,0:T(8,128)(2,1)}, bf16[2896,128]{1,0:T(8,128)(2,1)S(1)}, u32[]{:S(2)}, u32[]{:S(2)}) collective-permute-start(bf16[2896,128]{1,0:T(8,128)(2,1)} %get-tuple-element.44.x_ref), channel_id=1, source_target_pairs={{4,0},{5,1},{6,2},{7,3},{8,4},{9,5},{10,6},{11,7},{12,8},{13,9},{1... | collective-permute-start | bytes 2224136 | tf_op jit(solution)/shard_map/ppermute | solution.py:360
  39.3 18.7 %collective-permute-start.7 = (bf16[2896,128]{1,0:T(8,128)(2,1)}, bf16[2896,128]{1,0:T(8,128)(2,1)S(1)}, u32[]{:S(2)}, u32[]{:S(2)}) collective-permute-start(bf16[2896,128]{1,0:T(8,128)(2,1)} %get-tuple-element.44.x_ref), channel_id=1, source_target_pairs={{0,2},{1,3},{2,0},{3,1},{4,6},{5,7},{6,4},{7,5},{8,10},{9,11},{10,... | collective-permute-start | bytes 2224136 | tf_op jit(solution)/shard_map/ppermute | solution.py:433
  58.0 18.7 %copy-start = (bf16[2896,128]{1,0:T(8,128)(2,1)}, bf16[2896,128]{1,0:T(8,128)(2,1)S(1)}, u32[]{:S(2)}) copy-start(bf16[2896,128]{1,0:T(8,128)(2,1)S(1)} %broadcast_select_fusion.2.x_ref) | copy-start | bytes 2224132
  58.0 4.5 %copy-start.7 = (bf16[2896,128]{1,0:T(8,128)(2,1)}, bf16[2896,128]{1,0:T(8,128)(2,1)S(1)}, u32[]{:S(2)}) copy-start(bf16[2896,128]{1,0:T(8,128)(2,1)S(1)} %collective-permute-done.7.y_ref) | copy-start | bytes 2224132
  58.0 18.7 %collective-permute-start.12 = (bf16[2896,128]{1,0:T(8,128)(2,1)S(1)}, bf16[2896,128]{1,0:T(8,128)(2,1)}, u32[]{:S(2)}, u32[]{:S(2)}) collective-permute-start(bf16[2896,128]{1,0:T(8,128)(2,1)S(1)} %broadcast_select_fusion.2.x_ref), channel_id=1, source_target_pairs={{0,2},{1,3},{2,0},{3,1},{4,6},{5,7},{6,4},{7,5},{8,10},{9,11},{10,... | collective-permute-start | bytes 2224136 | tf_op jit(solution)/shard_map/ppermute | solution.py:439
  59.6 17.1 %collective-permute-start.13 = (bf16[2896,128]{1,0:T(8,128)(2,1)S(1)}, bf16[2896,128]{1,0:T(8,128)(2,1)}, u32[]{:S(2)}, u32[]{:S(2)}) collective-permute-start(bf16[2896,128]{1,0:T(8,128)(2,1)S(1)} %collective-permute-done.10), channel_id=1, source_target_pairs={{4,8},{5,9},{6,10},{7,11},{8,12},{9,13},{10,14},{11,15},{20,24},{2... | collective-permute-start | bytes 2224136 | tf_op jit(solution)/shard_map/ppermute | solution.py:359
  61.1 20.7 %collective-permute-start.14 = (bf16[2896,128]{1,0:T(8,128)(2,1)S(1)}, bf16[2896,128]{1,0:T(8,128)(2,1)}, u32[]{:S(2)}, u32[]{:S(2)}) collective-permute-start(bf16[2896,128]{1,0:T(8,128)(2,1)S(1)} %collective-permute-done.11), channel_id=1, source_target_pairs={{4,0},{5,1},{6,2},{7,3},{8,4},{9,5},{10,6},{11,7},{20,16},{21,17},... | collective-permute-start | bytes 2224136 | tf_op jit(solution)/shard_map/ppermute | solution.py:360
  83.2 15.8 %copy-start.2 = (bf16[2896,128]{1,0:T(8,128)(2,1)}, bf16[2896,128]{1,0:T(8,128)(2,1)S(1)}, u32[]{:S(2)}) copy-start(bf16[2896,128]{1,0:T(8,128)(2,1)S(1)} %get-tuple-element.52.x_ref) | copy-start | bytes 2224132
  83.2 17.3 %collective-permute-start.16 = (bf16[2896,128]{1,0:T(8,128)(2,1)S(1)}, bf16[2896,128]{1,0:T(8,128)(2,1)S(1)}, u32[]{:S(2)}, u32[]{:S(2)}) collective-permute-start(bf16[2896,128]{1,0:T(8,128)(2,1)S(1)} %get-tuple-element.53), channel_id=1, source_target_pairs={{8,12},{9,13},{10,14},{11,15},{4,0},{5,1},{6,2},{7,3},{24,28},{25,... | collective-permute-start | bytes 2224136 | tf_op jit(solution)/shard_map/ppermute | solution.py:356
  84.7 16.3 %collective-permute-start.15 = (bf16[2896,128]{1,0:T(8,128)(2,1)S(1)}, bf16[2896,128]{1,0:T(8,128)(2,1)S(1)}, u32[]{:S(2)}, u32[]{:S(2)}) collective-permute-start(bf16[2896,128]{1,0:T(8,128)(2,1)S(1)} %get-tuple-element.52.x_ref), channel_id=1, source_target_pairs={{0,2},{1,3},{2,0},{3,1},{4,6},{5,7},{6,4},{7,5},{8,10},{9,11},{10,... | collective-permute-start | bytes 2224136 | tf_op jit(solution)/shard_map/ppermute | solution.py:439
  99.0 2.4 %copy-start.13 = (bf16[2880,128]{1,0:T(8,128)(2,1)S(1)}, bf16[2880,128]{1,0:T(8,128)(2,1)}, u32[]{:S(2)}) copy-start(bf16[2880,128]{1,0:T(8,128)(2,1)} %get-tuple-element.54) | copy-start | bytes 2211844
  101.0 6.0 %copy-start.9 = (bf16[2896,128]{1,0:T(8,128)(2,1)}, bf16[2896,128]{1,0:T(8,128)(2,1)S(1)}, u32[]{:S(2)}) copy-start(bf16[2896,128]{1,0:T(8,128)(2,1)S(1)} %collective-permute-done.15.y_ref) | copy-start | bytes 2224132
  101.1 19.9 %copy-start.1 = (bf16[2896,128]{1,0:T(8,128)(2,1)}, bf16[2896,128]{1,0:T(8,128)(2,1)S(1)}, u32[]{:S(2)}) copy-start(bf16[2896,128]{1,0:T(8,128)(2,1)S(1)} %broadcast_select_fusion.x_ref) | copy-start | bytes 2224132
  101.1 19.9 %copy-start.12 = (bf16[2880,128]{1,0:T(8,128)(2,1)S(1)}, bf16[2880,128]{1,0:T(8,128)(2,1)}, u32[]{:S(2)}) copy-start(bf16[2880,128]{1,0:T(8,128)(2,1)} %get-tuple-element.63) | copy-start | bytes 2211844
  101.1 19.9 %collective-permute-start.19 = (bf16[2896,128]{1,0:T(8,128)(2,1)S(1)}, bf16[2896,128]{1,0:T(8,128)(2,1)S(1)}, u32[]{:S(2)}, u32[]{:S(2)}) collective-permute-start(bf16[2896,128]{1,0:T(8,128)(2,1)S(1)} %broadcast_select_fusion.x_ref), channel_id=1, source_target_pairs={{0,2},{1,3},{2,0},{3,1},{4,6},{5,7},{6,4},{7,5},{8,10},{9,11},{10,... | collective-permute-start | bytes 2224136 | tf_op jit(solution)/shard_map/ppermute | solution.py:439
  101.4 19.5 %collective-permute-start.17 = (bf16[2880,128]{1,0:T(8,128)(2,1)S(1)}, bf16[2880,128]{1,0:T(8,128)(2,1)S(1)}, u32[]{:S(2)}, u32[]{:S(2)}) collective-permute-start(bf16[2880,128]{1,0:T(8,128)(2,1)S(1)} %copy-done.13), channel_id=1, source_target_pairs={{0,4},{1,5},{2,6},{3,7},{4,8},{5,9},{6,10},{7,11},{16,20},{17,21},... | collective-permute-start | bytes 2211848 | tf_op jit(solution)/shard_map/ppermute | solution.py:464
  106.3 14.7 %collective-permute-start.18 = (bf16[2880,128]{1,0:T(8,128)(2,1)S(1)}, bf16[2880,128]{1,0:T(8,128)(2,1)S(1)}, u32[]{:S(2)}, u32[]{:S(2)}) collective-permute-start(bf16[2880,128]{1,0:T(8,128)(2,1)S(1)} %copy-done.13), channel_id=1, source_target_pairs={{8,4},{9,5},{10,6},{11,7},{12,8},{13,9},{14,10},{15,11},{24,20},{2... | collective-permute-start | bytes 2211848 | tf_op jit(solution)/shard_map/ppermute | solution.py:464
  121.0 6.5 %copy-start.8 = (bf16[2896,128]{1,0:T(8,128)(2,1)}, bf16[2896,128]{1,0:T(8,128)(2,1)S(1)}, u32[]{:S(2)}) copy-start(bf16[2896,128]{1,0:T(8,128)(2,1)S(1)} %collective-permute-done.19.y_ref) | copy-start | bytes 2224132
  121.0 21.2 %copy-start.5 = (f32[2880,128]{1,0:T(8,128)S(1)}, f32[2880,128]{1,0:T(8,128)}, u32[]{:S(2)}) copy-start(f32[2880,128]{1,0:T(8,128)} %get-tuple-element.55) | copy-start | bytes 4423684
  121.0 20.4 %collective-permute-start.23 = (bf16[2880,128]{1,0:T(8,128)(2,1)S(1)}, bf16[2880,128]{1,0:T(8,128)(2,1)S(1)}, u32[]{:S(2)}, u32[]{:S(2)}) collective-permute-start(bf16[2880,128]{1,0:T(8,128)(2,1)S(1)} %copy-done.12), channel_id=1, source_target_pairs={{8,4},{9,5},{10,6},{11,7},{12,8},{13,9},{14,10},{15,11},{24,20},{2... | collective-permute-start | bytes 2211848 | tf_op jit(solution)/shard_map/ppermute | solution.py:488
  121.9 19.6 %collective-permute-start.22 = (bf16[2880,128]{1,0:T(8,128)(2,1)S(1)}, bf16[2880,128]{1,0:T(8,128)(2,1)S(1)}, u32[]{:S(2)}, u32[]{:S(2)}) collective-permute-start(bf16[2880,128]{1,0:T(8,128)(2,1)S(1)} %copy-done.12), channel_id=1, source_target_pairs={{0,4},{1,5},{2,6},{3,7},{4,8},{5,9},{6,10},{7,11},{16,20},{17,21},... | collective-permute-start | bytes 2211848 | tf_op jit(solution)/shard_map/ppermute | solution.py:488
  126.0 15.5 %collective-permute-start.20 = (bf16[2880,128]{1,0:T(8,128)(2,1)}, bf16[2880,128]{1,0:T(8,128)(2,1)S(1)}, u32[]{:S(2)}, u32[]{:S(2)}) collective-permute-start(bf16[2880,128]{1,0:T(8,128)(2,1)} %get-tuple-element.59), channel_id=1, source_target_pairs={{0,2},{1,3},{2,0},{3,1},{4,6},{5,7},{6,4},{7,5},{8,10},{9,11},{10,... | collective-permute-start | bytes 2211848 | tf_op jit(solution)/shard_map/ppermute | solution.py:483
  141.5 16.3 %collective-permute-start.24 = (bf16[2880,128]{1,0:T(8,128)(2,1)}, bf16[2880,128]{1,0:T(8,128)(2,1)S(1)}, u32[]{:S(2)}, u32[]{:S(2)}) collective-permute-start(bf16[2880,128]{1,0:T(8,128)(2,1)} %get-tuple-element.64), channel_id=1, source_target_pairs={{0,2},{1,3},{2,0},{3,1},{4,6},{5,7},{6,4},{7,5},{8,10},{9,11},{10,... | collective-permute-start | bytes 2211848 | tf_op jit(solution)/shard_map/ppermute | solution.py:483
  142.2 2.3 %copy-start.4 = (f32[2880,128]{1,0:T(8,128)S(1)}, f32[2880,128]{1,0:T(8,128)}, u32[]{:S(2)}) copy-start(f32[2880,128]{1,0:T(8,128)} %get-tuple-element.65) | copy-start | bytes 4423684
  142.4 24.6 %collective-permute-start.21 = (bf16[2880,128]{1,0:T(8,128)(2,1)S(1)}, bf16[2880,128]{1,0:T(8,128)(2,1)S(1)}, u32[]{:S(2)}, u32[]{:S(2)}) collective-permute-start(bf16[2880,128]{1,0:T(8,128)(2,1)S(1)} %add_convert_fusion.3), channel_id=1, source_target_pairs={{0,8},{1,9},{2,10},{3,11},{4,0},{5,1},{6,2},{7,3},{8,12},{9,13},{1... | collective-permute-start | bytes 2211848 | tf_op jit(solution)/shard_map/ppermute | solution.py:494
  144.5 14.6 %copy-start.6 = (f32[2880,128]{1,0:T(8,128)S(1)}, f32[2880,128]{1,0:T(8,128)}, u32[]{:S(2)}) copy-start(f32[2880,128]{1,0:T(8,128)} %get-tuple-element.60) | copy-start | bytes 4423684
  157.9 13.1 %collective-permute-start.27 = (bf16[2880,128]{1,0:T(8,128)(2,1)S(1)}, bf16[2880,128]{1,0:T(8,128)(2,1)S(1)}, u32[]{:S(2)}, u32[]{:S(2)}) collective-permute-start(bf16[2880,128]{1,0:T(8,128)(2,1)S(1)} %add_convert_fusion.1), channel_id=1, source_target_pairs={{0,2},{1,3},{2,0},{3,1},{4,6},{5,7},{6,4},{7,5},{8,10},{9,11},{10,... | collective-permute-start | bytes 2211848 | tf_op jit(solution)/shard_map/ppermute | solution.py:498
  159.1 30.7 %copy-start.3 = (f32[2880,128]{1,0:T(8,128)S(1)}, f32[2880,128]{1,0:T(8,128)}, u32[]{:S(2)}) copy-start(f32[2880,128]{1,0:T(8,128)} %get-tuple-element.45) | copy-start | bytes 4423684
  159.1 30.7 %copy-start.10 = (bf16[2880,128]{1,0:T(8,128)(2,1)S(1)}, bf16[2880,128]{1,0:T(8,128)(2,1)}, u32[]{:S(2)}) copy-start(bf16[2880,128]{1,0:T(8,128)(2,1)} %get-tuple-element.43) | copy-start | bytes 2211844
  159.2 15.3 %collective-permute-start.26 = (bf16[2880,128]{1,0:T(8,128)(2,1)S(1)}, bf16[2880,128]{1,0:T(8,128)(2,1)S(1)}, u32[]{:S(2)}, u32[]{:S(2)}) collective-permute-start(bf16[2880,128]{1,0:T(8,128)(2,1)S(1)} %add_convert_fusion.2), channel_id=1, source_target_pairs={{4,12},{5,13},{6,14},{7,15},{12,0},{13,1},{14,2},{15,3},{20,28},{2... | collective-permute-start | bytes 2211848 | tf_op jit(solution)/shard_map/ppermute | solution.py:501
  160.7 29.2 %collective-permute-start.25 = (bf16[2880,128]{1,0:T(8,128)(2,1)S(1)}, bf16[2880,128]{1,0:T(8,128)(2,1)S(1)}, u32[]{:S(2)}, u32[]{:S(2)}) collective-permute-start(bf16[2880,128]{1,0:T(8,128)(2,1)S(1)} %add_convert_fusion.2), channel_id=1, source_target_pairs={{0,12},{1,13},{2,14},{3,15},{8,0},{9,1},{10,2},{11,3},{16,28},{17,... | collective-permute-start | bytes 2211848 | tf_op jit(solution)/shard_map/ppermute | solution.py:501

commit v2 on v1

--- a/solution.py
+++ b/solution.py
@@ -398,8 +398,9 @@
         my_index.reshape(1), sink_positions, key_rows, value_rows
     )
     halo_rows = lax.ppermute(local_rows, "seq", [(i, i + 1) for i in range(shards - 1)])
-    sink_rows, halo_rows, later = summed(sink_rows, "seq", halo_rows, (query_rows, norm_gain))
-    query_rows, norm_gain = later
+    later = (query_rows, gate_up, down_proj)
+    sink_rows, halo_rows, later = summed(sink_rows, "seq", halo_rows, later)
+    query_rows, gate_up, down_proj = later
 
     to_core = [(i, i ^ 1) for i in range(shards)]
     gu_own = jnp.swapaxes(gate_up[0], 0, 1)

time: 192 us -> 188 us (0.979)
  waiting for transfers between devices: 65.9 us -> 62.4 us
    ppermute x6, waiting for transfers between devices: 5.93 us -> 1.73 us  [summed(): lax.ppermute(block, axis, [(i, i ^ step * m) for i in range(shards)])]
  transfers between devices with their start and end apart: 28 -> 28, of which waited for: 11 -> 12; matrix products, arithmetic and copies ran while one was open for 3% -> 3% of each run, Pallas kernels for 35% -> 35%
where the time goes in v2:
time: 188 us; the launch traced here: 187 us
  Pallas kernels  67.3 us (36%)
  waiting for transfers between devices  62.4 us (33%)
  starting transfers between devices  48.8 us (26%)
  other arithmetic  5.11 us (3%)
  local copies, waits for them, and re-layouts  3.34 us (2%)
    pallas_call x4, Pallas kernels, expert_rows(): pl.pallas_call(functools.partial(expert_kernel, experts), out_shape=[jax....  55.8 us
    ppermute x3, waiting for transfers between devices, on_device(): back = lax.ppermute(both, 'seq', line_pairs(moves))  18.9 us
    ppermute x2, waiting for transfers between devices, next_blocks(): lax.ppermute(below, 'seq', line_pairs(up))  13.7 us
    ppermute x2, waiting for transfers between devices, on_device(): returned = lax.ppermute(theirs, 'seq', across)  13.5 us
    ppermute x3, starting transfers between devices, on_device(): back = lax.ppermute(both, 'seq', line_pairs(moves))  9.78 us
    pallas_call x1, Pallas kernels, attended_rows(): pl.pallas_call(functools.partial(attention_kernel, experts), out_shape=(j...  9.68 us
    ppermute x6, starting transfers between devices, summed(): lax.ppermute(block, axis, [(i, i ^ step * m) for i in range(shards)])  9.36 us
    ppermute x2, waiting for transfers between devices, next_blocks(): lax.ppermute(above, 'seq', line_pairs(down))  9.04 us
  transfers between devices with their start and end apart: 28, of which 12 were waited for; matrix products, arithmetic and copies ran while one was open for 3% of the time, Pallas kernels for 35%

profile of v2, /device:TPU:0, one launch (start us, length us, event | category | flops | bytes accessed | tf_op | source)
XLA Modules:
  0.0 187.3 jit_solution(14512626751827383667)
XLA Ops:
  0.0 1.8 shard_map.109
  1.8 2.4 %collective-permute-start.2 = (bf16[16,512]{1,0:T(8,128)(2,1)}, bf16[16,512]{1,0:T(8,128)(2,1)S(1)}, u32[]{:S(2)}, u32[]{:S(2)}) collective-permute-start(bf16[16,512]{1,0:T(8,128)(2,1)} %get-tuple-element.37), channel_id=1, source_target_pairs={{0,3},{1,2},{2,1},{3,0},{4,7},{5,6},{6,5},{7,4},{8,11},{9,10},{10,... | collective-permute-start | bytes 49160 | tf_op jit(solution)/shard_map/ppermute | solution.py:77
  4.2 0.6 collective-permute-start.1
  4.9 2.3 %collective-permute-start.3 = (bf16[128,512]{1,0:T(8,128)(2,1)}, bf16[128,512]{1,0:T(8,128)(2,1)S(1)}, u32[]{:S(2)}, u32[]{:S(2)}) collective-permute-start(bf16[128,512]{1,0:T(8,128)(2,1)} %get-tuple-element.38.local), channel_id=1, source_target_pairs={{0,1},{1,2},{2,3},{3,4},{4,5},{5,6},{6,7},{7,8},{8,9},{9,10},{10,1... | collective-permute-start | bytes 393224 | tf_op jit(solution)/shard_map/ppermute | solution.py:400
  7.2 0.9 collective-permute-done.1
  8.1 0.7 add_add_fusion.1
  8.9 2.0 %collective-permute-start.8 = (bf16[1440,2880]{1,0:T(8,128)(2,1)}, bf16[1440,2880]{1,0:T(8,128)(2,1)}, u32[]{:S(2)}, u32[]{:S(2)}) collective-permute-start(bf16[1440,2880]{1,0:T(8,128)(2,1)} %bitcast.13), channel_id=1, source_target_pairs={{0,1},{1,0},{2,3},{3,2},{4,5},{5,4},{6,7},{7,6},{8,9},{9,8},{10,11... | collective-permute-start | bytes 24883208 | tf_op jit(solution)/shard_map/ppermute | solution.py:408
  10.9 5.7 %collective-permute-start.6 = (bf16[16,512]{1,0:T(8,128)(2,1)S(1)}, bf16[16,512]{1,0:T(8,128)(2,1)S(1)}, u32[]{:S(2)}, u32[]{:S(2)}) collective-permute-start(bf16[16,512]{1,0:T(8,128)(2,1)S(1)} %add_add_fusion.1), channel_id=1, source_target_pairs={{0,12},{1,13},{2,14},{3,15},{4,8},{5,9},{6,10},{7,11},{8,4},{9,5},... | collective-permute-start | bytes 49160 | tf_op jit(solution)/shard_map/ppermute | solution.py:77
  16.6 0.6 collective-permute-start.4
  17.1 2.3 %broadcast_in_dim.4.gain = f32[2880,1]{1,0:T(8,128)} reshape(f32[2880]{0:T(1024)} %param.17) | data formatting | bytes 23040 | tf_op jit(solution)/shard_map/broadcast_in_dim | solution.py:419
  19.4 1.0 copy.13
  20.4 0.8 collective-permute-done.5
  21.2 0.6 add_add_fusion.sinks
  21.8 9.7 %shard_map.110 = (bf16[2880,128]{1,0:T(8,128)(2,1)}, bf16[2896,128]{1,0:T(8,128)(2,1)}) custom-call(bf16[2048,128]{1,0:T(8,128)(2,1)} %bitcast.24, bf16[128,512]{1,0:T(8,128)(2,1)} %copy-done.12, bf16[128,512]{1,0:T(8,128)(2,1)} %get-tuple-element.38.local, bf16[16,512]{1,0:T(8,128)(2,1)} %add_add_fusion.sinks, f32[272,128]{1,0:T(8,128)} %get-tuple-element.42.bias, ...), custom_call_target="tpu_custom_call" | custom-call | flops 1509949440 | bytes 11796480 | tf_op jit(solution)/shard_map/pallas_call | solution.py:209
  31.5 2.6 %collective-permute-start.10 = (bf16[2896,128]{1,0:T(8,128)(2,1)}, bf16[2896,128]{1,0:T(8,128)(2,1)S(1)}, u32[]{:S(2)}, u32[]{:S(2)}) collective-permute-start(bf16[2896,128]{1,0:T(8,128)(2,1)} %get-tuple-element.44.x_ref), channel_id=1, source_target_pairs={{0,4},{1,5},{2,6},{3,7},{4,8},{5,9},{6,10},{7,11},{8,12},{9,13},{1... | collective-permute-start | bytes 2224136 | tf_op jit(solution)/shard_map/ppermute | solution.py:359
  34.2 1.3 collective-permute-start.11
  35.5 0.7 collective-permute-start.7
  36.1 13.7 %collective-permute-done.10 = bf16[2896,128]{1,0:T(8,128)(2,1)S(1)} collective-permute-done((bf16[2896,128]{1,0:T(8,128)(2,1)}, bf16[2896,128]{1,0:T(8,128)(2,1)S(1)}, u32[]{:S(2)}, u32[]{:S(2)}) %collective-permute-start.10) | collective-permute-done | bytes 741408 | tf_op jit(solution)/shard_map/ppermute | solution.py:359
  49.9 4.1 %collective-permute-done.11 = bf16[2896,128]{1,0:T(8,128)(2,1)S(1)} collective-permute-done((bf16[2896,128]{1,0:T(8,128)(2,1)}, bf16[2896,128]{1,0:T(8,128)(2,1)S(1)}, u32[]{:S(2)}, u32[]{:S(2)}) %collective-permute-start.11) | collective-permute-done | bytes 741408 | tf_op jit(solution)/shard_map/ppermute | solution.py:360
  54.0 0.7 collective-permute-start.12
  54.7 1.5 collective-permute-start.13
  56.2 1.3 collective-permute-start.14
  57.6 14.2 %shard_map.111 = (f32[2880,128]{1,0:T(8,128)}, f32[2880,128]{1,0:T(8,128)}) custom-call(s32[1]{0:T(128)} %bitcast.6.me_ref, bf16[2896,128]{1,0:T(8,128)(2,1)} %get-tuple-element.44.x_ref, bf16[2896,128]{1,0:T(8,128)(2,1)} %copy-done.7, bf16[1440,2880]{1,0:T(8,128)(2,1)} %bitcast.14, bf16[1440,2880]{1,0:T(8,128)(2,1)} %collective-permute-done.8.gu1, ...), custom_call_target="tpu_custom_call" | custom-call | flops 6370099200 | bytes 24883200 | tf_op jit(solution)/shard_map/pallas_call | solution.py:300
  71.8 5.0 %collective-permute-done.14 = bf16[2896,128]{1,0:T(8,128)(2,1)} collective-permute-done((bf16[2896,128]{1,0:T(8,128)(2,1)S(1)}, bf16[2896,128]{1,0:T(8,128)(2,1)}, u32[]{:S(2)}, u32[]{:S(2)}) %collective-permute-start.14) | collective-permute-done | bytes 741408 | tf_op jit(solution)/shard_map/ppermute | solution.py:360
  76.8 1.4 select_select_fusion
  78.2 1.5 collective-permute-start.16
  79.7 1.5 collective-permute-start.15
  81.2 13.7 %shard_map.112 = (bf16[2880,128]{1,0:T(8,128)(2,1)}, bf16[2880,128]{1,0:T(8,128)(2,1)}) custom-call(s32[1]{0:T(128)} %bitcast.6.me_ref, bf16[2896,128]{1,0:T(8,128)(2,1)} %copy-done, bf16[2896,128]{1,0:T(8,128)(2,1)} %collective-permute-done.12.y_ref, bf16[1440,2880]{1,0:T(8,128)(2,1)} %bitcast.15, bf16[1440,2880]{1,0:T(8,128)(2,1)} %collective-permute-done.8.gu1, ...), custom_call_target="tpu_custom_call" | custom-call | flops 6370099200 | bytes 24883200 | tf_op jit(solution)/shard_map/pallas_call | solution.py:300
  94.9 0.4 collective-permute-done.16
  95.3 0.4 collective-permute-done.15.y_ref
  95.8 1.7 collective-permute-start.19
  97.5 4.9 %collective-permute-start.17 = (bf16[2880,128]{1,0:T(8,128)(2,1)S(1)}, bf16[2880,128]{1,0:T(8,128)(2,1)S(1)}, u32[]{:S(2)}, u32[]{:S(2)}) collective-permute-start(bf16[2880,128]{1,0:T(8,128)(2,1)S(1)} %copy-done.14), channel_id=1, source_target_pairs={{0,4},{1,5},{2,6},{3,7},{4,8},{5,9},{6,10},{7,11},{16,20},{17,21},... | collective-permute-start | bytes 2211848 | tf_op jit(solution)/shard_map/ppermute | solution.py:465
  102.4 0.7 collective-permute-start.18
  103.2 13.9 %shard_map.113 = (f32[2880,128]{1,0:T(8,128)}, bf16[2880,128]{1,0:T(8,128)(2,1)}) custom-call(s32[1]{0:T(128)} %bitcast.6.me_ref, bf16[2896,128]{1,0:T(8,128)(2,1)} %copy-done.2, bf16[2896,128]{1,0:T(8,128)(2,1)} %copy-done.9, bf16[1440,2880]{1,0:T(8,128)(2,1)} %bitcast.16, bf16[1440,2880]{1,0:T(8,128)(2,1)} %collective-permute-done.8.gu1, ...), custom_call_target="tpu_custom_call" | custom-call | flops 6370099200 | bytes 24883200 | tf_op jit(solution)/shard_map/pallas_call | solution.py:300
  117.2 0.8 collective-permute-start.23
  118.0 3.8 %collective-permute-start.22 = (bf16[2880,128]{1,0:T(8,128)(2,1)S(1)}, bf16[2880,128]{1,0:T(8,128)(2,1)S(1)}, u32[]{:S(2)}, u32[]{:S(2)}) collective-permute-start(bf16[2880,128]{1,0:T(8,128)(2,1)S(1)} %copy-done.13), channel_id=1, source_target_pairs={{0,4},{1,5},{2,6},{3,7},{4,8},{5,9},{6,10},{7,11},{16,20},{17,21},... | collective-permute-start | bytes 2211848 | tf_op jit(solution)/shard_map/ppermute | solution.py:489
  121.8 0.5 collective-permute-start.20
  122.3 14.0 %shard_map.114 = (f32[2880,128]{1,0:T(8,128)}, bf16[2880,128]{1,0:T(8,128)(2,1)}) custom-call(s32[1]{0:T(128)} %bitcast.6.me_ref, bf16[2896,128]{1,0:T(8,128)(2,1)} %copy-done.1, bf16[2896,128]{1,0:T(8,128)(2,1)} %copy-done.8, bf16[1440,2880]{1,0:T(8,128)(2,1)} %bitcast.17, bf16[1440,2880]{1,0:T(8,128)(2,1)} %collective-permute-done.8.gu1, ...), custom_call_target="tpu_custom_call" | custom-call | flops 6370099200 | bytes 24883200 | tf_op jit(solution)/shard_map/pallas_call | solution.py:300
  136.7 1.3 collective-permute-start.24
  138.2 2.0 %collective-permute-start.21 = (bf16[2880,128]{1,0:T(8,128)(2,1)S(1)}, bf16[2880,128]{1,0:T(8,128)(2,1)S(1)}, u32[]{:S(2)}, u32[]{:S(2)}) collective-permute-start(bf16[2880,128]{1,0:T(8,128)(2,1)S(1)} %add_convert_fusion.3), channel_id=1, source_target_pairs={{0,8},{1,9},{2,10},{3,11},{4,0},{5,1},{6,2},{7,3},{8,12},{9,13},{1... | collective-permute-start | bytes 2211848 | tf_op jit(solution)/shard_map/ppermute | solution.py:495
  140.5 13.1 %collective-permute-done.24 = bf16[2880,128]{1,0:T(8,128)(2,1)S(1)} collective-permute-done((bf16[2880,128]{1,0:T(8,128)(2,1)}, bf16[2880,128]{1,0:T(8,128)(2,1)S(1)}, u32[]{:S(2)}, u32[]{:S(2)}) %collective-permute-start.24) | collective-permute-done | bytes 737312 | tf_op jit(solution)/shard_map/ppermute | solution.py:484
  153.6 0.6 collective-permute-start.27
  154.3 1.4 collective-permute-start.26
  155.7 6.3 %collective-permute-start.25 = (bf16[2880,128]{1,0:T(8,128)(2,1)S(1)}, bf16[2880,128]{1,0:T(8,128)(2,1)S(1)}, u32[]{:S(2)}, u32[]{:S(2)}) collective-permute-start(bf16[2880,128]{1,0:T(8,128)(2,1)S(1)} %add_convert_fusion.2), channel_id=1, source_target_pairs={{0,12},{1,13},{2,14},{3,15},{8,0},{9,1},{10,2},{11,3},{16,28},{17,... | collective-permute-start | bytes 2211848 | tf_op jit(solution)/shard_map/ppermute | solution.py:502
  162.1 4.7 %collective-permute-done.27 = bf16[2880,128]{1,0:T(8,128)(2,1)S(1)} collective-permute-done((bf16[2880,128]{1,0:T(8,128)(2,1)S(1)}, bf16[2880,128]{1,0:T(8,128)(2,1)S(1)}, u32[]{:S(2)}, u32[]{:S(2)}) %collective-permute-start.27) | collective-permute-done | bytes 737312 | tf_op jit(solution)/shard_map/ppermute | solution.py:499
  166.8 3.2 %collective-permute-done.26 = bf16[2880,128]{1,0:T(8,128)(2,1)S(1)} collective-permute-done((bf16[2880,128]{1,0:T(8,128)(2,1)S(1)}, bf16[2880,128]{1,0:T(8,128)(2,1)S(1)}, u32[]{:S(2)}, u32[]{:S(2)}) %collective-permute-start.26) | collective-permute-done | bytes 737312 | tf_op jit(solution)/shard_map/ppermute | solution.py:502
  170.0 15.7 %collective-permute-done.25 = bf16[2880,128]{1,0:T(8,128)(2,1)S(1)} collective-permute-done((bf16[2880,128]{1,0:T(8,128)(2,1)S(1)}, bf16[2880,128]{1,0:T(8,128)(2,1)S(1)}, u32[]{:S(2)}, u32[]{:S(2)}) %collective-permute-start.25) | collective-permute-done | bytes 737312 | tf_op jit(solution)/shard_map/ppermute | solution.py:502
  185.7 1.6 fusion
  (55 shorter events, 1.3 us)
Async XLA Ops:
  0.0 19.4 %copy-start.11 = (bf16[128,2048]{1,0:T(8,128)(2,1)S(1)}, bf16[128,2048]{1,0:T(8,128)(2,1)}, u32[]{:S(2)}) copy-start(bf16[128,2048]{1,0:T(8,128)(2,1)} %param.11) | copy-start | bytes 1572868
  1.8 5.4 %collective-permute-start.2 = (bf16[16,512]{1,0:T(8,128)(2,1)}, bf16[16,512]{1,0:T(8,128)(2,1)S(1)}, u32[]{:S(2)}, u32[]{:S(2)}) collective-permute-start(bf16[16,512]{1,0:T(8,128)(2,1)} %get-tuple-element.37), channel_id=1, source_target_pairs={{0,3},{1,2},{2,1},{3,0},{4,7},{5,6},{6,5},{7,4},{8,11},{9,10},{10,... | collective-permute-start | bytes 49160 | tf_op jit(solution)/shard_map/ppermute | solution.py:77
  4.2 3.9 %collective-permute-start.1 = (bf16[16,512]{1,0:T(8,128)(2,1)}, bf16[16,512]{1,0:T(8,128)(2,1)S(1)}, u32[]{:S(2)}, u32[]{:S(2)}) collective-permute-start(bf16[16,512]{1,0:T(8,128)(2,1)} %get-tuple-element.37), channel_id=1, source_target_pairs={{0,2},{1,3},{2,0},{3,1},{4,6},{5,7},{6,4},{7,5},{8,10},{9,11},{10,... | collective-permute-start | bytes 49160 | tf_op jit(solution)/shard_map/ppermute | solution.py:77
  4.8 3.4 %collective-permute-start = (bf16[16,512]{1,0:T(8,128)(2,1)}, bf16[16,512]{1,0:T(8,128)(2,1)S(1)}, u32[]{:S(2)}, u32[]{:S(2)}) collective-permute-start(bf16[16,512]{1,0:T(8,128)(2,1)} %get-tuple-element.37), channel_id=1, source_target_pairs={{0,1},{1,0},{2,3},{3,2},{4,5},{5,4},{6,7},{7,6},{8,9},{9,8},{10,11... | collective-permute-start | bytes 49160 | tf_op jit(solution)/shard_map/ppermute | solution.py:77
  4.9 4.0 %collective-permute-start.3 = (bf16[128,512]{1,0:T(8,128)(2,1)}, bf16[128,512]{1,0:T(8,128)(2,1)S(1)}, u32[]{:S(2)}, u32[]{:S(2)}) collective-permute-start(bf16[128,512]{1,0:T(8,128)(2,1)} %get-tuple-element.38.local), channel_id=1, source_target_pairs={{0,1},{1,2},{2,3},{3,4},{4,5},{5,6},{6,7},{7,8},{8,9},{9,10},{10,1... | collective-permute-start | bytes 393224 | tf_op jit(solution)/shard_map/ppermute | solution.py:400
  8.9 13.0 %copy-start.12 = (bf16[128,512]{1,0:T(8,128)(2,1)}, bf16[128,512]{1,0:T(8,128)(2,1)S(1)}, u32[]{:S(2)}) copy-start(bf16[128,512]{1,0:T(8,128)(2,1)S(1)} %collective-permute-done.3.halo) | copy-start | bytes 393220
  8.9 48.7 %collective-permute-start.8 = (bf16[1440,2880]{1,0:T(8,128)(2,1)}, bf16[1440,2880]{1,0:T(8,128)(2,1)}, u32[]{:S(2)}, u32[]{:S(2)}) collective-permute-start(bf16[1440,2880]{1,0:T(8,128)(2,1)} %bitcast.13), channel_id=1, source_target_pairs={{0,1},{1,0},{2,3},{3,2},{4,5},{5,4},{6,7},{7,6},{8,9},{9,8},{10,11... | collective-permute-start | bytes 24883208 | tf_op jit(solution)/shard_map/ppermute | solution.py:408
  10.9 46.7 %collective-permute-start.9 = (bf16[720,2880]{1,0:T(8,128)(2,1)}, bf16[720,2880]{1,0:T(8,128)(2,1)}, u32[]{:S(2)}, u32[]{:S(2)}) collective-permute-start(bf16[720,2880]{1,0:T(8,128)(2,1)} %bitcast.18), channel_id=1, source_target_pairs={{0,1},{1,0},{2,3},{3,2},{4,5},{5,4},{6,7},{7,6},{8,9},{9,8},{10,11... | collective-permute-start | bytes 12441608 | tf_op jit(solution)/shard_map/ppermute | solution.py:409
  10.9 9.6 %collective-permute-start.6 = (bf16[16,512]{1,0:T(8,128)(2,1)S(1)}, bf16[16,512]{1,0:T(8,128)(2,1)S(1)}, u32[]{:S(2)}, u32[]{:S(2)}) collective-permute-start(bf16[16,512]{1,0:T(8,128)(2,1)S(1)} %add_add_fusion.1), channel_id=1, source_target_pairs={{0,12},{1,13},{2,14},{3,15},{4,8},{5,9},{6,10},{7,11},{8,4},{9,5},... | collective-permute-start | bytes 49160 | tf_op jit(solution)/shard_map/ppermute | solution.py:77
  16.6 4.6 %collective-permute-start.5 = (bf16[16,512]{1,0:T(8,128)(2,1)S(1)}, bf16[16,512]{1,0:T(8,128)(2,1)S(1)}, u32[]{:S(2)}, u32[]{:S(2)}) collective-permute-start(bf16[16,512]{1,0:T(8,128)(2,1)S(1)} %add_add_fusion.1), channel_id=1, source_target_pairs={{0,8},{1,9},{2,10},{3,11},{4,12},{5,13},{6,14},{7,15},{8,0},{9,1},... | collective-permute-start | bytes 49160 | tf_op jit(solution)/shard_map/ppermute | solution.py:77
  16.6 4.6 %collective-permute-start.4 = (bf16[16,512]{1,0:T(8,128)(2,1)S(1)}, bf16[16,512]{1,0:T(8,128)(2,1)S(1)}, u32[]{:S(2)}, u32[]{:S(2)}) collective-permute-start(bf16[16,512]{1,0:T(8,128)(2,1)S(1)} %add_add_fusion.1), channel_id=1, source_target_pairs={{0,4},{1,5},{2,6},{3,7},{4,0},{5,1},{6,2},{7,3},{8,12},{9,13},{10,... | collective-permute-start | bytes 49160 | tf_op jit(solution)/shard_map/ppermute | solution.py:77
  31.5 18.3 %collective-permute-start.10 = (bf16[2896,128]{1,0:T(8,128)(2,1)}, bf16[2896,128]{1,0:T(8,128)(2,1)S(1)}, u32[]{:S(2)}, u32[]{:S(2)}) collective-permute-start(bf16[2896,128]{1,0:T(8,128)(2,1)} %get-tuple-element.44.x_ref), channel_id=1, source_target_pairs={{0,4},{1,5},{2,6},{3,7},{4,8},{5,9},{6,10},{7,11},{8,12},{9,13},{1... | collective-permute-start | bytes 2224136 | tf_op jit(solution)/shard_map/ppermute | solution.py:359
  34.2 19.7 %collective-permute-start.11 = (bf16[2896,128]{1,0:T(8,128)(2,1)}, bf16[2896,128]{1,0:T(8,128)(2,1)S(1)}, u32[]{:S(2)}, u32[]{:S(2)}) collective-permute-start(bf16[2896,128]{1,0:T(8,128)(2,1)} %get-tuple-element.44.x_ref), channel_id=1, source_target_pairs={{4,0},{5,1},{6,2},{7,3},{8,4},{9,5},{10,6},{11,7},{12,8},{13,9},{1... | collective-permute-start | bytes 2224136 | tf_op jit(solution)/shard_map/ppermute | solution.py:360
  35.5 18.6 %collective-permute-start.7 = (bf16[2896,128]{1,0:T(8,128)(2,1)}, bf16[2896,128]{1,0:T(8,128)(2,1)S(1)}, u32[]{:S(2)}, u32[]{:S(2)}) collective-permute-start(bf16[2896,128]{1,0:T(8,128)(2,1)} %get-tuple-element.44.x_ref), channel_id=1, source_target_pairs={{0,2},{1,3},{2,0},{3,1},{4,6},{5,7},{6,4},{7,5},{8,10},{9,11},{10,... | collective-permute-start | bytes 2224136 | tf_op jit(solution)/shard_map/ppermute | solution.py:434
  54.0 17.8 %copy-start = (bf16[2896,128]{1,0:T(8,128)(2,1)}, bf16[2896,128]{1,0:T(8,128)(2,1)S(1)}, u32[]{:S(2)}) copy-start(bf16[2896,128]{1,0:T(8,128)(2,1)S(1)} %broadcast_select_fusion.2.x_ref) | copy-start | bytes 2224132
  54.0 3.5 %copy-start.7 = (bf16[2896,128]{1,0:T(8,128)(2,1)}, bf16[2896,128]{1,0:T(8,128)(2,1)S(1)}, u32[]{:S(2)}) copy-start(bf16[2896,128]{1,0:T(8,128)(2,1)S(1)} %collective-permute-done.7.y_ref) | copy-start | bytes 2224132
  54.0 17.7 %collective-permute-start.12 = (bf16[2896,128]{1,0:T(8,128)(2,1)S(1)}, bf16[2896,128]{1,0:T(8,128)(2,1)}, u32[]{:S(2)}, u32[]{:S(2)}) collective-permute-start(bf16[2896,128]{1,0:T(8,128)(2,1)S(1)} %broadcast_select_fusion.2.x_ref), channel_id=1, source_target_pairs={{0,2},{1,3},{2,0},{3,1},{4,6},{5,7},{6,4},{7,5},{8,10},{9,11},{10,... | collective-permute-start | bytes 2224136 | tf_op jit(solution)/shard_map/ppermute | solution.py:440
  54.7 17.1 %collective-permute-start.13 = (bf16[2896,128]{1,0:T(8,128)(2,1)S(1)}, bf16[2896,128]{1,0:T(8,128)(2,1)}, u32[]{:S(2)}, u32[]{:S(2)}) collective-permute-start(bf16[2896,128]{1,0:T(8,128)(2,1)S(1)} %collective-permute-done.10), channel_id=1, source_target_pairs={{4,8},{5,9},{6,10},{7,11},{8,12},{9,13},{10,14},{11,15},{20,24},{2... | collective-permute-start | bytes 2224136 | tf_op jit(solution)/shard_map/ppermute | solution.py:359
  56.2 20.5 %collective-permute-start.14 = (bf16[2896,128]{1,0:T(8,128)(2,1)S(1)}, bf16[2896,128]{1,0:T(8,128)(2,1)}, u32[]{:S(2)}, u32[]{:S(2)}) collective-permute-start(bf16[2896,128]{1,0:T(8,128)(2,1)S(1)} %collective-permute-done.11), channel_id=1, source_target_pairs={{4,0},{5,1},{6,2},{7,3},{8,4},{9,5},{10,6},{11,7},{20,16},{21,17},... | collective-permute-start | bytes 2224136 | tf_op jit(solution)/shard_map/ppermute | solution.py:360
  78.2 16.7 %copy-start.2 = (bf16[2896,128]{1,0:T(8,128)(2,1)}, bf16[2896,128]{1,0:T(8,128)(2,1)S(1)}, u32[]{:S(2)}) copy-start(bf16[2896,128]{1,0:T(8,128)(2,1)S(1)} %get-tuple-element.54.x_ref) | copy-start | bytes 2224132
  78.2 17.1 %collective-permute-start.16 = (bf16[2896,128]{1,0:T(8,128)(2,1)S(1)}, bf16[2896,128]{1,0:T(8,128)(2,1)S(1)}, u32[]{:S(2)}, u32[]{:S(2)}) collective-permute-start(bf16[2896,128]{1,0:T(8,128)(2,1)S(1)} %get-tuple-element.55), channel_id=1, source_target_pairs={{8,12},{9,13},{10,14},{11,15},{4,0},{5,1},{6,2},{7,3},{24,28},{25,... | collective-permute-start | bytes 2224136 | tf_op jit(solution)/shard_map/ppermute | solution.py:356
  79.7 16.0 %collective-permute-start.15 = (bf16[2896,128]{1,0:T(8,128)(2,1)S(1)}, bf16[2896,128]{1,0:T(8,128)(2,1)S(1)}, u32[]{:S(2)}, u32[]{:S(2)}) collective-permute-start(bf16[2896,128]{1,0:T(8,128)(2,1)S(1)} %get-tuple-element.54.x_ref), channel_id=1, source_target_pairs={{0,2},{1,3},{2,0},{3,1},{4,6},{5,7},{6,4},{7,5},{8,10},{9,11},{10,... | collective-permute-start | bytes 2224136 | tf_op jit(solution)/shard_map/ppermute | solution.py:440
  94.9 2.6 %copy-start.14 = (bf16[2880,128]{1,0:T(8,128)(2,1)S(1)}, bf16[2880,128]{1,0:T(8,128)(2,1)}, u32[]{:S(2)}) copy-start(bf16[2880,128]{1,0:T(8,128)(2,1)} %get-tuple-element.56) | copy-start | bytes 2211844
  95.7 7.4 %copy-start.9 = (bf16[2896,128]{1,0:T(8,128)(2,1)}, bf16[2896,128]{1,0:T(8,128)(2,1)S(1)}, u32[]{:S(2)}) copy-start(bf16[2896,128]{1,0:T(8,128)(2,1)S(1)} %collective-permute-done.15.y_ref) | copy-start | bytes 2224132
  95.8 21.3 %copy-start.1 = (bf16[2896,128]{1,0:T(8,128)(2,1)}, bf16[2896,128]{1,0:T(8,128)(2,1)S(1)}, u32[]{:S(2)}) copy-start(bf16[2896,128]{1,0:T(8,128)(2,1)S(1)} %broadcast_select_fusion.x_ref) | copy-start | bytes 2224132
  95.8 21.3 %copy-start.13 = (bf16[2880,128]{1,0:T(8,128)(2,1)S(1)}, bf16[2880,128]{1,0:T(8,128)(2,1)}, u32[]{:S(2)}) copy-start(bf16[2880,128]{1,0:T(8,128)(2,1)} %get-tuple-element.65) | copy-start | bytes 2211844
  95.8 21.3 %collective-permute-start.19 = (bf16[2896,128]{1,0:T(8,128)(2,1)S(1)}, bf16[2896,128]{1,0:T(8,128)(2,1)S(1)}, u32[]{:S(2)}, u32[]{:S(2)}) collective-permute-start(bf16[2896,128]{1,0:T(8,128)(2,1)S(1)} %broadcast_select_fusion.x_ref), channel_id=1, source_target_pairs={{0,2},{1,3},{2,0},{3,1},{4,6},{5,7},{6,4},{7,5},{8,10},{9,11},{10,... | collective-permute-start | bytes 2224136 | tf_op jit(solution)/shard_map/ppermute | solution.py:440
  97.5 19.6 %collective-permute-start.17 = (bf16[2880,128]{1,0:T(8,128)(2,1)S(1)}, bf16[2880,128]{1,0:T(8,128)(2,1)S(1)}, u32[]{:S(2)}, u32[]{:S(2)}) collective-permute-start(bf16[2880,128]{1,0:T(8,128)(2,1)S(1)} %copy-done.14), channel_id=1, source_target_pairs={{0,4},{1,5},{2,6},{3,7},{4,8},{5,9},{6,10},{7,11},{16,20},{17,21},... | collective-permute-start | bytes 2211848 | tf_op jit(solution)/shard_map/ppermute | solution.py:465
  102.4 14.7 %collective-permute-start.18 = (bf16[2880,128]{1,0:T(8,128)(2,1)S(1)}, bf16[2880,128]{1,0:T(8,128)(2,1)S(1)}, u32[]{:S(2)}, u32[]{:S(2)}) collective-permute-start(bf16[2880,128]{1,0:T(8,128)(2,1)S(1)} %copy-done.14), channel_id=1, source_target_pairs={{8,4},{9,5},{10,6},{11,7},{12,8},{13,9},{14,10},{15,11},{24,20},{2... | collective-permute-start | bytes 2211848 | tf_op jit(solution)/shard_map/ppermute | solution.py:465
  117.1 5.2 %copy-start.8 = (bf16[2896,128]{1,0:T(8,128)(2,1)}, bf16[2896,128]{1,0:T(8,128)(2,1)S(1)}, u32[]{:S(2)}) copy-start(bf16[2896,128]{1,0:T(8,128)(2,1)S(1)} %collective-permute-done.19.y_ref) | copy-start | bytes 2224132
  117.2 20.9 %copy-start.5 = (f32[2880,128]{1,0:T(8,128)S(1)}, f32[2880,128]{1,0:T(8,128)}, u32[]{:S(2)}) copy-start(f32[2880,128]{1,0:T(8,128)} %get-tuple-element.57) | copy-start | bytes 4423684
  117.2 19.1 %collective-permute-start.23 = (bf16[2880,128]{1,0:T(8,128)(2,1)S(1)}, bf16[2880,128]{1,0:T(8,128)(2,1)S(1)}, u32[]{:S(2)}, u32[]{:S(2)}) collective-permute-start(bf16[2880,128]{1,0:T(8,128)(2,1)S(1)} %copy-done.13), channel_id=1, source_target_pairs={{8,4},{9,5},{10,6},{11,7},{12,8},{13,9},{14,10},{15,11},{24,20},{2... | collective-permute-start | bytes 2211848 | tf_op jit(solution)/shard_map/ppermute | solution.py:489
  118.0 18.3 %collective-permute-start.22 = (bf16[2880,128]{1,0:T(8,128)(2,1)S(1)}, bf16[2880,128]{1,0:T(8,128)(2,1)S(1)}, u32[]{:S(2)}, u32[]{:S(2)}) collective-permute-start(bf16[2880,128]{1,0:T(8,128)(2,1)S(1)} %copy-done.13), channel_id=1, source_target_pairs={{0,4},{1,5},{2,6},{3,7},{4,8},{5,9},{6,10},{7,11},{16,20},{17,21},... | collective-permute-start | bytes 2211848 | tf_op jit(solution)/shard_map/ppermute | solution.py:489
  121.8 14.9 %collective-permute-start.20 = (bf16[2880,128]{1,0:T(8,128)(2,1)}, bf16[2880,128]{1,0:T(8,128)(2,1)S(1)}, u32[]{:S(2)}, u32[]{:S(2)}) collective-permute-start(bf16[2880,128]{1,0:T(8,128)(2,1)} %get-tuple-element.61), channel_id=1, source_target_pairs={{0,2},{1,3},{2,0},{3,1},{4,6},{5,7},{6,4},{7,5},{8,10},{9,11},{10,... | collective-permute-start | bytes 2211848 | tf_op jit(solution)/shard_map/ppermute | solution.py:484
  136.7 16.9 %collective-permute-start.24 = (bf16[2880,128]{1,0:T(8,128)(2,1)}, bf16[2880,128]{1,0:T(8,128)(2,1)S(1)}, u32[]{:S(2)}, u32[]{:S(2)}) collective-permute-start(bf16[2880,128]{1,0:T(8,128)(2,1)} %get-tuple-element.66), channel_id=1, source_target_pairs={{0,2},{1,3},{2,0},{3,1},{4,6},{5,7},{6,4},{7,5},{8,10},{9,11},{10,... | collective-permute-start | bytes 2211848 | tf_op jit(solution)/shard_map/ppermute | solution.py:484
  138.0 2.2 %copy-start.4 = (f32[2880,128]{1,0:T(8,128)S(1)}, f32[2880,128]{1,0:T(8,128)}, u32[]{:S(2)}) copy-start(f32[2880,128]{1,0:T(8,128)} %get-tuple-element.67) | copy-start | bytes 4423684
  138.2 23.9 %collective-permute-start.21 = (bf16[2880,128]{1,0:T(8,128)(2,1)S(1)}, bf16[2880,128]{1,0:T(8,128)(2,1)S(1)}, u32[]{:S(2)}, u32[]{:S(2)}) collective-permute-start(bf16[2880,128]{1,0:T(8,128)(2,1)S(1)} %add_convert_fusion.3), channel_id=1, source_target_pairs={{0,8},{1,9},{2,10},{3,11},{4,0},{5,1},{6,2},{7,3},{8,12},{9,13},{1... | collective-permute-start | bytes 2211848 | tf_op jit(solution)/shard_map/ppermute | solution.py:495
  140.2 13.9 %copy-start.6 = (f32[2880,128]{1,0:T(8,128)S(1)}, f32[2880,128]{1,0:T(8,128)}, u32[]{:S(2)}) copy-start(f32[2880,128]{1,0:T(8,128)} %get-tuple-element.62) | copy-start | bytes 4423684
  153.6 13.3 %collective-permute-start.27 = (bf16[2880,128]{1,0:T(8,128)(2,1)S(1)}, bf16[2880,128]{1,0:T(8,128)(2,1)S(1)}, u32[]{:S(2)}, u32[]{:S(2)}) collective-permute-start(bf16[2880,128]{1,0:T(8,128)(2,1)S(1)} %add_convert_fusion.1), channel_id=1, source_target_pairs={{0,2},{1,3},{2,0},{3,1},{4,6},{5,7},{6,4},{7,5},{8,10},{9,11},{10,... | collective-permute-start | bytes 2211848 | tf_op jit(solution)/shard_map/ppermute | solution.py:499
  154.1 31.6 %copy-start.3 = (f32[2880,128]{1,0:T(8,128)S(1)}, f32[2880,128]{1,0:T(8,128)}, u32[]{:S(2)}) copy-start(f32[2880,128]{1,0:T(8,128)} %get-tuple-element.47) | copy-start | bytes 4423684
  154.1 31.6 %copy-start.10 = (bf16[2880,128]{1,0:T(8,128)(2,1)S(1)}, bf16[2880,128]{1,0:T(8,128)(2,1)}, u32[]{:S(2)}) copy-start(bf16[2880,128]{1,0:T(8,128)(2,1)} %get-tuple-element.43) | copy-start | bytes 2211844
  154.3 15.7 %collective-permute-start.26 = (bf16[2880,128]{1,0:T(8,128)(2,1)S(1)}, bf16[2880,128]{1,0:T(8,128)(2,1)S(1)}, u32[]{:S(2)}, u32[]{:S(2)}) collective-permute-start(bf16[2880,128]{1,0:T(8,128)(2,1)S(1)} %add_convert_fusion.2), channel_id=1, source_target_pairs={{4,12},{5,13},{6,14},{7,15},{12,0},{13,1},{14,2},{15,3},{20,28},{2... | collective-permute-start | bytes 2211848 | tf_op jit(solution)/shard_map/ppermute | solution.py:502
  155.7 30.0 %collective-permute-start.25 = (bf16[2880,128]{1,0:T(8,128)(2,1)S(1)}, bf16[2880,128]{1,0:T(8,128)(2,1)S(1)}, u32[]{:S(2)}, u32[]{:S(2)}) collective-permute-start(bf16[2880,128]{1,0:T(8,128)(2,1)S(1)} %add_convert_fusion.2), channel_id=1, source_target_pairs={{0,12},{1,13},{2,14},{3,15},{8,0},{9,1},{10,2},{11,3},{16,28},{17,... | collective-permute-start | bytes 2211848 | tf_op jit(solution)/shard_map/ppermute | solution.py:502

commit v3 on v2

--- a/solution.py
+++ b/solution.py
@@ -433,7 +433,7 @@
     arrivals = {1: held}
     cross = lax.ppermute(own, "seq", across)
     block, ready = own, (cross, *held)
-    sums = []
+    sums, slow = [], []
     for j in range(1, planes):
         nearer = [after(x, *ready) for x in arrivals[j]]
         next_block = after(slot_block(arrivals, plane, [o[j - 1] for o in order]), *ready)
@@ -453,9 +453,7 @@
             done = near[0]
         else:
             if j == 3:
-                flows = [(0, near[0])]
-            elif j == 4:
-                flows = [(1, near[1])]
+                flows = [(0, near[0]), (1, near[1])]
             sums.append((j - 1, expert(block, cross, weights, experts, (jnp.float32, half))))
             done = sums[-1][1][1]
         backs = []
@@ -467,9 +465,9 @@
             if side == 0:
                 column_sum = column_sum + back.astype(jnp.float32)
             else:
-                cross_sum = cross_sum + back.astype(jnp.float32)
+                slow.append(back)
         block, cross = next_block, next_cross
-        ready = (next_cross, done, *held, *[back for _, back in backs])
+        ready = (next_cross, done, *held, *[back for side, back in backs if side == 0])
         if held:
             held = [after(x, *ready) for x in held]
             if len(held) == 2 and 2 * (j + 1) >= planes:
@@ -482,20 +480,17 @@
     for n, (j, (mine, theirs)) in enumerate(sums):
         theirs = after(theirs, *ready)
         returned = lax.ppermute(theirs, "seq", across)
-        backs = []
-        if n == 0 and planes <= 4:
-            part = after(near[1], *ready)
-            for moves in rounds([(p, o[0]) for p, o in enumerate(order)]):
-                back = lax.ppermute(part, "seq", line_pairs(moves))
+        if n == 0:
+            slow = [after(back, returned, parts[0]) for back in slow]
+            for back in slow:
                 cross_sum = cross_sum + back.astype(jnp.float32)
-                backs.append(back)
         if pending is not None:
             k, both = pending
             for moves in rounds([(p, o[k - 1]) for p, o in enumerate(order)]):
                 back = lax.ppermute(both, "seq", line_pairs(moves))
                 column_sum = column_sum + back.astype(jnp.float32)
         pending = (j, (mine + returned.astype(jnp.float32)).astype(half))
-        ready = (returned, *backs)
+        ready = (returned, *slow)
     crossing = lax.ppermute(after(cross_sum.astype(half), *ready), "seq", across)
     k, both = pending
     for moves in rounds([(p, o[k - 1]) for p, o in enumerate(order)]):

time: 188 us -> 187 us (level)
  waiting for transfers between devices: 62.4 us -> 60 us
    ppermute x2 -> x4, starting transfers between devices: 5.58 us -> 12.9 us  [on_device(): backs.append((side, lax.ppermute(part, 'seq', line_pairs(moves))))]
    ppermute x3, waiting for transfers between devices: 18.9 us -> 14 us  [on_device(): back = lax.ppermute(both, 'seq', line_pairs(moves))]
    ppermute x2 -> x0, starting transfers between devices: 4.63 us -> none  [on_device(): back = lax.ppermute(part, 'seq', line_pairs(moves))]
    ppermute x2, waiting for transfers between devices: 13.5 us -> 17 us  [on_device(): returned = lax.ppermute(theirs, 'seq', across)]
    ppermute x3, starting transfers between devices: 9.78 us -> 7.7 us  [on_device(): back = lax.ppermute(both, 'seq', line_pairs(moves))]
  transfers between devices with their start and end apart: 28 -> 28, of which waited for: 12 -> 10; matrix products, arithmetic and copies ran while one was open for 3% -> 3% of each run, Pallas kernels for 35% -> 35%
where the time goes in v3:
time: 187 us; the launch traced here: 186 us
  Pallas kernels  67.3 us (36%)
  waiting for transfers between devices  60 us (32%)
  starting transfers between devices  49 us (26%)
  other arithmetic  5.1 us (3%)
  local copies, waits for them, and re-layouts  4.41 us (2%)
    pallas_call x4, Pallas kernels, expert_rows(): pl.pallas_call(functools.partial(expert_kernel, experts), out_shape=[jax....  55.8 us
    ppermute x2, waiting for transfers between devices, on_device(): returned = lax.ppermute(theirs, 'seq', across)  17 us
    ppermute x3, waiting for transfers between devices, on_device(): back = lax.ppermute(both, 'seq', line_pairs(moves))  14 us
    ppermute x2, waiting for transfers between devices, next_blocks(): lax.ppermute(below, 'seq', line_pairs(up))  13.7 us
    ppermute x4, starting transfers between devices, on_device(): backs.append((side, lax.ppermute(part, 'seq', line_pairs(moves))))  12.9 us
    pallas_call x1, Pallas kernels, attended_rows(): pl.pallas_call(functools.partial(attention_kernel, experts), out_shape=(j...  9.7 us
    ppermute x6, starting transfers between devices, summed(): lax.ppermute(block, axis, [(i, i ^ step * m) for i in range(shards)])  9.36 us
    ppermute x2, waiting for transfers between devices, next_blocks(): lax.ppermute(above, 'seq', line_pairs(down))  9.02 us
  transfers between devices with their start and end apart: 28, of which 10 were waited for; matrix products, arithmetic and copies ran while one was open for 3% of the time, Pallas kernels for 35%

profile of v3, /device:TPU:0, one launch (start us, length us, event | category | flops | bytes accessed | tf_op | source)
XLA Modules:
  0.0 186.3 jit_solution(15026763736244780051)
XLA Ops:
  0.0 1.8 shard_map.109
  1.8 2.4 %collective-permute-start.2 = (bf16[16,512]{1,0:T(8,128)(2,1)}, bf16[16,512]{1,0:T(8,128)(2,1)S(1)}, u32[]{:S(2)}, u32[]{:S(2)}) collective-permute-start(bf16[16,512]{1,0:T(8,128)(2,1)} %get-tuple-element.39), channel_id=1, source_target_pairs={{0,3},{1,2},{2,1},{3,0},{4,7},{5,6},{6,5},{7,4},{8,11},{9,10},{10,... | collective-permute-start | bytes 49160 | tf_op jit(solution)/shard_map/ppermute | solution.py:77
  4.2 0.6 collective-permute-start.1
  4.9 2.3 %collective-permute-start.3 = (bf16[128,512]{1,0:T(8,128)(2,1)}, bf16[128,512]{1,0:T(8,128)(2,1)S(1)}, u32[]{:S(2)}, u32[]{:S(2)}) collective-permute-start(bf16[128,512]{1,0:T(8,128)(2,1)} %get-tuple-element.40.local), channel_id=1, source_target_pairs={{0,1},{1,2},{2,3},{3,4},{4,5},{5,6},{6,7},{7,8},{8,9},{9,10},{10,1... | collective-permute-start | bytes 393224 | tf_op jit(solution)/shard_map/ppermute | solution.py:400
  7.2 0.9 collective-permute-done.1
  8.1 0.7 add_add_fusion.1
  8.9 2.0 %collective-permute-start.8 = (bf16[1440,2880]{1,0:T(8,128)(2,1)}, bf16[1440,2880]{1,0:T(8,128)(2,1)}, u32[]{:S(2)}, u32[]{:S(2)}) collective-permute-start(bf16[1440,2880]{1,0:T(8,128)(2,1)} %bitcast.13), channel_id=1, source_target_pairs={{0,1},{1,0},{2,3},{3,2},{4,5},{5,4},{6,7},{7,6},{8,9},{9,8},{10,11... | collective-permute-start | bytes 24883208 | tf_op jit(solution)/shard_map/ppermute | solution.py:408
  10.9 5.7 %collective-permute-start.6 = (bf16[16,512]{1,0:T(8,128)(2,1)S(1)}, bf16[16,512]{1,0:T(8,128)(2,1)S(1)}, u32[]{:S(2)}, u32[]{:S(2)}) collective-permute-start(bf16[16,512]{1,0:T(8,128)(2,1)S(1)} %add_add_fusion.1), channel_id=1, source_target_pairs={{0,12},{1,13},{2,14},{3,15},{4,8},{5,9},{6,10},{7,11},{8,4},{9,5},... | collective-permute-start | bytes 49160 | tf_op jit(solution)/shard_map/ppermute | solution.py:77
  16.6 0.6 collective-permute-start.4
  17.1 2.2 %broadcast_in_dim.4.gain = f32[2880,1]{1,0:T(8,128)} reshape(f32[2880]{0:T(1024)} %param.17) | data formatting | bytes 23040 | tf_op jit(solution)/shard_map/broadcast_in_dim | solution.py:419
  19.4 1.0 copy.13
  20.4 0.8 collective-permute-done.5
  21.2 0.6 add_add_fusion.sinks
  21.8 9.7 %shard_map.110 = (bf16[2880,128]{1,0:T(8,128)(2,1)}, bf16[2896,128]{1,0:T(8,128)(2,1)}) custom-call(bf16[2048,128]{1,0:T(8,128)(2,1)} %bitcast.24, bf16[128,512]{1,0:T(8,128)(2,1)} %copy-done.12, bf16[128,512]{1,0:T(8,128)(2,1)} %get-tuple-element.40.local, bf16[16,512]{1,0:T(8,128)(2,1)} %add_add_fusion.sinks, f32[272,128]{1,0:T(8,128)} %get-tuple-element.44.bias, ...), custom_call_target="tpu_custom_call" | custom-call | flops 1509949440 | bytes 11796480 | tf_op jit(solution)/shard_map/pallas_call | solution.py:209
  31.5 2.6 %collective-permute-start.10 = (bf16[2896,128]{1,0:T(8,128)(2,1)}, bf16[2896,128]{1,0:T(8,128)(2,1)S(1)}, u32[]{:S(2)}, u32[]{:S(2)}) collective-permute-start(bf16[2896,128]{1,0:T(8,128)(2,1)} %get-tuple-element.46.x_ref), channel_id=1, source_target_pairs={{0,4},{1,5},{2,6},{3,7},{4,8},{5,9},{6,10},{7,11},{8,12},{9,13},{1... | collective-permute-start | bytes 2224136 | tf_op jit(solution)/shard_map/ppermute | solution.py:359
  34.1 1.3 collective-permute-start.11
  35.4 0.7 collective-permute-start.7
  36.1 13.7 %collective-permute-done.10 = bf16[2896,128]{1,0:T(8,128)(2,1)S(1)} collective-permute-done((bf16[2896,128]{1,0:T(8,128)(2,1)}, bf16[2896,128]{1,0:T(8,128)(2,1)S(1)}, u32[]{:S(2)}, u32[]{:S(2)}) %collective-permute-start.10) | collective-permute-done | bytes 741408 | tf_op jit(solution)/shard_map/ppermute | solution.py:359
  49.8 4.1 %collective-permute-done.11 = bf16[2896,128]{1,0:T(8,128)(2,1)S(1)} collective-permute-done((bf16[2896,128]{1,0:T(8,128)(2,1)}, bf16[2896,128]{1,0:T(8,128)(2,1)S(1)}, u32[]{:S(2)}, u32[]{:S(2)}) %collective-permute-start.11) | collective-permute-done | bytes 741408 | tf_op jit(solution)/shard_map/ppermute | solution.py:360
  54.0 0.7 collective-permute-start.12
  54.7 1.5 collective-permute-start.13
  56.2 1.3 collective-permute-start.14
  57.6 14.2 %shard_map.111 = (f32[2880,128]{1,0:T(8,128)}, f32[2880,128]{1,0:T(8,128)}) custom-call(s32[1]{0:T(128)} %bitcast.6.me_ref, bf16[2896,128]{1,0:T(8,128)(2,1)} %get-tuple-element.46.x_ref, bf16[2896,128]{1,0:T(8,128)(2,1)} %copy-done.7, bf16[1440,2880]{1,0:T(8,128)(2,1)} %bitcast.14, bf16[1440,2880]{1,0:T(8,128)(2,1)} %collective-permute-done.8.gu1, ...), custom_call_target="tpu_custom_call" | custom-call | flops 6370099200 | bytes 24883200 | tf_op jit(solution)/shard_map/pallas_call | solution.py:300
  71.8 5.0 %collective-permute-done.14 = bf16[2896,128]{1,0:T(8,128)(2,1)} collective-permute-done((bf16[2896,128]{1,0:T(8,128)(2,1)S(1)}, bf16[2896,128]{1,0:T(8,128)(2,1)}, u32[]{:S(2)}, u32[]{:S(2)}) %collective-permute-start.14) | collective-permute-done | bytes 741408 | tf_op jit(solution)/shard_map/ppermute | solution.py:360
  76.8 1.4 select_select_fusion
  78.2 1.5 collective-permute-start.15
  79.7 1.5 collective-permute-start.16
  81.1 13.7 %shard_map.112 = (bf16[2880,128]{1,0:T(8,128)(2,1)}, bf16[2880,128]{1,0:T(8,128)(2,1)}) custom-call(s32[1]{0:T(128)} %bitcast.6.me_ref, bf16[2896,128]{1,0:T(8,128)(2,1)} %copy-done, bf16[2896,128]{1,0:T(8,128)(2,1)} %collective-permute-done.12.y_ref, bf16[1440,2880]{1,0:T(8,128)(2,1)} %bitcast.15, bf16[1440,2880]{1,0:T(8,128)(2,1)} %collective-permute-done.8.gu1, ...), custom_call_target="tpu_custom_call" | custom-call | flops 6370099200 | bytes 24883200 | tf_op jit(solution)/shard_map/pallas_call | solution.py:300
  94.9 1.6 collective-permute-done.16
  96.6 0.7 collective-permute-start.19
  97.3 3.0 %collective-permute-start.17 = (bf16[2880,128]{1,0:T(8,128)(2,1)}, bf16[2880,128]{1,0:T(8,128)(2,1)S(1)}, u32[]{:S(2)}, u32[]{:S(2)}) collective-permute-start(bf16[2880,128]{1,0:T(8,128)(2,1)} %get-tuple-element.58), channel_id=1, source_target_pairs={{0,4},{1,5},{2,6},{3,7},{4,8},{5,9},{6,10},{7,11},{16,20},{17,21},... | collective-permute-start | bytes 2211848 | tf_op jit(solution)/shard_map/ppermute | solution.py:463
  100.3 0.7 collective-permute-start.18
  101.0 0.7 collective-permute-start.23
  101.8 14.0 %shard_map.113 = (f32[2880,128]{1,0:T(8,128)}, bf16[2880,128]{1,0:T(8,128)(2,1)}) custom-call(s32[1]{0:T(128)} %bitcast.6.me_ref, bf16[2896,128]{1,0:T(8,128)(2,1)} %copy-done.2, bf16[2896,128]{1,0:T(8,128)(2,1)} %copy-done.8, bf16[1440,2880]{1,0:T(8,128)(2,1)} %bitcast.16, bf16[1440,2880]{1,0:T(8,128)(2,1)} %collective-permute-done.8.gu1, ...), custom_call_target="tpu_custom_call" | custom-call | flops 6370099200 | bytes 24883200 | tf_op jit(solution)/shard_map/pallas_call | solution.py:300
  115.8 1.5 collective-permute-start.20
  117.3 8.5 %collective-permute-start.22 = (bf16[2880,128]{1,0:T(8,128)(2,1)}, bf16[2880,128]{1,0:T(8,128)(2,1)S(1)}, u32[]{:S(2)}, u32[]{:S(2)}) collective-permute-start(bf16[2880,128]{1,0:T(8,128)(2,1)} %get-tuple-element.67), channel_id=1, source_target_pairs={{0,4},{1,5},{2,6},{3,7},{4,8},{5,9},{6,10},{7,11},{16,20},{17,21},... | collective-permute-start | bytes 2211848 | tf_op jit(solution)/shard_map/ppermute | solution.py:463
  125.8 13.9 %shard_map.114 = (f32[2880,128]{1,0:T(8,128)}, bf16[2880,128]{1,0:T(8,128)(2,1)}) custom-call(s32[1]{0:T(128)} %bitcast.6.me_ref, bf16[2896,128]{1,0:T(8,128)(2,1)} %copy-done.1, bf16[2896,128]{1,0:T(8,128)(2,1)} %copy-done.9, bf16[1440,2880]{1,0:T(8,128)(2,1)} %bitcast.17, bf16[1440,2880]{1,0:T(8,128)(2,1)} %collective-permute-done.8.gu1, ...), custom_call_target="tpu_custom_call" | custom-call | flops 6370099200 | bytes 24883200 | tf_op jit(solution)/shard_map/pallas_call | solution.py:300
  139.7 0.8 collective-permute-start.24
  140.8 1.1 copy-done.4
  141.9 0.2 add_convert_fusion.1
  142.2 17.0 %collective-permute-done.24 = bf16[2880,128]{1,0:T(8,128)(2,1)S(1)} collective-permute-done((bf16[2880,128]{1,0:T(8,128)(2,1)}, bf16[2880,128]{1,0:T(8,128)(2,1)S(1)}, u32[]{:S(2)}, u32[]{:S(2)}) %collective-permute-start.24) | collective-permute-done | bytes 737312 | tf_op jit(solution)/shard_map/ppermute | solution.py:482
  159.2 0.7 collective-permute-start.27
  160.1 1.3 collective-permute-start.26
  161.4 6.3 %collective-permute-start.25 = (bf16[2880,128]{1,0:T(8,128)(2,1)S(1)}, bf16[2880,128]{1,0:T(8,128)(2,1)S(1)}, u32[]{:S(2)}, u32[]{:S(2)}) collective-permute-start(bf16[2880,128]{1,0:T(8,128)(2,1)S(1)} %add_convert_fusion.2), channel_id=1, source_target_pairs={{0,12},{1,13},{2,14},{3,15},{8,0},{9,1},{10,2},{11,3},{16,28},{17,... | collective-permute-start | bytes 2211848 | tf_op jit(solution)/shard_map/ppermute | solution.py:497
  167.8 2.9 %collective-permute-done.27 = bf16[2880,128]{1,0:T(8,128)(2,1)S(1)} collective-permute-done((bf16[2880,128]{1,0:T(8,128)(2,1)S(1)}, bf16[2880,128]{1,0:T(8,128)(2,1)S(1)}, u32[]{:S(2)}, u32[]{:S(2)}) %collective-permute-start.27) | collective-permute-done | bytes 737312 | tf_op jit(solution)/shard_map/ppermute | solution.py:494
  170.7 4.7 %collective-permute-done.26 = bf16[2880,128]{1,0:T(8,128)(2,1)S(1)} collective-permute-done((bf16[2880,128]{1,0:T(8,128)(2,1)S(1)}, bf16[2880,128]{1,0:T(8,128)(2,1)S(1)}, u32[]{:S(2)}, u32[]{:S(2)}) %collective-permute-start.26) | collective-permute-done | bytes 737312 | tf_op jit(solution)/shard_map/ppermute | solution.py:497
  175.4 9.3 %collective-permute-done.25 = bf16[2880,128]{1,0:T(8,128)(2,1)S(1)} collective-permute-done((bf16[2880,128]{1,0:T(8,128)(2,1)S(1)}, bf16[2880,128]{1,0:T(8,128)(2,1)S(1)}, u32[]{:S(2)}, u32[]{:S(2)}) %collective-permute-start.25) | collective-permute-done | bytes 737312 | tf_op jit(solution)/shard_map/ppermute | solution.py:497
  184.6 1.6 fusion
  (51 shorter events, 0.8 us)
Async XLA Ops:
  0.0 19.4 %copy-start.11 = (bf16[128,2048]{1,0:T(8,128)(2,1)S(1)}, bf16[128,2048]{1,0:T(8,128)(2,1)}, u32[]{:S(2)}) copy-start(bf16[128,2048]{1,0:T(8,128)(2,1)} %param.11) | copy-start | bytes 1572868
  1.8 5.4 %collective-permute-start.2 = (bf16[16,512]{1,0:T(8,128)(2,1)}, bf16[16,512]{1,0:T(8,128)(2,1)S(1)}, u32[]{:S(2)}, u32[]{:S(2)}) collective-permute-start(bf16[16,512]{1,0:T(8,128)(2,1)} %get-tuple-element.39), channel_id=1, source_target_pairs={{0,3},{1,2},{2,1},{3,0},{4,7},{5,6},{6,5},{7,4},{8,11},{9,10},{10,... | collective-permute-start | bytes 49160 | tf_op jit(solution)/shard_map/ppermute | solution.py:77
  4.2 3.9 %collective-permute-start.1 = (bf16[16,512]{1,0:T(8,128)(2,1)}, bf16[16,512]{1,0:T(8,128)(2,1)S(1)}, u32[]{:S(2)}, u32[]{:S(2)}) collective-permute-start(bf16[16,512]{1,0:T(8,128)(2,1)} %get-tuple-element.39), channel_id=1, source_target_pairs={{0,2},{1,3},{2,0},{3,1},{4,6},{5,7},{6,4},{7,5},{8,10},{9,11},{10,... | collective-permute-start | bytes 49160 | tf_op jit(solution)/shard_map/ppermute | solution.py:77
  4.8 3.4 %collective-permute-start = (bf16[16,512]{1,0:T(8,128)(2,1)}, bf16[16,512]{1,0:T(8,128)(2,1)S(1)}, u32[]{:S(2)}, u32[]{:S(2)}) collective-permute-start(bf16[16,512]{1,0:T(8,128)(2,1)} %get-tuple-element.39), channel_id=1, source_target_pairs={{0,1},{1,0},{2,3},{3,2},{4,5},{5,4},{6,7},{7,6},{8,9},{9,8},{10,11... | collective-permute-start | bytes 49160 | tf_op jit(solution)/shard_map/ppermute | solution.py:77
  4.9 4.0 %collective-permute-start.3 = (bf16[128,512]{1,0:T(8,128)(2,1)}, bf16[128,512]{1,0:T(8,128)(2,1)S(1)}, u32[]{:S(2)}, u32[]{:S(2)}) collective-permute-start(bf16[128,512]{1,0:T(8,128)(2,1)} %get-tuple-element.40.local), channel_id=1, source_target_pairs={{0,1},{1,2},{2,3},{3,4},{4,5},{5,6},{6,7},{7,8},{8,9},{9,10},{10,1... | collective-permute-start | bytes 393224 | tf_op jit(solution)/shard_map/ppermute | solution.py:400
  8.9 13.0 %copy-start.12 = (bf16[128,512]{1,0:T(8,128)(2,1)}, bf16[128,512]{1,0:T(8,128)(2,1)S(1)}, u32[]{:S(2)}) copy-start(bf16[128,512]{1,0:T(8,128)(2,1)S(1)} %collective-permute-done.3.halo) | copy-start | bytes 393220
  8.9 48.7 %collective-permute-start.8 = (bf16[1440,2880]{1,0:T(8,128)(2,1)}, bf16[1440,2880]{1,0:T(8,128)(2,1)}, u32[]{:S(2)}, u32[]{:S(2)}) collective-permute-start(bf16[1440,2880]{1,0:T(8,128)(2,1)} %bitcast.13), channel_id=1, source_target_pairs={{0,1},{1,0},{2,3},{3,2},{4,5},{5,4},{6,7},{7,6},{8,9},{9,8},{10,11... | collective-permute-start | bytes 24883208 | tf_op jit(solution)/shard_map/ppermute | solution.py:408
  10.9 46.7 %collective-permute-start.9 = (bf16[720,2880]{1,0:T(8,128)(2,1)}, bf16[720,2880]{1,0:T(8,128)(2,1)}, u32[]{:S(2)}, u32[]{:S(2)}) collective-permute-start(bf16[720,2880]{1,0:T(8,128)(2,1)} %bitcast.18), channel_id=1, source_target_pairs={{0,1},{1,0},{2,3},{3,2},{4,5},{5,4},{6,7},{7,6},{8,9},{9,8},{10,11... | collective-permute-start | bytes 12441608 | tf_op jit(solution)/shard_map/ppermute | solution.py:409
  10.9 9.5 %collective-permute-start.6 = (bf16[16,512]{1,0:T(8,128)(2,1)S(1)}, bf16[16,512]{1,0:T(8,128)(2,1)S(1)}, u32[]{:S(2)}, u32[]{:S(2)}) collective-permute-start(bf16[16,512]{1,0:T(8,128)(2,1)S(1)} %add_add_fusion.1), channel_id=1, source_target_pairs={{0,12},{1,13},{2,14},{3,15},{4,8},{5,9},{6,10},{7,11},{8,4},{9,5},... | collective-permute-start | bytes 49160 | tf_op jit(solution)/shard_map/ppermute | solution.py:77
  16.6 4.6 %collective-permute-start.5 = (bf16[16,512]{1,0:T(8,128)(2,1)S(1)}, bf16[16,512]{1,0:T(8,128)(2,1)S(1)}, u32[]{:S(2)}, u32[]{:S(2)}) collective-permute-start(bf16[16,512]{1,0:T(8,128)(2,1)S(1)} %add_add_fusion.1), channel_id=1, source_target_pairs={{0,8},{1,9},{2,10},{3,11},{4,12},{5,13},{6,14},{7,15},{8,0},{9,1},... | collective-permute-start | bytes 49160 | tf_op jit(solution)/shard_map/ppermute | solution.py:77
  16.6 4.6 %collective-permute-start.4 = (bf16[16,512]{1,0:T(8,128)(2,1)S(1)}, bf16[16,512]{1,0:T(8,128)(2,1)S(1)}, u32[]{:S(2)}, u32[]{:S(2)}) collective-permute-start(bf16[16,512]{1,0:T(8,128)(2,1)S(1)} %add_add_fusion.1), channel_id=1, source_target_pairs={{0,4},{1,5},{2,6},{3,7},{4,0},{5,1},{6,2},{7,3},{8,12},{9,13},{10,... | collective-permute-start | bytes 49160 | tf_op jit(solution)/shard_map/ppermute | solution.py:77
  31.5 18.3 %collective-permute-start.10 = (bf16[2896,128]{1,0:T(8,128)(2,1)}, bf16[2896,128]{1,0:T(8,128)(2,1)S(1)}, u32[]{:S(2)}, u32[]{:S(2)}) collective-permute-start(bf16[2896,128]{1,0:T(8,128)(2,1)} %get-tuple-element.46.x_ref), channel_id=1, source_target_pairs={{0,4},{1,5},{2,6},{3,7},{4,8},{5,9},{6,10},{7,11},{8,12},{9,13},{1... | collective-permute-start | bytes 2224136 | tf_op jit(solution)/shard_map/ppermute | solution.py:359
  34.1 19.8 %collective-permute-start.11 = (bf16[2896,128]{1,0:T(8,128)(2,1)}, bf16[2896,128]{1,0:T(8,128)(2,1)S(1)}, u32[]{:S(2)}, u32[]{:S(2)}) collective-permute-start(bf16[2896,128]{1,0:T(8,128)(2,1)} %get-tuple-element.46.x_ref), channel_id=1, source_target_pairs={{4,0},{5,1},{6,2},{7,3},{8,4},{9,5},{10,6},{11,7},{12,8},{13,9},{1... | collective-permute-start | bytes 2224136 | tf_op jit(solution)/shard_map/ppermute | solution.py:360
  35.4 18.6 %collective-permute-start.7 = (bf16[2896,128]{1,0:T(8,128)(2,1)}, bf16[2896,128]{1,0:T(8,128)(2,1)S(1)}, u32[]{:S(2)}, u32[]{:S(2)}) collective-permute-start(bf16[2896,128]{1,0:T(8,128)(2,1)} %get-tuple-element.46.x_ref), channel_id=1, source_target_pairs={{0,2},{1,3},{2,0},{3,1},{4,6},{5,7},{6,4},{7,5},{8,10},{9,11},{10,... | collective-permute-start | bytes 2224136 | tf_op jit(solution)/shard_map/ppermute | solution.py:434
  54.0 17.8 %copy-start = (bf16[2896,128]{1,0:T(8,128)(2,1)}, bf16[2896,128]{1,0:T(8,128)(2,1)S(1)}, u32[]{:S(2)}) copy-start(bf16[2896,128]{1,0:T(8,128)(2,1)S(1)} %broadcast_select_fusion.2.x_ref) | copy-start | bytes 2224132
  54.0 3.5 %copy-start.7 = (bf16[2896,128]{1,0:T(8,128)(2,1)}, bf16[2896,128]{1,0:T(8,128)(2,1)S(1)}, u32[]{:S(2)}) copy-start(bf16[2896,128]{1,0:T(8,128)(2,1)S(1)} %collective-permute-done.7.y_ref) | copy-start | bytes 2224132
  54.0 17.8 %collective-permute-start.12 = (bf16[2896,128]{1,0:T(8,128)(2,1)S(1)}, bf16[2896,128]{1,0:T(8,128)(2,1)}, u32[]{:S(2)}, u32[]{:S(2)}) collective-permute-start(bf16[2896,128]{1,0:T(8,128)(2,1)S(1)} %broadcast_select_fusion.2.x_ref), channel_id=1, source_target_pairs={{0,2},{1,3},{2,0},{3,1},{4,6},{5,7},{6,4},{7,5},{8,10},{9,11},{10,... | collective-permute-start | bytes 2224136 | tf_op jit(solution)/shard_map/ppermute | solution.py:440
  54.7 17.1 %collective-permute-start.13 = (bf16[2896,128]{1,0:T(8,128)(2,1)S(1)}, bf16[2896,128]{1,0:T(8,128)(2,1)}, u32[]{:S(2)}, u32[]{:S(2)}) collective-permute-start(bf16[2896,128]{1,0:T(8,128)(2,1)S(1)} %collective-permute-done.10), channel_id=1, source_target_pairs={{4,8},{5,9},{6,10},{7,11},{8,12},{9,13},{10,14},{11,15},{20,24},{2... | collective-permute-start | bytes 2224136 | tf_op jit(solution)/shard_map/ppermute | solution.py:359
  56.2 20.5 %collective-permute-start.14 = (bf16[2896,128]{1,0:T(8,128)(2,1)S(1)}, bf16[2896,128]{1,0:T(8,128)(2,1)}, u32[]{:S(2)}, u32[]{:S(2)}) collective-permute-start(bf16[2896,128]{1,0:T(8,128)(2,1)S(1)} %collective-permute-done.11), channel_id=1, source_target_pairs={{4,0},{5,1},{6,2},{7,3},{8,4},{9,5},{10,6},{11,7},{20,16},{21,17},... | collective-permute-start | bytes 2224136 | tf_op jit(solution)/shard_map/ppermute | solution.py:360
  78.2 16.7 %copy-start.2 = (bf16[2896,128]{1,0:T(8,128)(2,1)}, bf16[2896,128]{1,0:T(8,128)(2,1)S(1)}, u32[]{:S(2)}) copy-start(bf16[2896,128]{1,0:T(8,128)(2,1)S(1)} %get-tuple-element.56.x_ref) | copy-start | bytes 2224132
  78.2 16.7 %collective-permute-start.15 = (bf16[2896,128]{1,0:T(8,128)(2,1)S(1)}, bf16[2896,128]{1,0:T(8,128)(2,1)S(1)}, u32[]{:S(2)}, u32[]{:S(2)}) collective-permute-start(bf16[2896,128]{1,0:T(8,128)(2,1)S(1)} %get-tuple-element.56.x_ref), channel_id=1, source_target_pairs={{0,2},{1,3},{2,0},{3,1},{4,6},{5,7},{6,4},{7,5},{8,10},{9,11},{10,... | collective-permute-start | bytes 2224136 | tf_op jit(solution)/shard_map/ppermute | solution.py:440
  79.7 16.8 %collective-permute-start.16 = (bf16[2896,128]{1,0:T(8,128)(2,1)S(1)}, bf16[2896,128]{1,0:T(8,128)(2,1)S(1)}, u32[]{:S(2)}, u32[]{:S(2)}) collective-permute-start(bf16[2896,128]{1,0:T(8,128)(2,1)S(1)} %get-tuple-element.57), channel_id=1, source_target_pairs={{8,12},{9,13},{10,14},{11,15},{4,0},{5,1},{6,2},{7,3},{24,28},{25,... | collective-permute-start | bytes 2224136 | tf_op jit(solution)/shard_map/ppermute | solution.py:356
  94.9 6.9 %copy-start.8 = (bf16[2896,128]{1,0:T(8,128)(2,1)}, bf16[2896,128]{1,0:T(8,128)(2,1)S(1)}, u32[]{:S(2)}) copy-start(bf16[2896,128]{1,0:T(8,128)(2,1)S(1)} %collective-permute-done.15.y_ref) | copy-start | bytes 2224132
  96.6 19.2 %copy-start.1 = (bf16[2896,128]{1,0:T(8,128)(2,1)}, bf16[2896,128]{1,0:T(8,128)(2,1)S(1)}, u32[]{:S(2)}) copy-start(bf16[2896,128]{1,0:T(8,128)(2,1)S(1)} %broadcast_select_fusion.x_ref) | copy-start | bytes 2224132
  96.6 19.2 %collective-permute-start.19 = (bf16[2896,128]{1,0:T(8,128)(2,1)S(1)}, bf16[2896,128]{1,0:T(8,128)(2,1)S(1)}, u32[]{:S(2)}, u32[]{:S(2)}) collective-permute-start(bf16[2896,128]{1,0:T(8,128)(2,1)S(1)} %broadcast_select_fusion.x_ref), channel_id=1, source_target_pairs={{0,2},{1,3},{2,0},{3,1},{4,6},{5,7},{6,4},{7,5},{8,10},{9,11},{10,... | collective-permute-start | bytes 2224136 | tf_op jit(solution)/shard_map/ppermute | solution.py:440
  97.3 18.5 %collective-permute-start.17 = (bf16[2880,128]{1,0:T(8,128)(2,1)}, bf16[2880,128]{1,0:T(8,128)(2,1)S(1)}, u32[]{:S(2)}, u32[]{:S(2)}) collective-permute-start(bf16[2880,128]{1,0:T(8,128)(2,1)} %get-tuple-element.58), channel_id=1, source_target_pairs={{0,4},{1,5},{2,6},{3,7},{4,8},{5,9},{6,10},{7,11},{16,20},{17,21},... | collective-permute-start | bytes 2211848 | tf_op jit(solution)/shard_map/ppermute | solution.py:463
  100.3 15.4 %collective-permute-start.18 = (bf16[2880,128]{1,0:T(8,128)(2,1)}, bf16[2880,128]{1,0:T(8,128)(2,1)S(1)}, u32[]{:S(2)}, u32[]{:S(2)}) collective-permute-start(bf16[2880,128]{1,0:T(8,128)(2,1)} %get-tuple-element.58), channel_id=1, source_target_pairs={{8,4},{9,5},{10,6},{11,7},{12,8},{13,9},{14,10},{15,11},{24,20},{2... | collective-permute-start | bytes 2211848 | tf_op jit(solution)/shard_map/ppermute | solution.py:463
  101.0 38.7 %collective-permute-start.23 = (bf16[2880,128]{1,0:T(8,128)(2,1)}, bf16[2880,128]{1,0:T(8,128)(2,1)S(1)}, u32[]{:S(2)}, u32[]{:S(2)}) collective-permute-start(bf16[2880,128]{1,0:T(8,128)(2,1)} %get-tuple-element.67), channel_id=1, source_target_pairs={{8,4},{9,5},{10,6},{11,7},{12,8},{13,9},{14,10},{15,11},{24,20},{2... | collective-permute-start | bytes 2211848 | tf_op jit(solution)/shard_map/ppermute | solution.py:463
  115.8 10.0 %copy-start.9 = (bf16[2896,128]{1,0:T(8,128)(2,1)}, bf16[2896,128]{1,0:T(8,128)(2,1)S(1)}, u32[]{:S(2)}) copy-start(bf16[2896,128]{1,0:T(8,128)(2,1)S(1)} %collective-permute-done.19.y_ref) | copy-start | bytes 2224132
  115.8 24.8 %copy-start.5 = (f32[2880,128]{1,0:T(8,128)S(1)}, f32[2880,128]{1,0:T(8,128)}, u32[]{:S(2)}) copy-start(f32[2880,128]{1,0:T(8,128)} %get-tuple-element.59) | copy-start | bytes 4423684
  115.8 23.9 %collective-permute-start.20 = (bf16[2880,128]{1,0:T(8,128)(2,1)}, bf16[2880,128]{1,0:T(8,128)(2,1)S(1)}, u32[]{:S(2)}, u32[]{:S(2)}) collective-permute-start(bf16[2880,128]{1,0:T(8,128)(2,1)} %get-tuple-element.63), channel_id=1, source_target_pairs={{0,2},{1,3},{2,0},{3,1},{4,6},{5,7},{6,4},{7,5},{8,10},{9,11},{10,... | collective-permute-start | bytes 2211848 | tf_op jit(solution)/shard_map/ppermute | solution.py:482
  117.3 22.5 %collective-permute-start.22 = (bf16[2880,128]{1,0:T(8,128)(2,1)}, bf16[2880,128]{1,0:T(8,128)(2,1)S(1)}, u32[]{:S(2)}, u32[]{:S(2)}) collective-permute-start(bf16[2880,128]{1,0:T(8,128)(2,1)} %get-tuple-element.67), channel_id=1, source_target_pairs={{0,4},{1,5},{2,6},{3,7},{4,8},{5,9},{6,10},{7,11},{16,20},{17,21},... | collective-permute-start | bytes 2211848 | tf_op jit(solution)/shard_map/ppermute | solution.py:463
  139.7 19.5 %collective-permute-start.24 = (bf16[2880,128]{1,0:T(8,128)(2,1)}, bf16[2880,128]{1,0:T(8,128)(2,1)S(1)}, u32[]{:S(2)}, u32[]{:S(2)}) collective-permute-start(bf16[2880,128]{1,0:T(8,128)(2,1)} %get-tuple-element.70), channel_id=1, source_target_pairs={{0,2},{1,3},{2,0},{3,1},{4,6},{5,7},{6,4},{7,5},{8,10},{9,11},{10,... | collective-permute-start | bytes 2211848 | tf_op jit(solution)/shard_map/ppermute | solution.py:482
  140.6 1.4 copy-start.4
  140.8 27.0 %collective-permute-start.21 = (bf16[2880,128]{1,0:T(8,128)(2,1)S(1)}, bf16[2880,128]{1,0:T(8,128)(2,1)S(1)}, u32[]{:S(2)}, u32[]{:S(2)}) collective-permute-start(bf16[2880,128]{1,0:T(8,128)(2,1)S(1)} %add_convert_fusion.3), channel_id=1, source_target_pairs={{0,8},{1,9},{2,10},{3,11},{4,0},{5,1},{6,2},{7,3},{8,12},{9,13},{1... | collective-permute-start | bytes 2211848 | tf_op jit(solution)/shard_map/ppermute | solution.py:490
  141.9 18.0 %copy-start.6 = (f32[2880,128]{1,0:T(8,128)S(1)}, f32[2880,128]{1,0:T(8,128)}, u32[]{:S(2)}) copy-start(f32[2880,128]{1,0:T(8,128)} %get-tuple-element.64) | copy-start | bytes 4423684
  142.2 42.5 %copy-start.3 = (f32[2880,128]{1,0:T(8,128)S(1)}, f32[2880,128]{1,0:T(8,128)}, u32[]{:S(2)}) copy-start(f32[2880,128]{1,0:T(8,128)} %get-tuple-element.49) | copy-start | bytes 4423684
  142.2 42.4 %copy-start.10 = (bf16[2880,128]{1,0:T(8,128)(2,1)S(1)}, bf16[2880,128]{1,0:T(8,128)(2,1)}, u32[]{:S(2)}) copy-start(bf16[2880,128]{1,0:T(8,128)(2,1)} %get-tuple-element.45) | copy-start | bytes 2211844
  159.2 11.5 %collective-permute-start.27 = (bf16[2880,128]{1,0:T(8,128)(2,1)S(1)}, bf16[2880,128]{1,0:T(8,128)(2,1)S(1)}, u32[]{:S(2)}, u32[]{:S(2)}) collective-permute-start(bf16[2880,128]{1,0:T(8,128)(2,1)S(1)} %add_convert_fusion.1), channel_id=1, source_target_pairs={{0,2},{1,3},{2,0},{3,1},{4,6},{5,7},{6,4},{7,5},{8,10},{9,11},{10,... | collective-permute-start | bytes 2211848 | tf_op jit(solution)/shard_map/ppermute | solution.py:494
  160.1 15.3 %collective-permute-start.26 = (bf16[2880,128]{1,0:T(8,128)(2,1)S(1)}, bf16[2880,128]{1,0:T(8,128)(2,1)S(1)}, u32[]{:S(2)}, u32[]{:S(2)}) collective-permute-start(bf16[2880,128]{1,0:T(8,128)(2,1)S(1)} %add_convert_fusion.2), channel_id=1, source_target_pairs={{4,12},{5,13},{6,14},{7,15},{12,0},{13,1},{14,2},{15,3},{20,28},{2... | collective-permute-start | bytes 2211848 | tf_op jit(solution)/shard_map/ppermute | solution.py:497
  161.4 23.2 %collective-permute-start.25 = (bf16[2880,128]{1,0:T(8,128)(2,1)S(1)}, bf16[2880,128]{1,0:T(8,128)(2,1)S(1)}, u32[]{:S(2)}, u32[]{:S(2)}) collective-permute-start(bf16[2880,128]{1,0:T(8,128)(2,1)S(1)} %add_convert_fusion.2), channel_id=1, source_target_pairs={{0,12},{1,13},{2,14},{3,15},{8,0},{9,1},{10,2},{11,3},{16,28},{17,... | collective-permute-start | bytes 2211848 | tf_op jit(solution)/shard_map/ppermute | solution.py:497

commit v4 on v3

--- a/solution.py
+++ b/solution.py
@@ -398,9 +398,12 @@
         my_index.reshape(1), sink_positions, key_rows, value_rows
     )
     halo_rows = lax.ppermute(local_rows, "seq", [(i, i + 1) for i in range(shards - 1)])
-    later = (query_rows, gate_up, down_proj)
-    sink_rows, halo_rows, later = summed(sink_rows, "seq", halo_rows, later)
-    query_rows, gate_up, down_proj = later
+    sink_rows, halo_rows, query_rows = summed(sink_rows, "seq", halo_rows, query_rows)
+    query_t = query_rows.T
+    gain = jnp.broadcast_to(norm_gain[:, None], (width, rows_dev))
+    gate_up, down_proj, query_t, gain, sink_rows = lax.optimization_barrier(
+        (gate_up, down_proj, query_t, gain, sink_rows)
+    )
 
     to_core = [(i, i ^ 1) for i in range(shards)]
     gu_own = jnp.swapaxes(gate_up[0], 0, 1)
@@ -410,13 +413,13 @@
     weights = (gu_own, gu_other, dn_own, dn_other)
 
     hidden_state, own = attended_rows(
-        query_rows.T,
+        query_t,
         halo_rows,
         local_rows,
         sink_rows,
         bias,
         residual.T,
-        norm_gain[:, None],
+        gain,
         expert_ids.T,
         route_weights.T,
         out_proj.T,

time: 187 us -> 191 us (1.021)
  waiting for transfers between devices: 60 us -> 64.3 us
    ppermute x1, starting transfers between devices: 1.99 us -> 0.01 us  [on_device(): gu_other = lax.ppermute(gu_own, 'seq', to_core)]
    ppermute x2, waiting for transfers between devices: 9.02 us -> 10.9 us  [next_blocks(): lax.ppermute(above, 'seq', line_pairs(down))]
  transfers between devices with their start and end apart: 28 -> 28, of which waited for: 10 -> 10; matrix products, arithmetic and copies ran while one was open for 3% -> 2% of each run, Pallas kernels for 35% -> 34%
where the time goes in v4:
time: 191 us; the launch traced here: 190 us
  Pallas kernels  67 us (35%)
  waiting for transfers between devices  64.3 us (34%)
  starting transfers between devices  47.5 us (25%)
  local copies, waits for them, and re-layouts  5.46 us (3%)
  other arithmetic  5.11 us (3%)
    pallas_call x4, Pallas kernels, expert_rows(): pl.pallas_call(functools.partial(expert_kernel, experts), out_shape=[jax....  55.8 us
    ppermute x2, waiting for transfers between devices, on_device(): returned = lax.ppermute(theirs, 'seq', across)  16.8 us
    ppermute x3, waiting for transfers between devices, on_device(): back = lax.ppermute(both, 'seq', line_pairs(moves))  14.5 us
    ppermute x2, waiting for transfers between devices, next_blocks(): lax.ppermute(below, 'seq', line_pairs(up))  14.1 us
    ppermute x4, starting transfers between devices, on_device(): backs.append((side, lax.ppermute(part, 'seq', line_pairs(moves))))  12.1 us
    ppermute x2, waiting for transfers between devices, next_blocks(): lax.ppermute(above, 'seq', line_pairs(down))  10.9 us
    ppermute x6, starting transfers between devices, summed(): lax.ppermute(block, axis, [(i, i ^ step * m) for i in range(shards)])  10.8 us
    pallas_call x1, Pallas kernels, attended_rows(): pl.pallas_call(functools.partial(attention_kernel, experts), out_shape=(j...  9.47 us
  transfers between devices with their start and end apart: 28, of which 10 were waited for; matrix products, arithmetic and copies ran while one was open for 2% of the time, Pallas kernels for 34%

profile of v4, /device:TPU:0, one launch (start us, length us, event | category | flops | bytes accessed | tf_op | source)
XLA Modules:
  0.0 189.7 jit_solution(9388816798746019898)
XLA Ops:
  0.0 1.7 shard_map.109
  1.7 2.4 %collective-permute-start.2 = (bf16[16,512]{1,0:T(8,128)(2,1)}, bf16[16,512]{1,0:T(8,128)(2,1)S(1)}, u32[]{:S(2)}, u32[]{:S(2)}) collective-permute-start(bf16[16,512]{1,0:T(8,128)(2,1)} %get-tuple-element.42), channel_id=1, source_target_pairs={{0,3},{1,2},{2,1},{3,0},{4,7},{5,6},{6,5},{7,4},{8,11},{9,10},{10,... | collective-permute-start | bytes 49160 | tf_op jit(solution)/shard_map/ppermute | solution.py:77
  4.1 0.6 collective-permute-start.1
  4.8 2.3 %collective-permute-start.3 = (bf16[128,512]{1,0:T(8,128)(2,1)}, bf16[128,512]{1,0:T(8,128)(2,1)S(1)}, u32[]{:S(2)}, u32[]{:S(2)}) collective-permute-start(bf16[128,512]{1,0:T(8,128)(2,1)} %get-tuple-element.43.local), channel_id=1, source_target_pairs={{0,1},{1,2},{2,3},{3,4},{4,5},{5,6},{6,7},{7,8},{8,9},{9,10},{10,1... | collective-permute-start | bytes 393224 | tf_op jit(solution)/shard_map/ppermute | solution.py:400
  7.2 0.9 collective-permute-done.1
  8.1 0.7 add_add_fusion.1
  8.8 7.2 %collective-permute-start.6 = (bf16[16,512]{1,0:T(8,128)(2,1)S(1)}, bf16[16,512]{1,0:T(8,128)(2,1)S(1)}, u32[]{:S(2)}, u32[]{:S(2)}) collective-permute-start(bf16[16,512]{1,0:T(8,128)(2,1)S(1)} %add_add_fusion.1), channel_id=1, source_target_pairs={{0,12},{1,13},{2,14},{3,15},{4,8},{5,9},{6,10},{7,11},{8,4},{9,5},... | collective-permute-start | bytes 49160 | tf_op jit(solution)/shard_map/ppermute | solution.py:77
  16.0 0.6 collective-permute-start.4
  16.6 2.0 %copy.12 = bf16[128,2048]{0,1:T(8,128)(2,1)} copy(bf16[128,2048]{1,0:T(8,128)(2,1)} %param.11) | data formatting | bytes 1048576 | tf_op jit(solution)/shard_map/optimization_barrier | solution.py:83
  18.6 2.0 %collective-permute-done.5 = bf16[16,512]{1,0:T(8,128)(2,1)S(1)} collective-permute-done((bf16[16,512]{1,0:T(8,128)(2,1)S(1)}, bf16[16,512]{1,0:T(8,128)(2,1)S(1)}, u32[]{:S(2)}, u32[]{:S(2)}) %collective-permute-start.5) | collective-permute-done | bytes 16416 | tf_op jit(solution)/shard_map/ppermute | solution.py:77
  20.7 0.6 add_add_fusion.sinks
  21.3 2.2 %broadcast_in_dim.2.gain = f32[2880,128]{1,0:T(8,128)} broadcast(f32[2880]{0:T(1024)} %param.17), dimensions={0} | broadcast | bytes 1486080 | tf_op jit(solution)/shard_map/broadcast_in_dim | solution.py:403
  23.5 0.5 collective-permute-start.9
  24.0 9.5 %shard_map.110 = (bf16[2880,128]{1,0:T(8,128)(2,1)}, bf16[2896,128]{1,0:T(8,128)(2,1)}) custom-call(bf16[2048,128]{1,0:T(8,128)(2,1)} %bitcast.24, bf16[128,512]{1,0:T(8,128)(2,1)} %copy-done.11, bf16[128,512]{1,0:T(8,128)(2,1)} %get-tuple-element.43.local, bf16[16,512]{1,0:T(8,128)(2,1)} %add_add_fusion.sinks, f32[272,128]{1,0:T(8,128)} %get-tuple-element.49.bias, ...), custom_call_target="tpu_custom_call" | custom-call | flops 1509949440 | bytes 11796480 | tf_op jit(solution)/shard_map/pallas_call | solution.py:209
  33.5 1.6 collective-permute-start.10
  35.1 1.3 collective-permute-start.11
  36.4 0.9 collective-permute-start.7
  37.3 14.1 %collective-permute-done.10 = bf16[2896,128]{1,0:T(8,128)(2,1)S(1)} collective-permute-done((bf16[2896,128]{1,0:T(8,128)(2,1)}, bf16[2896,128]{1,0:T(8,128)(2,1)S(1)}, u32[]{:S(2)}, u32[]{:S(2)}) %collective-permute-start.10) | collective-permute-done | bytes 741408 | tf_op jit(solution)/shard_map/ppermute | solution.py:359
  51.4 5.2 %collective-permute-done.11 = bf16[2896,128]{1,0:T(8,128)(2,1)S(1)} collective-permute-done((bf16[2896,128]{1,0:T(8,128)(2,1)}, bf16[2896,128]{1,0:T(8,128)(2,1)S(1)}, u32[]{:S(2)}, u32[]{:S(2)}) %collective-permute-start.11) | collective-permute-done | bytes 741408 | tf_op jit(solution)/shard_map/ppermute | solution.py:360
  56.7 0.7 collective-permute-start.12
  57.4 1.5 collective-permute-start.13
  58.9 1.3 collective-permute-start.14
  60.3 14.2 %shard_map.111 = (f32[2880,128]{1,0:T(8,128)}, f32[2880,128]{1,0:T(8,128)}) custom-call(s32[1]{0:T(128)} %bitcast.6.me_ref, bf16[2896,128]{1,0:T(8,128)(2,1)} %get-tuple-element.52.x_ref, bf16[2896,128]{1,0:T(8,128)(2,1)} %copy-done.7, bf16[1440,2880]{1,0:T(8,128)(2,1)} %bitcast.14, bf16[1440,2880]{1,0:T(8,128)(2,1)} %collective-permute-done.8.gu1, ...), custom_call_target="tpu_custom_call" | custom-call | flops 6370099200 | bytes 24883200 | tf_op jit(solution)/shard_map/pallas_call | solution.py:300
  74.5 5.7 %collective-permute-done.14 = bf16[2896,128]{1,0:T(8,128)(2,1)} collective-permute-done((bf16[2896,128]{1,0:T(8,128)(2,1)S(1)}, bf16[2896,128]{1,0:T(8,128)(2,1)}, u32[]{:S(2)}, u32[]{:S(2)}) %collective-permute-start.14) | collective-permute-done | bytes 741408 | tf_op jit(solution)/shard_map/ppermute | solution.py:360
  80.2 1.4 select_select_fusion
  81.7 1.5 collective-permute-start.15
  83.1 1.5 collective-permute-start.16
  84.6 13.7 %shard_map.112 = (bf16[2880,128]{1,0:T(8,128)(2,1)}, bf16[2880,128]{1,0:T(8,128)(2,1)}) custom-call(s32[1]{0:T(128)} %bitcast.6.me_ref, bf16[2896,128]{1,0:T(8,128)(2,1)} %copy-done, bf16[2896,128]{1,0:T(8,128)(2,1)} %collective-permute-done.12.y_ref, bf16[1440,2880]{1,0:T(8,128)(2,1)} %bitcast.15, bf16[1440,2880]{1,0:T(8,128)(2,1)} %collective-permute-done.8.gu1, ...), custom_call_target="tpu_custom_call" | custom-call | flops 6370099200 | bytes 24883200 | tf_op jit(solution)/shard_map/pallas_call | solution.py:300
  98.3 2.2 %collective-permute-done.16 = bf16[2896,128]{1,0:T(8,128)(2,1)S(1)} collective-permute-done((bf16[2896,128]{1,0:T(8,128)(2,1)S(1)}, bf16[2896,128]{1,0:T(8,128)(2,1)S(1)}, u32[]{:S(2)}, u32[]{:S(2)}) %collective-permute-start.16) | collective-permute-done | bytes 741408 | tf_op jit(solution)/shard_map/ppermute | solution.py:356
  100.6 0.7 collective-permute-start.19
  101.3 2.5 %collective-permute-start.17 = (bf16[2880,128]{1,0:T(8,128)(2,1)}, bf16[2880,128]{1,0:T(8,128)(2,1)S(1)}, u32[]{:S(2)}, u32[]{:S(2)}) collective-permute-start(bf16[2880,128]{1,0:T(8,128)(2,1)} %get-tuple-element.64), channel_id=1, source_target_pairs={{0,4},{1,5},{2,6},{3,7},{4,8},{5,9},{6,10},{7,11},{16,20},{17,21},... | collective-permute-start | bytes 2211848 | tf_op jit(solution)/shard_map/ppermute | solution.py:466
  103.8 0.7 collective-permute-start.18
  104.5 0.7 collective-permute-start.23
  105.2 13.9 %shard_map.113 = (f32[2880,128]{1,0:T(8,128)}, bf16[2880,128]{1,0:T(8,128)(2,1)}) custom-call(s32[1]{0:T(128)} %bitcast.6.me_ref, bf16[2896,128]{1,0:T(8,128)(2,1)} %copy-done.2, bf16[2896,128]{1,0:T(8,128)(2,1)} %copy-done.8, bf16[1440,2880]{1,0:T(8,128)(2,1)} %bitcast.16, bf16[1440,2880]{1,0:T(8,128)(2,1)} %collective-permute-done.8.gu1, ...), custom_call_target="tpu_custom_call" | custom-call | flops 6370099200 | bytes 24883200 | tf_op jit(solution)/shard_map/pallas_call | solution.py:300
  119.2 1.5 collective-permute-start.20
  120.7 8.2 %collective-permute-start.22 = (bf16[2880,128]{1,0:T(8,128)(2,1)}, bf16[2880,128]{1,0:T(8,128)(2,1)S(1)}, u32[]{:S(2)}, u32[]{:S(2)}) collective-permute-start(bf16[2880,128]{1,0:T(8,128)(2,1)} %get-tuple-element.73), channel_id=1, source_target_pairs={{0,4},{1,5},{2,6},{3,7},{4,8},{5,9},{6,10},{7,11},{16,20},{17,21},... | collective-permute-start | bytes 2211848 | tf_op jit(solution)/shard_map/ppermute | solution.py:466
  128.9 14.0 %shard_map.114 = (f32[2880,128]{1,0:T(8,128)}, bf16[2880,128]{1,0:T(8,128)(2,1)}) custom-call(s32[1]{0:T(128)} %bitcast.6.me_ref, bf16[2896,128]{1,0:T(8,128)(2,1)} %copy-done.1, bf16[2896,128]{1,0:T(8,128)(2,1)} %copy-done.9, bf16[1440,2880]{1,0:T(8,128)(2,1)} %bitcast.17, bf16[1440,2880]{1,0:T(8,128)(2,1)} %collective-permute-done.8.gu1, ...), custom_call_target="tpu_custom_call" | custom-call | flops 6370099200 | bytes 24883200 | tf_op jit(solution)/shard_map/pallas_call | solution.py:300
  142.9 0.8 collective-permute-start.24
  144.0 1.1 copy-done.4
  145.1 0.2 add_convert_fusion.1
  145.4 16.8 %collective-permute-done.24 = bf16[2880,128]{1,0:T(8,128)(2,1)S(1)} collective-permute-done((bf16[2880,128]{1,0:T(8,128)(2,1)}, bf16[2880,128]{1,0:T(8,128)(2,1)S(1)}, u32[]{:S(2)}, u32[]{:S(2)}) %collective-permute-start.24) | collective-permute-done | bytes 737312 | tf_op jit(solution)/shard_map/ppermute | solution.py:485
  162.2 0.8 collective-permute-start.27
  163.1 1.3 collective-permute-start.26
  164.4 6.3 %collective-permute-start.25 = (bf16[2880,128]{1,0:T(8,128)(2,1)S(1)}, bf16[2880,128]{1,0:T(8,128)(2,1)S(1)}, u32[]{:S(2)}, u32[]{:S(2)}) collective-permute-start(bf16[2880,128]{1,0:T(8,128)(2,1)S(1)} %add_convert_fusion.2), channel_id=1, source_target_pairs={{0,12},{1,13},{2,14},{3,15},{8,0},{9,1},{10,2},{11,3},{16,28},{17,... | collective-permute-start | bytes 2211848 | tf_op jit(solution)/shard_map/ppermute | solution.py:500
  170.8 2.9 %collective-permute-done.27 = bf16[2880,128]{1,0:T(8,128)(2,1)S(1)} collective-permute-done((bf16[2880,128]{1,0:T(8,128)(2,1)S(1)}, bf16[2880,128]{1,0:T(8,128)(2,1)S(1)}, u32[]{:S(2)}, u32[]{:S(2)}) %collective-permute-start.27) | collective-permute-done | bytes 737312 | tf_op jit(solution)/shard_map/ppermute | solution.py:497
  173.6 4.7 %collective-permute-done.26 = bf16[2880,128]{1,0:T(8,128)(2,1)S(1)} collective-permute-done((bf16[2880,128]{1,0:T(8,128)(2,1)S(1)}, bf16[2880,128]{1,0:T(8,128)(2,1)S(1)}, u32[]{:S(2)}, u32[]{:S(2)}) %collective-permute-start.26) | collective-permute-done | bytes 737312 | tf_op jit(solution)/shard_map/ppermute | solution.py:500
  178.4 9.8 %collective-permute-done.25 = bf16[2880,128]{1,0:T(8,128)(2,1)S(1)} collective-permute-done((bf16[2880,128]{1,0:T(8,128)(2,1)S(1)}, bf16[2880,128]{1,0:T(8,128)(2,1)S(1)}, u32[]{:S(2)}, u32[]{:S(2)}) %collective-permute-start.25) | collective-permute-done | bytes 737312 | tf_op jit(solution)/shard_map/ppermute | solution.py:500
  188.1 1.6 fusion
  (49 shorter events, 0.8 us)
Async XLA Ops:
  1.7 5.4 %collective-permute-start.2 = (bf16[16,512]{1,0:T(8,128)(2,1)}, bf16[16,512]{1,0:T(8,128)(2,1)S(1)}, u32[]{:S(2)}, u32[]{:S(2)}) collective-permute-start(bf16[16,512]{1,0:T(8,128)(2,1)} %get-tuple-element.42), channel_id=1, source_target_pairs={{0,3},{1,2},{2,1},{3,0},{4,7},{5,6},{6,5},{7,4},{8,11},{9,10},{10,... | collective-permute-start | bytes 49160 | tf_op jit(solution)/shard_map/ppermute | solution.py:77
  4.1 3.9 %collective-permute-start.1 = (bf16[16,512]{1,0:T(8,128)(2,1)}, bf16[16,512]{1,0:T(8,128)(2,1)S(1)}, u32[]{:S(2)}, u32[]{:S(2)}) collective-permute-start(bf16[16,512]{1,0:T(8,128)(2,1)} %get-tuple-element.42), channel_id=1, source_target_pairs={{0,2},{1,3},{2,0},{3,1},{4,6},{5,7},{6,4},{7,5},{8,10},{9,11},{10,... | collective-permute-start | bytes 49160 | tf_op jit(solution)/shard_map/ppermute | solution.py:77
  4.7 3.4 %collective-permute-start = (bf16[16,512]{1,0:T(8,128)(2,1)}, bf16[16,512]{1,0:T(8,128)(2,1)S(1)}, u32[]{:S(2)}, u32[]{:S(2)}) collective-permute-start(bf16[16,512]{1,0:T(8,128)(2,1)} %get-tuple-element.42), channel_id=1, source_target_pairs={{0,1},{1,0},{2,3},{3,2},{4,5},{5,4},{6,7},{7,6},{8,9},{9,8},{10,11... | collective-permute-start | bytes 49160 | tf_op jit(solution)/shard_map/ppermute | solution.py:77
  4.8 4.0 %collective-permute-start.3 = (bf16[128,512]{1,0:T(8,128)(2,1)}, bf16[128,512]{1,0:T(8,128)(2,1)S(1)}, u32[]{:S(2)}, u32[]{:S(2)}) collective-permute-start(bf16[128,512]{1,0:T(8,128)(2,1)} %get-tuple-element.43.local), channel_id=1, source_target_pairs={{0,1},{1,2},{2,3},{3,4},{4,5},{5,6},{6,7},{7,8},{8,9},{9,10},{10,1... | collective-permute-start | bytes 393224 | tf_op jit(solution)/shard_map/ppermute | solution.py:400
  8.8 15.2 %copy-start.11 = (bf16[128,512]{1,0:T(8,128)(2,1)}, bf16[128,512]{1,0:T(8,128)(2,1)S(1)}, u32[]{:S(2)}) copy-start(bf16[128,512]{1,0:T(8,128)(2,1)S(1)} %collective-permute-done.3.halo) | copy-start | bytes 393220
  8.8 9.8 %collective-permute-start.6 = (bf16[16,512]{1,0:T(8,128)(2,1)S(1)}, bf16[16,512]{1,0:T(8,128)(2,1)S(1)}, u32[]{:S(2)}, u32[]{:S(2)}) collective-permute-start(bf16[16,512]{1,0:T(8,128)(2,1)S(1)} %add_add_fusion.1), channel_id=1, source_target_pairs={{0,12},{1,13},{2,14},{3,15},{4,8},{5,9},{6,10},{7,11},{8,4},{9,5},... | collective-permute-start | bytes 49160 | tf_op jit(solution)/shard_map/ppermute | solution.py:77
  16.0 4.6 %collective-permute-start.5 = (bf16[16,512]{1,0:T(8,128)(2,1)S(1)}, bf16[16,512]{1,0:T(8,128)(2,1)S(1)}, u32[]{:S(2)}, u32[]{:S(2)}) collective-permute-start(bf16[16,512]{1,0:T(8,128)(2,1)S(1)} %add_add_fusion.1), channel_id=1, source_target_pairs={{0,8},{1,9},{2,10},{3,11},{4,12},{5,13},{6,14},{7,15},{8,0},{9,1},... | collective-permute-start | bytes 49160 | tf_op jit(solution)/shard_map/ppermute | solution.py:77
  16.0 4.6 %collective-permute-start.4 = (bf16[16,512]{1,0:T(8,128)(2,1)S(1)}, bf16[16,512]{1,0:T(8,128)(2,1)S(1)}, u32[]{:S(2)}, u32[]{:S(2)}) collective-permute-start(bf16[16,512]{1,0:T(8,128)(2,1)S(1)} %add_add_fusion.1), channel_id=1, source_target_pairs={{0,4},{1,5},{2,6},{3,7},{4,0},{5,1},{6,2},{7,3},{8,12},{9,13},{10,... | collective-permute-start | bytes 49160 | tf_op jit(solution)/shard_map/ppermute | solution.py:77
  23.5 36.7 %collective-permute-start.8 = (bf16[1440,2880]{1,0:T(8,128)(2,1)}, bf16[1440,2880]{1,0:T(8,128)(2,1)}, u32[]{:S(2)}, u32[]{:S(2)}) collective-permute-start(bf16[1440,2880]{1,0:T(8,128)(2,1)} %bitcast.13), channel_id=1, source_target_pairs={{0,1},{1,0},{2,3},{3,2},{4,5},{5,4},{6,7},{7,6},{8,9},{9,8},{10,11... | collective-permute-start | bytes 24883208 | tf_op jit(solution)/shard_map/ppermute | solution.py:411
  23.5 36.7 %collective-permute-start.9 = (bf16[720,2880]{1,0:T(8,128)(2,1)}, bf16[720,2880]{1,0:T(8,128)(2,1)}, u32[]{:S(2)}, u32[]{:S(2)}) collective-permute-start(bf16[720,2880]{1,0:T(8,128)(2,1)} %bitcast.18), channel_id=1, source_target_pairs={{0,1},{1,0},{2,3},{3,2},{4,5},{5,4},{6,7},{7,6},{8,9},{9,8},{10,11... | collective-permute-start | bytes 12441608 | tf_op jit(solution)/shard_map/ppermute | solution.py:412
  33.5 17.9 %collective-permute-start.10 = (bf16[2896,128]{1,0:T(8,128)(2,1)}, bf16[2896,128]{1,0:T(8,128)(2,1)S(1)}, u32[]{:S(2)}, u32[]{:S(2)}) collective-permute-start(bf16[2896,128]{1,0:T(8,128)(2,1)} %get-tuple-element.52.x_ref), channel_id=1, source_target_pairs={{0,4},{1,5},{2,6},{3,7},{4,8},{5,9},{6,10},{7,11},{8,12},{9,13},{1... | collective-permute-start | bytes 2224136 | tf_op jit(solution)/shard_map/ppermute | solution.py:359
  35.1 21.4 %collective-permute-start.11 = (bf16[2896,128]{1,0:T(8,128)(2,1)}, bf16[2896,128]{1,0:T(8,128)(2,1)S(1)}, u32[]{:S(2)}, u32[]{:S(2)}) collective-permute-start(bf16[2896,128]{1,0:T(8,128)(2,1)} %get-tuple-element.52.x_ref), channel_id=1, source_target_pairs={{4,0},{5,1},{6,2},{7,3},{8,4},{9,5},{10,6},{11,7},{12,8},{13,9},{1... | collective-permute-start | bytes 2224136 | tf_op jit(solution)/shard_map/ppermute | solution.py:360
  36.4 20.3 %collective-permute-start.7 = (bf16[2896,128]{1,0:T(8,128)(2,1)}, bf16[2896,128]{1,0:T(8,128)(2,1)S(1)}, u32[]{:S(2)}, u32[]{:S(2)}) collective-permute-start(bf16[2896,128]{1,0:T(8,128)(2,1)} %get-tuple-element.52.x_ref), channel_id=1, source_target_pairs={{0,2},{1,3},{2,0},{3,1},{4,6},{5,7},{6,4},{7,5},{8,10},{9,11},{10,... | collective-permute-start | bytes 2224136 | tf_op jit(solution)/shard_map/ppermute | solution.py:437
  56.7 17.8 %copy-start = (bf16[2896,128]{1,0:T(8,128)(2,1)}, bf16[2896,128]{1,0:T(8,128)(2,1)S(1)}, u32[]{:S(2)}) copy-start(bf16[2896,128]{1,0:T(8,128)(2,1)S(1)} %broadcast_select_fusion.2.x_ref) | copy-start | bytes 2224132
  56.7 3.6 %copy-start.7 = (bf16[2896,128]{1,0:T(8,128)(2,1)}, bf16[2896,128]{1,0:T(8,128)(2,1)S(1)}, u32[]{:S(2)}) copy-start(bf16[2896,128]{1,0:T(8,128)(2,1)S(1)} %collective-permute-done.7.y_ref) | copy-start | bytes 2224132
  56.7 17.8 %collective-permute-start.12 = (bf16[2896,128]{1,0:T(8,128)(2,1)S(1)}, bf16[2896,128]{1,0:T(8,128)(2,1)}, u32[]{:S(2)}, u32[]{:S(2)}) collective-permute-start(bf16[2896,128]{1,0:T(8,128)(2,1)S(1)} %broadcast_select_fusion.2.x_ref), channel_id=1, source_target_pairs={{0,2},{1,3},{2,0},{3,1},{4,6},{5,7},{6,4},{7,5},{8,10},{9,11},{10,... | collective-permute-start | bytes 2224136 | tf_op jit(solution)/shard_map/ppermute | solution.py:443
  57.4 17.1 %collective-permute-start.13 = (bf16[2896,128]{1,0:T(8,128)(2,1)S(1)}, bf16[2896,128]{1,0:T(8,128)(2,1)}, u32[]{:S(2)}, u32[]{:S(2)}) collective-permute-start(bf16[2896,128]{1,0:T(8,128)(2,1)S(1)} %collective-permute-done.10), channel_id=1, source_target_pairs={{4,8},{5,9},{6,10},{7,11},{8,12},{9,13},{10,14},{11,15},{20,24},{2... | collective-permute-start | bytes 2224136 | tf_op jit(solution)/shard_map/ppermute | solution.py:359
  58.9 21.3 %collective-permute-start.14 = (bf16[2896,128]{1,0:T(8,128)(2,1)S(1)}, bf16[2896,128]{1,0:T(8,128)(2,1)}, u32[]{:S(2)}, u32[]{:S(2)}) collective-permute-start(bf16[2896,128]{1,0:T(8,128)(2,1)S(1)} %collective-permute-done.11), channel_id=1, source_target_pairs={{4,0},{5,1},{6,2},{7,3},{8,4},{9,5},{10,6},{11,7},{20,16},{21,17},... | collective-permute-start | bytes 2224136 | tf_op jit(solution)/shard_map/ppermute | solution.py:360
  81.7 16.7 %copy-start.2 = (bf16[2896,128]{1,0:T(8,128)(2,1)}, bf16[2896,128]{1,0:T(8,128)(2,1)S(1)}, u32[]{:S(2)}) copy-start(bf16[2896,128]{1,0:T(8,128)(2,1)S(1)} %get-tuple-element.62.x_ref) | copy-start | bytes 2224132
  81.7 16.7 %collective-permute-start.15 = (bf16[2896,128]{1,0:T(8,128)(2,1)S(1)}, bf16[2896,128]{1,0:T(8,128)(2,1)S(1)}, u32[]{:S(2)}, u32[]{:S(2)}) collective-permute-start(bf16[2896,128]{1,0:T(8,128)(2,1)S(1)} %get-tuple-element.62.x_ref), channel_id=1, source_target_pairs={{0,2},{1,3},{2,0},{3,1},{4,6},{5,7},{6,4},{7,5},{8,10},{9,11},{10,... | collective-permute-start | bytes 2224136 | tf_op jit(solution)/shard_map/ppermute | solution.py:443
  83.1 17.4 %collective-permute-start.16 = (bf16[2896,128]{1,0:T(8,128)(2,1)S(1)}, bf16[2896,128]{1,0:T(8,128)(2,1)S(1)}, u32[]{:S(2)}, u32[]{:S(2)}) collective-permute-start(bf16[2896,128]{1,0:T(8,128)(2,1)S(1)} %get-tuple-element.63), channel_id=1, source_target_pairs={{8,12},{9,13},{10,14},{11,15},{4,0},{5,1},{6,2},{7,3},{24,28},{25,... | collective-permute-start | bytes 2224136 | tf_op jit(solution)/shard_map/ppermute | solution.py:356
  98.3 6.9 %copy-start.8 = (bf16[2896,128]{1,0:T(8,128)(2,1)}, bf16[2896,128]{1,0:T(8,128)(2,1)S(1)}, u32[]{:S(2)}) copy-start(bf16[2896,128]{1,0:T(8,128)(2,1)S(1)} %collective-permute-done.15.y_ref) | copy-start | bytes 2224132
  100.6 18.6 %copy-start.1 = (bf16[2896,128]{1,0:T(8,128)(2,1)}, bf16[2896,128]{1,0:T(8,128)(2,1)S(1)}, u32[]{:S(2)}) copy-start(bf16[2896,128]{1,0:T(8,128)(2,1)S(1)} %broadcast_select_fusion.x_ref) | copy-start | bytes 2224132
  100.6 18.6 %collective-permute-start.19 = (bf16[2896,128]{1,0:T(8,128)(2,1)S(1)}, bf16[2896,128]{1,0:T(8,128)(2,1)S(1)}, u32[]{:S(2)}, u32[]{:S(2)}) collective-permute-start(bf16[2896,128]{1,0:T(8,128)(2,1)S(1)} %broadcast_select_fusion.x_ref), channel_id=1, source_target_pairs={{0,2},{1,3},{2,0},{3,1},{4,6},{5,7},{6,4},{7,5},{8,10},{9,11},{10,... | collective-permute-start | bytes 2224136 | tf_op jit(solution)/shard_map/ppermute | solution.py:443
  101.3 17.9 %collective-permute-start.17 = (bf16[2880,128]{1,0:T(8,128)(2,1)}, bf16[2880,128]{1,0:T(8,128)(2,1)S(1)}, u32[]{:S(2)}, u32[]{:S(2)}) collective-permute-start(bf16[2880,128]{1,0:T(8,128)(2,1)} %get-tuple-element.64), channel_id=1, source_target_pairs={{0,4},{1,5},{2,6},{3,7},{4,8},{5,9},{6,10},{7,11},{16,20},{17,21},... | collective-permute-start | bytes 2211848 | tf_op jit(solution)/shard_map/ppermute | solution.py:466
  103.8 15.4 %collective-permute-start.18 = (bf16[2880,128]{1,0:T(8,128)(2,1)}, bf16[2880,128]{1,0:T(8,128)(2,1)S(1)}, u32[]{:S(2)}, u32[]{:S(2)}) collective-permute-start(bf16[2880,128]{1,0:T(8,128)(2,1)} %get-tuple-element.64), channel_id=1, source_target_pairs={{8,4},{9,5},{10,6},{11,7},{12,8},{13,9},{14,10},{15,11},{24,20},{2... | collective-permute-start | bytes 2211848 | tf_op jit(solution)/shard_map/ppermute | solution.py:466
  104.5 38.4 %collective-permute-start.23 = (bf16[2880,128]{1,0:T(8,128)(2,1)}, bf16[2880,128]{1,0:T(8,128)(2,1)S(1)}, u32[]{:S(2)}, u32[]{:S(2)}) collective-permute-start(bf16[2880,128]{1,0:T(8,128)(2,1)} %get-tuple-element.73), channel_id=1, source_target_pairs={{8,4},{9,5},{10,6},{11,7},{12,8},{13,9},{14,10},{15,11},{24,20},{2... | collective-permute-start | bytes 2211848 | tf_op jit(solution)/shard_map/ppermute | solution.py:466
  119.2 9.7 %copy-start.9 = (bf16[2896,128]{1,0:T(8,128)(2,1)}, bf16[2896,128]{1,0:T(8,128)(2,1)S(1)}, u32[]{:S(2)}) copy-start(bf16[2896,128]{1,0:T(8,128)(2,1)S(1)} %collective-permute-done.19.y_ref) | copy-start | bytes 2224132
  119.2 24.5 %copy-start.5 = (f32[2880,128]{1,0:T(8,128)S(1)}, f32[2880,128]{1,0:T(8,128)}, u32[]{:S(2)}) copy-start(f32[2880,128]{1,0:T(8,128)} %get-tuple-element.65) | copy-start | bytes 4423684
  119.2 23.7 %collective-permute-start.20 = (bf16[2880,128]{1,0:T(8,128)(2,1)}, bf16[2880,128]{1,0:T(8,128)(2,1)S(1)}, u32[]{:S(2)}, u32[]{:S(2)}) collective-permute-start(bf16[2880,128]{1,0:T(8,128)(2,1)} %get-tuple-element.69), channel_id=1, source_target_pairs={{0,2},{1,3},{2,0},{3,1},{4,6},{5,7},{6,4},{7,5},{8,10},{9,11},{10,... | collective-permute-start | bytes 2211848 | tf_op jit(solution)/shard_map/ppermute | solution.py:485
  120.7 22.2 %collective-permute-start.22 = (bf16[2880,128]{1,0:T(8,128)(2,1)}, bf16[2880,128]{1,0:T(8,128)(2,1)S(1)}, u32[]{:S(2)}, u32[]{:S(2)}) collective-permute-start(bf16[2880,128]{1,0:T(8,128)(2,1)} %get-tuple-element.73), channel_id=1, source_target_pairs={{0,4},{1,5},{2,6},{3,7},{4,8},{5,9},{6,10},{7,11},{16,20},{17,21},... | collective-permute-start | bytes 2211848 | tf_op jit(solution)/shard_map/ppermute | solution.py:466
  142.9 19.3 %collective-permute-start.24 = (bf16[2880,128]{1,0:T(8,128)(2,1)}, bf16[2880,128]{1,0:T(8,128)(2,1)S(1)}, u32[]{:S(2)}, u32[]{:S(2)}) collective-permute-start(bf16[2880,128]{1,0:T(8,128)(2,1)} %get-tuple-element.76), channel_id=1, source_target_pairs={{0,2},{1,3},{2,0},{3,1},{4,6},{5,7},{6,4},{7,5},{8,10},{9,11},{10,... | collective-permute-start | bytes 2211848 | tf_op jit(solution)/shard_map/ppermute | solution.py:485
  143.8 1.4 copy-start.4
  143.9 26.8 %collective-permute-start.21 = (bf16[2880,128]{1,0:T(8,128)(2,1)S(1)}, bf16[2880,128]{1,0:T(8,128)(2,1)S(1)}, u32[]{:S(2)}, u32[]{:S(2)}) collective-permute-start(bf16[2880,128]{1,0:T(8,128)(2,1)S(1)} %add_convert_fusion.3), channel_id=1, source_target_pairs={{0,8},{1,9},{2,10},{3,11},{4,0},{5,1},{6,2},{7,3},{8,12},{9,13},{1... | collective-permute-start | bytes 2211848 | tf_op jit(solution)/shard_map/ppermute | solution.py:493
  145.1 17.8 %copy-start.6 = (f32[2880,128]{1,0:T(8,128)S(1)}, f32[2880,128]{1,0:T(8,128)}, u32[]{:S(2)}) copy-start(f32[2880,128]{1,0:T(8,128)} %get-tuple-element.70) | copy-start | bytes 4423684
  145.4 42.7 %copy-start.3 = (f32[2880,128]{1,0:T(8,128)S(1)}, f32[2880,128]{1,0:T(8,128)}, u32[]{:S(2)}) copy-start(f32[2880,128]{1,0:T(8,128)} %get-tuple-element.55) | copy-start | bytes 4423684
  145.4 42.7 %copy-start.10 = (bf16[2880,128]{1,0:T(8,128)(2,1)S(1)}, bf16[2880,128]{1,0:T(8,128)(2,1)}, u32[]{:S(2)}) copy-start(bf16[2880,128]{1,0:T(8,128)(2,1)} %get-tuple-element.51) | copy-start | bytes 2211844
  162.2 11.5 %collective-permute-start.27 = (bf16[2880,128]{1,0:T(8,128)(2,1)S(1)}, bf16[2880,128]{1,0:T(8,128)(2,1)S(1)}, u32[]{:S(2)}, u32[]{:S(2)}) collective-permute-start(bf16[2880,128]{1,0:T(8,128)(2,1)S(1)} %add_convert_fusion.1), channel_id=1, source_target_pairs={{0,2},{1,3},{2,0},{3,1},{4,6},{5,7},{6,4},{7,5},{8,10},{9,11},{10,... | collective-permute-start | bytes 2211848 | tf_op jit(solution)/shard_map/ppermute | solution.py:497
  163.1 15.3 %collective-permute-start.26 = (bf16[2880,128]{1,0:T(8,128)(2,1)S(1)}, bf16[2880,128]{1,0:T(8,128)(2,1)S(1)}, u32[]{:S(2)}, u32[]{:S(2)}) collective-permute-start(bf16[2880,128]{1,0:T(8,128)(2,1)S(1)} %add_convert_fusion.2), channel_id=1, source_target_pairs={{4,12},{5,13},{6,14},{7,15},{12,0},{13,1},{14,2},{15,3},{20,28},{2... | collective-permute-start | bytes 2211848 | tf_op jit(solution)/shard_map/ppermute | solution.py:500
  164.4 23.7 %collective-permute-start.25 = (bf16[2880,128]{1,0:T(8,128)(2,1)S(1)}, bf16[2880,128]{1,0:T(8,128)(2,1)S(1)}, u32[]{:S(2)}, u32[]{:S(2)}) collective-permute-start(bf16[2880,128]{1,0:T(8,128)(2,1)S(1)} %add_convert_fusion.2), channel_id=1, source_target_pairs={{0,12},{1,13},{2,14},{3,15},{8,0},{9,1},{10,2},{11,3},{16,28},{17,... | collective-permute-start | bytes 2211848 | tf_op jit(solution)/shard_map/ppermute | solution.py:500

commit v5 on v3

--- a/solution.py
+++ b/solution.py
@@ -481,7 +481,7 @@
         theirs = after(theirs, *ready)
         returned = lax.ppermute(theirs, "seq", across)
         if n == 0:
-            slow = [after(back, returned, parts[0]) for back in slow]
+            slow = [after(back, parts[0]) for back in slow]
             for back in slow:
                 cross_sum = cross_sum + back.astype(jnp.float32)
         if pending is not None:

time: 187 us -> 201 us (1.075)
  waiting for transfers between devices: 60 us -> 73.1 us
    ppermute x2, waiting for transfers between devices: 17 us -> 27.3 us  [on_device(): returned = lax.ppermute(theirs, 'seq', across)]
    ppermute x4, starting transfers between devices: 12.9 us -> 9.6 us  [on_device(): backs.append((side, lax.ppermute(part, 'seq', line_pairs(moves))))]
    ppermute x3, waiting for transfers between devices: 14 us -> 17.2 us  [on_device(): back = lax.ppermute(both, 'seq', line_pairs(moves))]
    ppermute x3, starting transfers between devices: 7.7 us -> 10.3 us  [on_device(): back = lax.ppermute(both, 'seq', line_pairs(moves))]
  transfers between devices with their start and end apart: 28 -> 28, of which waited for: 10 -> 11; matrix products, arithmetic and copies ran while one was open for 3% -> 3% of each run, Pallas kernels for 35% -> 33%
where the time goes in v5:
time: 201 us; the launch traced here: 200 us
  waiting for transfers between devices  73.1 us (36%)
  Pallas kernels  67.4 us (34%)
  starting transfers between devices  49.6 us (25%)
  other arithmetic  5.18 us (3%)
  local copies, waits for them, and re-layouts  4.22 us (2%)
    pallas_call x4, Pallas kernels, expert_rows(): pl.pallas_call(functools.partial(expert_kernel, experts), out_shape=[jax....  55.9 us
    ppermute x2, waiting for transfers between devices, on_device(): returned = lax.ppermute(theirs, 'seq', across)  27.3 us
    ppermute x3, waiting for transfers between devices, on_device(): back = lax.ppermute(both, 'seq', line_pairs(moves))  17.2 us
    ppermute x2, waiting for transfers between devices, next_blocks(): lax.ppermute(below, 'seq', line_pairs(up))  13.7 us
    ppermute x3, starting transfers between devices, on_device(): back = lax.ppermute(both, 'seq', line_pairs(moves))  10.3 us
    pallas_call x1, Pallas kernels, attended_rows(): pl.pallas_call(functools.partial(attention_kernel, experts), out_shape=(j...  9.68 us
    ppermute x4, starting transfers between devices, on_device(): backs.append((side, lax.ppermute(part, 'seq', line_pairs(moves))))  9.6 us
    ppermute x6, starting transfers between devices, summed(): lax.ppermute(block, axis, [(i, i ^ step * m) for i in range(shards)])  9.36 us
  transfers between devices with their start and end apart: 28, of which 11 were waited for; matrix products, arithmetic and copies ran while one was open for 3% of the time, Pallas kernels for 33%

profile of v5, /device:TPU:0, one launch (start us, length us, event | category | flops | bytes accessed | tf_op | source)
XLA Modules:
  0.0 199.9 jit_solution(5860176759744345140)
XLA Ops:
  0.0 1.8 shard_map.109
  1.8 2.4 %collective-permute-start.2 = (bf16[16,512]{1,0:T(8,128)(2,1)}, bf16[16,512]{1,0:T(8,128)(2,1)S(1)}, u32[]{:S(2)}, u32[]{:S(2)}) collective-permute-start(bf16[16,512]{1,0:T(8,128)(2,1)} %get-tuple-element.39), channel_id=1, source_target_pairs={{0,3},{1,2},{2,1},{3,0},{4,7},{5,6},{6,5},{7,4},{8,11},{9,10},{10,... | collective-permute-start | bytes 49160 | tf_op jit(solution)/shard_map/ppermute | solution.py:77
  4.2 0.6 collective-permute-start.1
  4.9 2.3 %collective-permute-start.3 = (bf16[128,512]{1,0:T(8,128)(2,1)}, bf16[128,512]{1,0:T(8,128)(2,1)S(1)}, u32[]{:S(2)}, u32[]{:S(2)}) collective-permute-start(bf16[128,512]{1,0:T(8,128)(2,1)} %get-tuple-element.40.local), channel_id=1, source_target_pairs={{0,1},{1,2},{2,3},{3,4},{4,5},{5,6},{6,7},{7,8},{8,9},{9,10},{10,1... | collective-permute-start | bytes 393224 | tf_op jit(solution)/shard_map/ppermute | solution.py:400
  7.2 0.9 collective-permute-done.1
  8.1 0.7 add_add_fusion.1
  8.9 2.0 collective-permute-start.8
  10.9 5.7 %collective-permute-start.6 = (bf16[16,512]{1,0:T(8,128)(2,1)S(1)}, bf16[16,512]{1,0:T(8,128)(2,1)S(1)}, u32[]{:S(2)}, u32[]{:S(2)}) collective-permute-start(bf16[16,512]{1,0:T(8,128)(2,1)S(1)} %add_add_fusion.1), channel_id=1, source_target_pairs={{0,12},{1,13},{2,14},{3,15},{4,8},{5,9},{6,10},{7,11},{8,4},{9,5},... | collective-permute-start | bytes 49160 | tf_op jit(solution)/shard_map/ppermute | solution.py:77
  17.1 2.3 %broadcast_in_dim.4.gain = f32[2880,1]{1,0:T(8,128)} reshape(f32[2880]{0:T(1024)} %param.17) | data formatting | bytes 23040 | tf_op jit(solution)/shard_map/broadcast_in_dim | solution.py:419
  19.4 1.0 copy.13
  20.4 0.8 collective-permute-done.5
  21.2 0.6 add_add_fusion.sinks
  21.8 9.7 %shard_map.110 = (bf16[2880,128]{1,0:T(8,128)(2,1)}, bf16[2896,128]{1,0:T(8,128)(2,1)}) custom-call(bf16[2048,128]{1,0:T(8,128)(2,1)} %bitcast.24, bf16[128,512]{1,0:T(8,128)(2,1)} %copy-done.12, bf16[128,512]{1,0:T(8,128)(2,1)} %get-tuple-element.40.local, bf16[16,512]{1,0:T(8,128)(2,1)} %add_add_fusion.sinks, f32[272,128]{1,0:T(8,128)} %get-tuple-element.44.bias, ...), custom_call_target="tpu_custom_call" | custom-call | flops 1509949440 | bytes 11796480 | tf_op jit(solution)/shard_map/pallas_call | solution.py:209
  31.5 2.6 %collective-permute-start.10 = (bf16[2896,128]{1,0:T(8,128)(2,1)}, bf16[2896,128]{1,0:T(8,128)(2,1)S(1)}, u32[]{:S(2)}, u32[]{:S(2)}) collective-permute-start(bf16[2896,128]{1,0:T(8,128)(2,1)} %get-tuple-element.46.x_ref), channel_id=1, source_target_pairs={{0,4},{1,5},{2,6},{3,7},{4,8},{5,9},{6,10},{7,11},{8,12},{9,13},{1... | collective-permute-start | bytes 2224136 | tf_op jit(solution)/shard_map/ppermute | solution.py:359
  34.2 1.3 collective-permute-start.11
  35.5 0.7 collective-permute-start.7
  36.1 13.7 %collective-permute-done.10 = bf16[2896,128]{1,0:T(8,128)(2,1)S(1)} collective-permute-done((bf16[2896,128]{1,0:T(8,128)(2,1)}, bf16[2896,128]{1,0:T(8,128)(2,1)S(1)}, u32[]{:S(2)}, u32[]{:S(2)}) %collective-permute-start.10) | collective-permute-done | bytes 741408 | tf_op jit(solution)/shard_map/ppermute | solution.py:359
  49.9 4.1 %collective-permute-done.11 = bf16[2896,128]{1,0:T(8,128)(2,1)S(1)} collective-permute-done((bf16[2896,128]{1,0:T(8,128)(2,1)}, bf16[2896,128]{1,0:T(8,128)(2,1)S(1)}, u32[]{:S(2)}, u32[]{:S(2)}) %collective-permute-start.11) | collective-permute-done | bytes 741408 | tf_op jit(solution)/shard_map/ppermute | solution.py:360
  54.0 0.7 collective-permute-start.12
  54.7 1.5 collective-permute-start.13
  56.2 1.3 collective-permute-start.14
  57.6 14.2 %shard_map.111 = (f32[2880,128]{1,0:T(8,128)}, f32[2880,128]{1,0:T(8,128)}) custom-call(s32[1]{0:T(128)} %bitcast.6.me_ref, bf16[2896,128]{1,0:T(8,128)(2,1)} %get-tuple-element.46.x_ref, bf16[2896,128]{1,0:T(8,128)(2,1)} %copy-done.7, bf16[1440,2880]{1,0:T(8,128)(2,1)} %bitcast.14, bf16[1440,2880]{1,0:T(8,128)(2,1)} %collective-permute-done.8.gu1, ...), custom_call_target="tpu_custom_call" | custom-call | flops 6370099200 | bytes 24883200 | tf_op jit(solution)/shard_map/pallas_call | solution.py:300
  71.8 5.0 %collective-permute-done.14 = bf16[2896,128]{1,0:T(8,128)(2,1)} collective-permute-done((bf16[2896,128]{1,0:T(8,128)(2,1)S(1)}, bf16[2896,128]{1,0:T(8,128)(2,1)}, u32[]{:S(2)}, u32[]{:S(2)}) %collective-permute-start.14) | collective-permute-done | bytes 741408 | tf_op jit(solution)/shard_map/ppermute | solution.py:360
  76.8 1.4 select_select_fusion
  78.2 1.5 collective-permute-start.15
  79.7 1.5 collective-permute-start.16
  81.1 13.7 %shard_map.112 = (bf16[2880,128]{1,0:T(8,128)(2,1)}, bf16[2880,128]{1,0:T(8,128)(2,1)}) custom-call(s32[1]{0:T(128)} %bitcast.6.me_ref, bf16[2896,128]{1,0:T(8,128)(2,1)} %copy-done, bf16[2896,128]{1,0:T(8,128)(2,1)} %collective-permute-done.12.y_ref, bf16[1440,2880]{1,0:T(8,128)(2,1)} %bitcast.15, bf16[1440,2880]{1,0:T(8,128)(2,1)} %collective-permute-done.8.gu1, ...), custom_call_target="tpu_custom_call" | custom-call | flops 6370099200 | bytes 24883200 | tf_op jit(solution)/shard_map/pallas_call | solution.py:300
  94.9 1.6 collective-permute-done.16
  96.6 0.7 collective-permute-start.19
  97.3 0.7 collective-permute-start.23
  98.0 3.6 %collective-permute-start.22 = (bf16[2880,128]{1,0:T(8,128)(2,1)}, bf16[2880,128]{1,0:T(8,128)(2,1)S(1)}, u32[]{:S(2)}, u32[]{:S(2)}) collective-permute-start(bf16[2880,128]{1,0:T(8,128)(2,1)} %get-tuple-element.67), channel_id=1, source_target_pairs={{0,4},{1,5},{2,6},{3,7},{4,8},{5,9},{6,10},{7,11},{16,20},{17,21},... | collective-permute-start | bytes 2211848 | tf_op jit(solution)/shard_map/ppermute | solution.py:463
  101.7 4.5 %collective-permute-start.17 = (bf16[2880,128]{1,0:T(8,128)(2,1)}, bf16[2880,128]{1,0:T(8,128)(2,1)S(1)}, u32[]{:S(2)}, u32[]{:S(2)}) collective-permute-start(bf16[2880,128]{1,0:T(8,128)(2,1)} %get-tuple-element.58), channel_id=1, source_target_pairs={{0,4},{1,5},{2,6},{3,7},{4,8},{5,9},{6,10},{7,11},{16,20},{17,21},... | collective-permute-start | bytes 2211848 | tf_op jit(solution)/shard_map/ppermute | solution.py:463
  106.2 0.7 collective-permute-start.18
  106.9 14.0 %shard_map.113 = (f32[2880,128]{1,0:T(8,128)}, bf16[2880,128]{1,0:T(8,128)(2,1)}) custom-call(s32[1]{0:T(128)} %bitcast.6.me_ref, bf16[2896,128]{1,0:T(8,128)(2,1)} %copy-done.2, bf16[2896,128]{1,0:T(8,128)(2,1)} %copy-done.8, bf16[1440,2880]{1,0:T(8,128)(2,1)} %bitcast.16, bf16[1440,2880]{1,0:T(8,128)(2,1)} %collective-permute-done.8.gu1, ...), custom_call_target="tpu_custom_call" | custom-call | flops 6370099200 | bytes 24883200 | tf_op jit(solution)/shard_map/pallas_call | solution.py:300
  121.0 0.9 copy-done.9
  121.9 14.0 %shard_map.114 = (f32[2880,128]{1,0:T(8,128)}, bf16[2880,128]{1,0:T(8,128)(2,1)}) custom-call(s32[1]{0:T(128)} %bitcast.6.me_ref, bf16[2896,128]{1,0:T(8,128)(2,1)} %copy-done.1, bf16[2896,128]{1,0:T(8,128)(2,1)} %copy-done.9, bf16[1440,2880]{1,0:T(8,128)(2,1)} %bitcast.17, bf16[1440,2880]{1,0:T(8,128)(2,1)} %collective-permute-done.8.gu1, ...), custom_call_target="tpu_custom_call" | custom-call | flops 6370099200 | bytes 24883200 | tf_op jit(solution)/shard_map/pallas_call | solution.py:300
  135.9 1.5 collective-permute-start.20
  137.7 14.9 %collective-permute-done.20 = bf16[2880,128]{1,0:T(8,128)(2,1)S(1)} collective-permute-done((bf16[2880,128]{1,0:T(8,128)(2,1)S(1)}, bf16[2880,128]{1,0:T(8,128)(2,1)S(1)}, u32[]{:S(2)}, u32[]{:S(2)}) %collective-permute-start.20) | collective-permute-done | bytes 737312 | tf_op jit(solution)/shard_map/ppermute | solution.py:482
  152.7 1.4 collective-permute-start.24
  154.3 2.7 %collective-permute-start.21 = (bf16[2880,128]{1,0:T(8,128)(2,1)S(1)}, bf16[2880,128]{1,0:T(8,128)(2,1)S(1)}, u32[]{:S(2)}, u32[]{:S(2)}) collective-permute-start(bf16[2880,128]{1,0:T(8,128)(2,1)S(1)} %add_convert_fusion.3), channel_id=1, source_target_pairs={{0,8},{1,9},{2,10},{3,11},{4,0},{5,1},{6,2},{7,3},{8,12},{9,13},{1... | collective-permute-start | bytes 2211848 | tf_op jit(solution)/shard_map/ppermute | solution.py:490
  157.0 12.3 %collective-permute-done.24 = bf16[2880,128]{1,0:T(8,128)(2,1)S(1)} collective-permute-done((bf16[2880,128]{1,0:T(8,128)(2,1)S(1)}, bf16[2880,128]{1,0:T(8,128)(2,1)S(1)}, u32[]{:S(2)}, u32[]{:S(2)}) %collective-permute-start.24) | collective-permute-done | bytes 737312 | tf_op jit(solution)/shard_map/ppermute | solution.py:482
  169.3 1.4 collective-permute-start.27
  170.9 1.3 collective-permute-start.26
  172.2 6.3 %collective-permute-start.25 = (bf16[2880,128]{1,0:T(8,128)(2,1)S(1)}, bf16[2880,128]{1,0:T(8,128)(2,1)S(1)}, u32[]{:S(2)}, u32[]{:S(2)}) collective-permute-start(bf16[2880,128]{1,0:T(8,128)(2,1)S(1)} %add_convert_fusion.2), channel_id=1, source_target_pairs={{0,12},{1,13},{2,14},{3,15},{8,0},{9,1},{10,2},{11,3},{16,28},{17,... | collective-permute-start | bytes 2211848 | tf_op jit(solution)/shard_map/ppermute | solution.py:497
  178.5 2.5 %collective-permute-done.27 = bf16[2880,128]{1,0:T(8,128)(2,1)S(1)} collective-permute-done((bf16[2880,128]{1,0:T(8,128)(2,1)S(1)}, bf16[2880,128]{1,0:T(8,128)(2,1)S(1)}, u32[]{:S(2)}, u32[]{:S(2)}) %collective-permute-start.27) | collective-permute-done | bytes 737312 | tf_op jit(solution)/shard_map/ppermute | solution.py:494
  181.1 5.1 %collective-permute-done.26 = bf16[2880,128]{1,0:T(8,128)(2,1)S(1)} collective-permute-done((bf16[2880,128]{1,0:T(8,128)(2,1)S(1)}, bf16[2880,128]{1,0:T(8,128)(2,1)S(1)}, u32[]{:S(2)}, u32[]{:S(2)}) %collective-permute-start.26) | collective-permute-done | bytes 737312 | tf_op jit(solution)/shard_map/ppermute | solution.py:497
  186.1 12.2 %collective-permute-done.25 = bf16[2880,128]{1,0:T(8,128)(2,1)S(1)} collective-permute-done((bf16[2880,128]{1,0:T(8,128)(2,1)S(1)}, bf16[2880,128]{1,0:T(8,128)(2,1)S(1)}, u32[]{:S(2)}, u32[]{:S(2)}) %collective-permute-start.25) | collective-permute-done | bytes 737312 | tf_op jit(solution)/shard_map/ppermute | solution.py:497
  198.3 1.6 fusion
  (55 shorter events, 1.6 us)
Async XLA Ops:
  0.0 19.4 %copy-start.11 = (bf16[128,2048]{1,0:T(8,128)(2,1)S(1)}, bf16[128,2048]{1,0:T(8,128)(2,1)}, u32[]{:S(2)}) copy-start(bf16[128,2048]{1,0:T(8,128)(2,1)} %param.11) | copy-start | bytes 1572868
  1.8 5.4 %collective-permute-start.2 = (bf16[16,512]{1,0:T(8,128)(2,1)}, bf16[16,512]{1,0:T(8,128)(2,1)S(1)}, u32[]{:S(2)}, u32[]{:S(2)}) collective-permute-start(bf16[16,512]{1,0:T(8,128)(2,1)} %get-tuple-element.39), channel_id=1, source_target_pairs={{0,3},{1,2},{2,1},{3,0},{4,7},{5,6},{6,5},{7,4},{8,11},{9,10},{10,... | collective-permute-start | bytes 49160 | tf_op jit(solution)/shard_map/ppermute | solution.py:77
  4.2 3.9 %collective-permute-start.1 = (bf16[16,512]{1,0:T(8,128)(2,1)}, bf16[16,512]{1,0:T(8,128)(2,1)S(1)}, u32[]{:S(2)}, u32[]{:S(2)}) collective-permute-start(bf16[16,512]{1,0:T(8,128)(2,1)} %get-tuple-element.39), channel_id=1, source_target_pairs={{0,2},{1,3},{2,0},{3,1},{4,6},{5,7},{6,4},{7,5},{8,10},{9,11},{10,... | collective-permute-start | bytes 49160 | tf_op jit(solution)/shard_map/ppermute | solution.py:77
  4.8 3.4 %collective-permute-start = (bf16[16,512]{1,0:T(8,128)(2,1)}, bf16[16,512]{1,0:T(8,128)(2,1)S(1)}, u32[]{:S(2)}, u32[]{:S(2)}) collective-permute-start(bf16[16,512]{1,0:T(8,128)(2,1)} %get-tuple-element.39), channel_id=1, source_target_pairs={{0,1},{1,0},{2,3},{3,2},{4,5},{5,4},{6,7},{7,6},{8,9},{9,8},{10,11... | collective-permute-start | bytes 49160 | tf_op jit(solution)/shard_map/ppermute | solution.py:77
  4.9 4.0 %collective-permute-start.3 = (bf16[128,512]{1,0:T(8,128)(2,1)}, bf16[128,512]{1,0:T(8,128)(2,1)S(1)}, u32[]{:S(2)}, u32[]{:S(2)}) collective-permute-start(bf16[128,512]{1,0:T(8,128)(2,1)} %get-tuple-element.40.local), channel_id=1, source_target_pairs={{0,1},{1,2},{2,3},{3,4},{4,5},{5,6},{6,7},{7,8},{8,9},{9,10},{10,1... | collective-permute-start | bytes 393224 | tf_op jit(solution)/shard_map/ppermute | solution.py:400
  8.9 13.0 %copy-start.12 = (bf16[128,512]{1,0:T(8,128)(2,1)}, bf16[128,512]{1,0:T(8,128)(2,1)S(1)}, u32[]{:S(2)}) copy-start(bf16[128,512]{1,0:T(8,128)(2,1)S(1)} %collective-permute-done.3.halo) | copy-start | bytes 393220
  8.9 48.7 %collective-permute-start.8 = (bf16[1440,2880]{1,0:T(8,128)(2,1)}, bf16[1440,2880]{1,0:T(8,128)(2,1)}, u32[]{:S(2)}, u32[]{:S(2)}) collective-permute-start(bf16[1440,2880]{1,0:T(8,128)(2,1)} %bitcast.13), channel_id=1, source_target_pairs={{0,1},{1,0},{2,3},{3,2},{4,5},{5,4},{6,7},{7,6},{8,9},{9,8},{10,11... | collective-permute-start | bytes 24883208 | tf_op jit(solution)/shard_map/ppermute | solution.py:408
  10.9 46.7 %collective-permute-start.9 = (bf16[720,2880]{1,0:T(8,128)(2,1)}, bf16[720,2880]{1,0:T(8,128)(2,1)}, u32[]{:S(2)}, u32[]{:S(2)}) collective-permute-start(bf16[720,2880]{1,0:T(8,128)(2,1)} %bitcast.18), channel_id=1, source_target_pairs={{0,1},{1,0},{2,3},{3,2},{4,5},{5,4},{6,7},{7,6},{8,9},{9,8},{10,11... | collective-permute-start | bytes 12441608 | tf_op jit(solution)/shard_map/ppermute | solution.py:409
  10.9 9.6 %collective-permute-start.6 = (bf16[16,512]{1,0:T(8,128)(2,1)S(1)}, bf16[16,512]{1,0:T(8,128)(2,1)S(1)}, u32[]{:S(2)}, u32[]{:S(2)}) collective-permute-start(bf16[16,512]{1,0:T(8,128)(2,1)S(1)} %add_add_fusion.1), channel_id=1, source_target_pairs={{0,12},{1,13},{2,14},{3,15},{4,8},{5,9},{6,10},{7,11},{8,4},{9,5},... | collective-permute-start | bytes 49160 | tf_op jit(solution)/shard_map/ppermute | solution.py:77
  16.6 4.6 %collective-permute-start.5 = (bf16[16,512]{1,0:T(8,128)(2,1)S(1)}, bf16[16,512]{1,0:T(8,128)(2,1)S(1)}, u32[]{:S(2)}, u32[]{:S(2)}) collective-permute-start(bf16[16,512]{1,0:T(8,128)(2,1)S(1)} %add_add_fusion.1), channel_id=1, source_target_pairs={{0,8},{1,9},{2,10},{3,11},{4,12},{5,13},{6,14},{7,15},{8,0},{9,1},... | collective-permute-start | bytes 49160 | tf_op jit(solution)/shard_map/ppermute | solution.py:77
  16.6 4.6 %collective-permute-start.4 = (bf16[16,512]{1,0:T(8,128)(2,1)S(1)}, bf16[16,512]{1,0:T(8,128)(2,1)S(1)}, u32[]{:S(2)}, u32[]{:S(2)}) collective-permute-start(bf16[16,512]{1,0:T(8,128)(2,1)S(1)} %add_add_fusion.1), channel_id=1, source_target_pairs={{0,4},{1,5},{2,6},{3,7},{4,0},{5,1},{6,2},{7,3},{8,12},{9,13},{10,... | collective-permute-start | bytes 49160 | tf_op jit(solution)/shard_map/ppermute | solution.py:77
  31.5 18.3 %collective-permute-start.10 = (bf16[2896,128]{1,0:T(8,128)(2,1)}, bf16[2896,128]{1,0:T(8,128)(2,1)S(1)}, u32[]{:S(2)}, u32[]{:S(2)}) collective-permute-start(bf16[2896,128]{1,0:T(8,128)(2,1)} %get-tuple-element.46.x_ref), channel_id=1, source_target_pairs={{0,4},{1,5},{2,6},{3,7},{4,8},{5,9},{6,10},{7,11},{8,12},{9,13},{1... | collective-permute-start | bytes 2224136 | tf_op jit(solution)/shard_map/ppermute | solution.py:359
  34.2 19.7 %collective-permute-start.11 = (bf16[2896,128]{1,0:T(8,128)(2,1)}, bf16[2896,128]{1,0:T(8,128)(2,1)S(1)}, u32[]{:S(2)}, u32[]{:S(2)}) collective-permute-start(bf16[2896,128]{1,0:T(8,128)(2,1)} %get-tuple-element.46.x_ref), channel_id=1, source_target_pairs={{4,0},{5,1},{6,2},{7,3},{8,4},{9,5},{10,6},{11,7},{12,8},{13,9},{1... | collective-permute-start | bytes 2224136 | tf_op jit(solution)/shard_map/ppermute | solution.py:360
  35.5 18.6 %collective-permute-start.7 = (bf16[2896,128]{1,0:T(8,128)(2,1)}, bf16[2896,128]{1,0:T(8,128)(2,1)S(1)}, u32[]{:S(2)}, u32[]{:S(2)}) collective-permute-start(bf16[2896,128]{1,0:T(8,128)(2,1)} %get-tuple-element.46.x_ref), channel_id=1, source_target_pairs={{0,2},{1,3},{2,0},{3,1},{4,6},{5,7},{6,4},{7,5},{8,10},{9,11},{10,... | collective-permute-start | bytes 2224136 | tf_op jit(solution)/shard_map/ppermute | solution.py:434
  54.0 17.8 %copy-start = (bf16[2896,128]{1,0:T(8,128)(2,1)}, bf16[2896,128]{1,0:T(8,128)(2,1)S(1)}, u32[]{:S(2)}) copy-start(bf16[2896,128]{1,0:T(8,128)(2,1)S(1)} %broadcast_select_fusion.2.x_ref) | copy-start | bytes 2224132
  54.0 3.5 %copy-start.7 = (bf16[2896,128]{1,0:T(8,128)(2,1)}, bf16[2896,128]{1,0:T(8,128)(2,1)S(1)}, u32[]{:S(2)}) copy-start(bf16[2896,128]{1,0:T(8,128)(2,1)S(1)} %collective-permute-done.7.y_ref) | copy-start | bytes 2224132
  54.0 17.7 %collective-permute-start.12 = (bf16[2896,128]{1,0:T(8,128)(2,1)S(1)}, bf16[2896,128]{1,0:T(8,128)(2,1)}, u32[]{:S(2)}, u32[]{:S(2)}) collective-permute-start(bf16[2896,128]{1,0:T(8,128)(2,1)S(1)} %broadcast_select_fusion.2.x_ref), channel_id=1, source_target_pairs={{0,2},{1,3},{2,0},{3,1},{4,6},{5,7},{6,4},{7,5},{8,10},{9,11},{10,... | collective-permute-start | bytes 2224136 | tf_op jit(solution)/shard_map/ppermute | solution.py:440
  54.7 17.1 %collective-permute-start.13 = (bf16[2896,128]{1,0:T(8,128)(2,1)S(1)}, bf16[2896,128]{1,0:T(8,128)(2,1)}, u32[]{:S(2)}, u32[]{:S(2)}) collective-permute-start(bf16[2896,128]{1,0:T(8,128)(2,1)S(1)} %collective-permute-done.10), channel_id=1, source_target_pairs={{4,8},{5,9},{6,10},{7,11},{8,12},{9,13},{10,14},{11,15},{20,24},{2... | collective-permute-start | bytes 2224136 | tf_op jit(solution)/shard_map/ppermute | solution.py:359
  56.2 20.5 %collective-permute-start.14 = (bf16[2896,128]{1,0:T(8,128)(2,1)S(1)}, bf16[2896,128]{1,0:T(8,128)(2,1)}, u32[]{:S(2)}, u32[]{:S(2)}) collective-permute-start(bf16[2896,128]{1,0:T(8,128)(2,1)S(1)} %collective-permute-done.11), channel_id=1, source_target_pairs={{4,0},{5,1},{6,2},{7,3},{8,4},{9,5},{10,6},{11,7},{20,16},{21,17},... | collective-permute-start | bytes 2224136 | tf_op jit(solution)/shard_map/ppermute | solution.py:360
  78.2 16.7 %copy-start.2 = (bf16[2896,128]{1,0:T(8,128)(2,1)}, bf16[2896,128]{1,0:T(8,128)(2,1)S(1)}, u32[]{:S(2)}) copy-start(bf16[2896,128]{1,0:T(8,128)(2,1)S(1)} %get-tuple-element.56.x_ref) | copy-start | bytes 2224132
  78.2 16.7 %collective-permute-start.15 = (bf16[2896,128]{1,0:T(8,128)(2,1)S(1)}, bf16[2896,128]{1,0:T(8,128)(2,1)S(1)}, u32[]{:S(2)}, u32[]{:S(2)}) collective-permute-start(bf16[2896,128]{1,0:T(8,128)(2,1)S(1)} %get-tuple-element.56.x_ref), channel_id=1, source_target_pairs={{0,2},{1,3},{2,0},{3,1},{4,6},{5,7},{6,4},{7,5},{8,10},{9,11},{10,... | collective-permute-start | bytes 2224136 | tf_op jit(solution)/shard_map/ppermute | solution.py:440
  79.7 16.8 %collective-permute-start.16 = (bf16[2896,128]{1,0:T(8,128)(2,1)S(1)}, bf16[2896,128]{1,0:T(8,128)(2,1)S(1)}, u32[]{:S(2)}, u32[]{:S(2)}) collective-permute-start(bf16[2896,128]{1,0:T(8,128)(2,1)S(1)} %get-tuple-element.57), channel_id=1, source_target_pairs={{8,12},{9,13},{10,14},{11,15},{4,0},{5,1},{6,2},{7,3},{24,28},{25,... | collective-permute-start | bytes 2224136 | tf_op jit(solution)/shard_map/ppermute | solution.py:356
  94.9 12.0 %copy-start.8 = (bf16[2896,128]{1,0:T(8,128)(2,1)}, bf16[2896,128]{1,0:T(8,128)(2,1)S(1)}, u32[]{:S(2)}) copy-start(bf16[2896,128]{1,0:T(8,128)(2,1)S(1)} %collective-permute-done.15.y_ref) | copy-start | bytes 2224132
  96.6 24.3 %copy-start.1 = (bf16[2896,128]{1,0:T(8,128)(2,1)}, bf16[2896,128]{1,0:T(8,128)(2,1)S(1)}, u32[]{:S(2)}) copy-start(bf16[2896,128]{1,0:T(8,128)(2,1)S(1)} %broadcast_select_fusion.x_ref) | copy-start | bytes 2224132
  96.6 24.4 %collective-permute-start.19 = (bf16[2896,128]{1,0:T(8,128)(2,1)S(1)}, bf16[2896,128]{1,0:T(8,128)(2,1)S(1)}, u32[]{:S(2)}, u32[]{:S(2)}) collective-permute-start(bf16[2896,128]{1,0:T(8,128)(2,1)S(1)} %broadcast_select_fusion.x_ref), channel_id=1, source_target_pairs={{0,2},{1,3},{2,0},{3,1},{4,6},{5,7},{6,4},{7,5},{8,10},{9,11},{10,... | collective-permute-start | bytes 2224136 | tf_op jit(solution)/shard_map/ppermute | solution.py:440
  97.3 38.6 %collective-permute-start.23 = (bf16[2880,128]{1,0:T(8,128)(2,1)}, bf16[2880,128]{1,0:T(8,128)(2,1)S(1)}, u32[]{:S(2)}, u32[]{:S(2)}) collective-permute-start(bf16[2880,128]{1,0:T(8,128)(2,1)} %get-tuple-element.67), channel_id=1, source_target_pairs={{8,4},{9,5},{10,6},{11,7},{12,8},{13,9},{14,10},{15,11},{24,20},{2... | collective-permute-start | bytes 2211848 | tf_op jit(solution)/shard_map/ppermute | solution.py:463
  98.0 37.9 %collective-permute-start.22 = (bf16[2880,128]{1,0:T(8,128)(2,1)}, bf16[2880,128]{1,0:T(8,128)(2,1)S(1)}, u32[]{:S(2)}, u32[]{:S(2)}) collective-permute-start(bf16[2880,128]{1,0:T(8,128)(2,1)} %get-tuple-element.67), channel_id=1, source_target_pairs={{0,4},{1,5},{2,6},{3,7},{4,8},{5,9},{6,10},{7,11},{16,20},{17,21},... | collective-permute-start | bytes 2211848 | tf_op jit(solution)/shard_map/ppermute | solution.py:463
  101.7 34.3 %collective-permute-start.17 = (bf16[2880,128]{1,0:T(8,128)(2,1)}, bf16[2880,128]{1,0:T(8,128)(2,1)S(1)}, u32[]{:S(2)}, u32[]{:S(2)}) collective-permute-start(bf16[2880,128]{1,0:T(8,128)(2,1)} %get-tuple-element.58), channel_id=1, source_target_pairs={{0,4},{1,5},{2,6},{3,7},{4,8},{5,9},{6,10},{7,11},{16,20},{17,21},... | collective-permute-start | bytes 2211848 | tf_op jit(solution)/shard_map/ppermute | solution.py:463
  106.2 29.7 %collective-permute-start.18 = (bf16[2880,128]{1,0:T(8,128)(2,1)}, bf16[2880,128]{1,0:T(8,128)(2,1)S(1)}, u32[]{:S(2)}, u32[]{:S(2)}) collective-permute-start(bf16[2880,128]{1,0:T(8,128)(2,1)} %get-tuple-element.58), channel_id=1, source_target_pairs={{8,4},{9,5},{10,6},{11,7},{12,8},{13,9},{14,10},{15,11},{24,20},{2... | collective-permute-start | bytes 2211848 | tf_op jit(solution)/shard_map/ppermute | solution.py:463
  121.0 15.0 %copy-start.14 = (bf16[2880,128]{1,0:T(8,128)(2,1)S(1)}, bf16[2880,128]{1,0:T(8,128)(2,1)}, u32[]{:S(2)}) copy-start(bf16[2880,128]{1,0:T(8,128)(2,1)} %get-tuple-element.63) | copy-start | bytes 2211844
  121.0 16.4 %copy-start.4 = (f32[2880,128]{1,0:T(8,128)S(1)}, f32[2880,128]{1,0:T(8,128)}, u32[]{:S(2)}) copy-start(f32[2880,128]{1,0:T(8,128)} %get-tuple-element.71) | copy-start | bytes 4423684
  121.0 0.9 copy-start.9
  135.9 16.7 %collective-permute-start.20 = (bf16[2880,128]{1,0:T(8,128)(2,1)S(1)}, bf16[2880,128]{1,0:T(8,128)(2,1)S(1)}, u32[]{:S(2)}, u32[]{:S(2)}) collective-permute-start(bf16[2880,128]{1,0:T(8,128)(2,1)S(1)} %copy-done.14), channel_id=1, source_target_pairs={{0,2},{1,3},{2,0},{3,1},{4,6},{5,7},{6,4},{7,5},{8,10},{9,11},{10,... | collective-permute-start | bytes 2211848 | tf_op jit(solution)/shard_map/ppermute | solution.py:482
  137.4 15.2 %copy-start.13 = (bf16[2880,128]{1,0:T(8,128)(2,1)S(1)}, bf16[2880,128]{1,0:T(8,128)(2,1)}, u32[]{:S(2)}) copy-start(bf16[2880,128]{1,0:T(8,128)(2,1)} %get-tuple-element.70) | copy-start | bytes 2211844
  137.4 16.7 %copy-start.6 = (f32[2880,128]{1,0:T(8,128)S(1)}, f32[2880,128]{1,0:T(8,128)}, u32[]{:S(2)}) copy-start(f32[2880,128]{1,0:T(8,128)} %get-tuple-element.59) | copy-start | bytes 4423684
  152.7 16.7 %collective-permute-start.24 = (bf16[2880,128]{1,0:T(8,128)(2,1)S(1)}, bf16[2880,128]{1,0:T(8,128)(2,1)S(1)}, u32[]{:S(2)}, u32[]{:S(2)}) collective-permute-start(bf16[2880,128]{1,0:T(8,128)(2,1)S(1)} %copy-done.13), channel_id=1, source_target_pairs={{0,2},{1,3},{2,0},{3,1},{4,6},{5,7},{6,4},{7,5},{8,10},{9,11},{10,... | collective-permute-start | bytes 2211848 | tf_op jit(solution)/shard_map/ppermute | solution.py:482
  154.1 16.7 %copy-start.5 = (f32[2880,128]{1,0:T(8,128)S(1)}, f32[2880,128]{1,0:T(8,128)}, u32[]{:S(2)}) copy-start(f32[2880,128]{1,0:T(8,128)} %get-tuple-element.64) | copy-start | bytes 4423684
  154.3 44.0 %copy-start.3 = (f32[2880,128]{1,0:T(8,128)S(1)}, f32[2880,128]{1,0:T(8,128)}, u32[]{:S(2)}) copy-start(f32[2880,128]{1,0:T(8,128)} %get-tuple-element.49) | copy-start | bytes 4423684
  154.3 44.0 %copy-start.10 = (bf16[2880,128]{1,0:T(8,128)(2,1)S(1)}, bf16[2880,128]{1,0:T(8,128)(2,1)}, u32[]{:S(2)}) copy-start(bf16[2880,128]{1,0:T(8,128)(2,1)} %get-tuple-element.45) | copy-start | bytes 2211844
  154.3 24.2 %collective-permute-start.21 = (bf16[2880,128]{1,0:T(8,128)(2,1)S(1)}, bf16[2880,128]{1,0:T(8,128)(2,1)S(1)}, u32[]{:S(2)}, u32[]{:S(2)}) collective-permute-start(bf16[2880,128]{1,0:T(8,128)(2,1)S(1)} %add_convert_fusion.3), channel_id=1, source_target_pairs={{0,8},{1,9},{2,10},{3,11},{4,0},{5,1},{6,2},{7,3},{8,12},{9,13},{1... | collective-permute-start | bytes 2211848 | tf_op jit(solution)/shard_map/ppermute | solution.py:490
  169.3 11.8 %collective-permute-start.27 = (bf16[2880,128]{1,0:T(8,128)(2,1)S(1)}, bf16[2880,128]{1,0:T(8,128)(2,1)S(1)}, u32[]{:S(2)}, u32[]{:S(2)}) collective-permute-start(bf16[2880,128]{1,0:T(8,128)(2,1)S(1)} %add_convert_fusion.1), channel_id=1, source_target_pairs={{0,2},{1,3},{2,0},{3,1},{4,6},{5,7},{6,4},{7,5},{8,10},{9,11},{10,... | collective-permute-start | bytes 2211848 | tf_op jit(solution)/shard_map/ppermute | solution.py:494
  170.9 15.3 %collective-permute-start.26 = (bf16[2880,128]{1,0:T(8,128)(2,1)S(1)}, bf16[2880,128]{1,0:T(8,128)(2,1)S(1)}, u32[]{:S(2)}, u32[]{:S(2)}) collective-permute-start(bf16[2880,128]{1,0:T(8,128)(2,1)S(1)} %add_convert_fusion.2), channel_id=1, source_target_pairs={{4,12},{5,13},{6,14},{7,15},{12,0},{13,1},{14,2},{15,3},{20,28},{2... | collective-permute-start | bytes 2211848 | tf_op jit(solution)/shard_map/ppermute | solution.py:497
  172.2 26.1 %collective-permute-start.25 = (bf16[2880,128]{1,0:T(8,128)(2,1)S(1)}, bf16[2880,128]{1,0:T(8,128)(2,1)S(1)}, u32[]{:S(2)}, u32[]{:S(2)}) collective-permute-start(bf16[2880,128]{1,0:T(8,128)(2,1)S(1)} %add_convert_fusion.2), channel_id=1, source_target_pairs={{0,12},{1,13},{2,14},{3,15},{8,0},{9,1},{10,2},{11,3},{16,28},{17,... | collective-permute-start | bytes 2211848 | tf_op jit(solution)/shard_map/ppermute | solution.py:497

commit v6 on v5

--- a/solution.py
+++ b/solution.py
@@ -481,7 +481,9 @@
         theirs = after(theirs, *ready)
         returned = lax.ppermute(theirs, "seq", across)
         if n == 0:
-            slow = [after(back, parts[0]) for back in slow]
+            slow = [after(slow[0], parts[0])] + [
+                after(back, returned, parts[0]) for back in slow[1:]
+            ]
             for back in slow:
                 cross_sum = cross_sum + back.astype(jnp.float32)
         if pending is not None:

time: 201 us -> 187 us (0.930)
  waiting for transfers between devices: 73.1 us -> 62.9 us
  starting transfers between devices: 49.6 us -> 47.4 us
    ppermute x2, waiting for transfers between devices: 27.3 us -> 12.8 us  [on_device(): returned = lax.ppermute(theirs, 'seq', across)]
    ppermute x1, waiting for transfers between devices: 2.53 us -> 4.63 us  [on_device(): lax.ppermute(after(cross_sum.astype(half), *ready), 'seq', across)]
    ppermute x3, waiting for transfers between devices: 17.2 us -> 19.3 us  [on_device(): back = lax.ppermute(both, 'seq', line_pairs(moves))]
  transfers between devices with their start and end apart: 28 -> 28, of which waited for: 11 -> 10; matrix products, arithmetic and copies ran while one was open for 3% -> 3% of each run, Pallas kernels for 33% -> 35%
where the time goes in v6:
time: 187 us; the launch traced here: 186 us
  Pallas kernels  67.3 us (36%)
  waiting for transfers between devices  62.9 us (34%)
  starting transfers between devices  47.4 us (25%)
  other arithmetic  5.1 us (3%)
  local copies, waits for them, and re-layouts  3.3 us (2%)
    pallas_call x4, Pallas kernels, expert_rows(): pl.pallas_call(functools.partial(expert_kernel, experts), out_shape=[jax....  55.8 us
    ppermute x3, waiting for transfers between devices, on_device(): back = lax.ppermute(both, 'seq', line_pairs(moves))  19.3 us
    ppermute x2, waiting for transfers between devices, next_blocks(): lax.ppermute(below, 'seq', line_pairs(up))  13.7 us
    ppermute x2, waiting for transfers between devices, on_device(): returned = lax.ppermute(theirs, 'seq', across)  12.8 us
    ppermute x3, starting transfers between devices, on_device(): back = lax.ppermute(both, 'seq', line_pairs(moves))  9.74 us
    pallas_call x1, Pallas kernels, attended_rows(): pl.pallas_call(functools.partial(attention_kernel, experts), out_shape=(j...  9.7 us
    ppermute x6, starting transfers between devices, summed(): lax.ppermute(block, axis, [(i, i ^ step * m) for i in range(shards)])  9.36 us
    ppermute x2, waiting for transfers between devices, next_blocks(): lax.ppermute(above, 'seq', line_pairs(down))  9.02 us
  transfers between devices with their start and end apart: 28, of which 10 were waited for; matrix products, arithmetic and copies ran while one was open for 3% of the time, Pallas kernels for 35%

profile of v6, /device:TPU:0, one launch (start us, length us, event | category | flops | bytes accessed | tf_op | source)
XLA Modules:
  0.0 186.3 jit_solution(10357872220673635043)
XLA Ops:
  0.0 1.8 shard_map.109
  1.8 2.4 %collective-permute-start.2 = (bf16[16,512]{1,0:T(8,128)(2,1)}, bf16[16,512]{1,0:T(8,128)(2,1)S(1)}, u32[]{:S(2)}, u32[]{:S(2)}) collective-permute-start(bf16[16,512]{1,0:T(8,128)(2,1)} %get-tuple-element.39), channel_id=1, source_target_pairs={{0,3},{1,2},{2,1},{3,0},{4,7},{5,6},{6,5},{7,4},{8,11},{9,10},{10,... | collective-permute-start | bytes 49160 | tf_op jit(solution)/shard_map/ppermute | solution.py:77
  4.2 0.6 collective-permute-start.1
  4.9 2.3 %collective-permute-start.3 = (bf16[128,512]{1,0:T(8,128)(2,1)}, bf16[128,512]{1,0:T(8,128)(2,1)S(1)}, u32[]{:S(2)}, u32[]{:S(2)}) collective-permute-start(bf16[128,512]{1,0:T(8,128)(2,1)} %get-tuple-element.40.local), channel_id=1, source_target_pairs={{0,1},{1,2},{2,3},{3,4},{4,5},{5,6},{6,7},{7,8},{8,9},{9,10},{10,1... | collective-permute-start | bytes 393224 | tf_op jit(solution)/shard_map/ppermute | solution.py:400
  7.2 0.9 collective-permute-done.1
  8.1 0.7 add_add_fusion.1
  8.9 2.0 %collective-permute-start.8 = (bf16[1440,2880]{1,0:T(8,128)(2,1)}, bf16[1440,2880]{1,0:T(8,128)(2,1)}, u32[]{:S(2)}, u32[]{:S(2)}) collective-permute-start(bf16[1440,2880]{1,0:T(8,128)(2,1)} %bitcast.13), channel_id=1, source_target_pairs={{0,1},{1,0},{2,3},{3,2},{4,5},{5,4},{6,7},{7,6},{8,9},{9,8},{10,11... | collective-permute-start | bytes 24883208 | tf_op jit(solution)/shard_map/ppermute | solution.py:408
  10.9 5.7 %collective-permute-start.6 = (bf16[16,512]{1,0:T(8,128)(2,1)S(1)}, bf16[16,512]{1,0:T(8,128)(2,1)S(1)}, u32[]{:S(2)}, u32[]{:S(2)}) collective-permute-start(bf16[16,512]{1,0:T(8,128)(2,1)S(1)} %add_add_fusion.1), channel_id=1, source_target_pairs={{0,12},{1,13},{2,14},{3,15},{4,8},{5,9},{6,10},{7,11},{8,4},{9,5},... | collective-permute-start | bytes 49160 | tf_op jit(solution)/shard_map/ppermute | solution.py:77
  16.6 0.6 collective-permute-start.4
  17.1 2.2 %broadcast_in_dim.4.gain = f32[2880,1]{1,0:T(8,128)} reshape(f32[2880]{0:T(1024)} %param.17) | data formatting | bytes 23040 | tf_op jit(solution)/shard_map/broadcast_in_dim | solution.py:419
  19.4 1.0 copy.13
  20.4 0.8 collective-permute-done.5
  21.2 0.6 add_add_fusion.sinks
  21.8 9.7 %shard_map.110 = (bf16[2880,128]{1,0:T(8,128)(2,1)}, bf16[2896,128]{1,0:T(8,128)(2,1)}) custom-call(bf16[2048,128]{1,0:T(8,128)(2,1)} %bitcast.24, bf16[128,512]{1,0:T(8,128)(2,1)} %copy-done.12, bf16[128,512]{1,0:T(8,128)(2,1)} %get-tuple-element.40.local, bf16[16,512]{1,0:T(8,128)(2,1)} %add_add_fusion.sinks, f32[272,128]{1,0:T(8,128)} %get-tuple-element.44.bias, ...), custom_call_target="tpu_custom_call" | custom-call | flops 1509949440 | bytes 11796480 | tf_op jit(solution)/shard_map/pallas_call | solution.py:209
  31.5 2.6 %collective-permute-start.10 = (bf16[2896,128]{1,0:T(8,128)(2,1)}, bf16[2896,128]{1,0:T(8,128)(2,1)S(1)}, u32[]{:S(2)}, u32[]{:S(2)}) collective-permute-start(bf16[2896,128]{1,0:T(8,128)(2,1)} %get-tuple-element.46.x_ref), channel_id=1, source_target_pairs={{0,4},{1,5},{2,6},{3,7},{4,8},{5,9},{6,10},{7,11},{8,12},{9,13},{1... | collective-permute-start | bytes 2224136 | tf_op jit(solution)/shard_map/ppermute | solution.py:359
  34.1 1.3 collective-permute-start.11
  35.4 0.7 collective-permute-start.7
  36.1 13.7 %collective-permute-done.10 = bf16[2896,128]{1,0:T(8,128)(2,1)S(1)} collective-permute-done((bf16[2896,128]{1,0:T(8,128)(2,1)}, bf16[2896,128]{1,0:T(8,128)(2,1)S(1)}, u32[]{:S(2)}, u32[]{:S(2)}) %collective-permute-start.10) | collective-permute-done | bytes 741408 | tf_op jit(solution)/shard_map/ppermute | solution.py:359
  49.8 4.1 %collective-permute-done.11 = bf16[2896,128]{1,0:T(8,128)(2,1)S(1)} collective-permute-done((bf16[2896,128]{1,0:T(8,128)(2,1)}, bf16[2896,128]{1,0:T(8,128)(2,1)S(1)}, u32[]{:S(2)}, u32[]{:S(2)}) %collective-permute-start.11) | collective-permute-done | bytes 741408 | tf_op jit(solution)/shard_map/ppermute | solution.py:360
  54.0 0.7 collective-permute-start.12
  54.7 1.5 collective-permute-start.13
  56.2 1.3 collective-permute-start.14
  57.6 14.2 %shard_map.111 = (f32[2880,128]{1,0:T(8,128)}, f32[2880,128]{1,0:T(8,128)}) custom-call(s32[1]{0:T(128)} %bitcast.6.me_ref, bf16[2896,128]{1,0:T(8,128)(2,1)} %get-tuple-element.46.x_ref, bf16[2896,128]{1,0:T(8,128)(2,1)} %copy-done.7, bf16[1440,2880]{1,0:T(8,128)(2,1)} %bitcast.14, bf16[1440,2880]{1,0:T(8,128)(2,1)} %collective-permute-done.8.gu1, ...), custom_call_target="tpu_custom_call" | custom-call | flops 6370099200 | bytes 24883200 | tf_op jit(solution)/shard_map/pallas_call | solution.py:300
  71.8 5.0 %collective-permute-done.14 = bf16[2896,128]{1,0:T(8,128)(2,1)} collective-permute-done((bf16[2896,128]{1,0:T(8,128)(2,1)S(1)}, bf16[2896,128]{1,0:T(8,128)(2,1)}, u32[]{:S(2)}, u32[]{:S(2)}) %collective-permute-start.14) | collective-permute-done | bytes 741408 | tf_op jit(solution)/shard_map/ppermute | solution.py:360
  76.8 1.4 select_select_fusion
  78.2 1.5 collective-permute-start.15
  79.7 1.5 collective-permute-start.16
  81.1 13.7 %shard_map.112 = (bf16[2880,128]{1,0:T(8,128)(2,1)}, bf16[2880,128]{1,0:T(8,128)(2,1)}) custom-call(s32[1]{0:T(128)} %bitcast.6.me_ref, bf16[2896,128]{1,0:T(8,128)(2,1)} %copy-done, bf16[2896,128]{1,0:T(8,128)(2,1)} %collective-permute-done.12.y_ref, bf16[1440,2880]{1,0:T(8,128)(2,1)} %bitcast.15, bf16[1440,2880]{1,0:T(8,128)(2,1)} %collective-permute-done.8.gu1, ...), custom_call_target="tpu_custom_call" | custom-call | flops 6370099200 | bytes 24883200 | tf_op jit(solution)/shard_map/pallas_call | solution.py:300
  94.9 1.6 collective-permute-done.16
  96.6 0.7 collective-permute-start.19
  97.3 3.0 %collective-permute-start.17 = (bf16[2880,128]{1,0:T(8,128)(2,1)}, bf16[2880,128]{1,0:T(8,128)(2,1)S(1)}, u32[]{:S(2)}, u32[]{:S(2)}) collective-permute-start(bf16[2880,128]{1,0:T(8,128)(2,1)} %get-tuple-element.58), channel_id=1, source_target_pairs={{0,4},{1,5},{2,6},{3,7},{4,8},{5,9},{6,10},{7,11},{16,20},{17,21},... | collective-permute-start | bytes 2211848 | tf_op jit(solution)/shard_map/ppermute | solution.py:463
  100.3 0.7 collective-permute-start.18
  101.0 0.7 collective-permute-start.23
  101.8 3.4 %collective-permute-start.22 = (bf16[2880,128]{1,0:T(8,128)(2,1)}, bf16[2880,128]{1,0:T(8,128)(2,1)S(1)}, u32[]{:S(2)}, u32[]{:S(2)}) collective-permute-start(bf16[2880,128]{1,0:T(8,128)(2,1)} %get-tuple-element.67), channel_id=1, source_target_pairs={{0,4},{1,5},{2,6},{3,7},{4,8},{5,9},{6,10},{7,11},{16,20},{17,21},... | collective-permute-start | bytes 2211848 | tf_op jit(solution)/shard_map/ppermute | solution.py:463
  105.1 14.0 %shard_map.113 = (f32[2880,128]{1,0:T(8,128)}, bf16[2880,128]{1,0:T(8,128)(2,1)}) custom-call(s32[1]{0:T(128)} %bitcast.6.me_ref, bf16[2896,128]{1,0:T(8,128)(2,1)} %copy-done.2, bf16[2896,128]{1,0:T(8,128)(2,1)} %copy-done.8, bf16[1440,2880]{1,0:T(8,128)(2,1)} %bitcast.16, bf16[1440,2880]{1,0:T(8,128)(2,1)} %collective-permute-done.8.gu1, ...), custom_call_target="tpu_custom_call" | custom-call | flops 6370099200 | bytes 24883200 | tf_op jit(solution)/shard_map/pallas_call | solution.py:300
  119.2 1.5 collective-permute-start.20
  120.6 13.9 %shard_map.114 = (f32[2880,128]{1,0:T(8,128)}, bf16[2880,128]{1,0:T(8,128)(2,1)}) custom-call(s32[1]{0:T(128)} %bitcast.6.me_ref, bf16[2896,128]{1,0:T(8,128)(2,1)} %copy-done.1, bf16[2896,128]{1,0:T(8,128)(2,1)} %copy-done.9, bf16[1440,2880]{1,0:T(8,128)(2,1)} %bitcast.17, bf16[1440,2880]{1,0:T(8,128)(2,1)} %collective-permute-done.8.gu1, ...), custom_call_target="tpu_custom_call" | custom-call | flops 6370099200 | bytes 24883200 | tf_op jit(solution)/shard_map/pallas_call | solution.py:300
  134.6 1.5 collective-permute-start.24
  136.3 2.1 %collective-permute-start.21 = (bf16[2880,128]{1,0:T(8,128)(2,1)S(1)}, bf16[2880,128]{1,0:T(8,128)(2,1)S(1)}, u32[]{:S(2)}, u32[]{:S(2)}) collective-permute-start(bf16[2880,128]{1,0:T(8,128)(2,1)S(1)} %add_convert_fusion.3), channel_id=1, source_target_pairs={{0,8},{1,9},{2,10},{3,11},{4,0},{5,1},{6,2},{7,3},{8,12},{9,13},{1... | collective-permute-start | bytes 2211848 | tf_op jit(solution)/shard_map/ppermute | solution.py:492
  138.4 0.2 add_convert_fusion.1
  138.7 12.8 %collective-permute-done.24 = bf16[2880,128]{1,0:T(8,128)(2,1)S(1)} collective-permute-done((bf16[2880,128]{1,0:T(8,128)(2,1)}, bf16[2880,128]{1,0:T(8,128)(2,1)S(1)}, u32[]{:S(2)}, u32[]{:S(2)}) %collective-permute-start.24) | collective-permute-done | bytes 737312 | tf_op jit(solution)/shard_map/ppermute | solution.py:482
  151.6 1.4 collective-permute-start.27
  153.1 1.3 collective-permute-start.26
  154.4 6.3 %collective-permute-start.25 = (bf16[2880,128]{1,0:T(8,128)(2,1)S(1)}, bf16[2880,128]{1,0:T(8,128)(2,1)S(1)}, u32[]{:S(2)}, u32[]{:S(2)}) collective-permute-start(bf16[2880,128]{1,0:T(8,128)(2,1)S(1)} %add_convert_fusion.2), channel_id=1, source_target_pairs={{0,12},{1,13},{2,14},{3,15},{8,0},{9,1},{10,2},{11,3},{16,28},{17,... | collective-permute-start | bytes 2211848 | tf_op jit(solution)/shard_map/ppermute | solution.py:499
  160.8 4.6 %collective-permute-done.27 = bf16[2880,128]{1,0:T(8,128)(2,1)S(1)} collective-permute-done((bf16[2880,128]{1,0:T(8,128)(2,1)S(1)}, bf16[2880,128]{1,0:T(8,128)(2,1)S(1)}, u32[]{:S(2)}, u32[]{:S(2)}) %collective-permute-start.27) | collective-permute-done | bytes 737312 | tf_op jit(solution)/shard_map/ppermute | solution.py:496
  165.4 3.6 %collective-permute-done.26 = bf16[2880,128]{1,0:T(8,128)(2,1)S(1)} collective-permute-done((bf16[2880,128]{1,0:T(8,128)(2,1)S(1)}, bf16[2880,128]{1,0:T(8,128)(2,1)S(1)}, u32[]{:S(2)}, u32[]{:S(2)}) %collective-permute-start.26) | collective-permute-done | bytes 737312 | tf_op jit(solution)/shard_map/ppermute | solution.py:499
  169.0 15.7 %collective-permute-done.25 = bf16[2880,128]{1,0:T(8,128)(2,1)S(1)} collective-permute-done((bf16[2880,128]{1,0:T(8,128)(2,1)S(1)}, bf16[2880,128]{1,0:T(8,128)(2,1)S(1)}, u32[]{:S(2)}, u32[]{:S(2)}) %collective-permute-start.25) | collective-permute-done | bytes 737312 | tf_op jit(solution)/shard_map/ppermute | solution.py:499
  184.7 1.6 fusion
  (51 shorter events, 0.7 us)
Async XLA Ops:
  0.0 19.4 %copy-start.11 = (bf16[128,2048]{1,0:T(8,128)(2,1)S(1)}, bf16[128,2048]{1,0:T(8,128)(2,1)}, u32[]{:S(2)}) copy-start(bf16[128,2048]{1,0:T(8,128)(2,1)} %param.11) | copy-start | bytes 1572868
  1.8 5.4 %collective-permute-start.2 = (bf16[16,512]{1,0:T(8,128)(2,1)}, bf16[16,512]{1,0:T(8,128)(2,1)S(1)}, u32[]{:S(2)}, u32[]{:S(2)}) collective-permute-start(bf16[16,512]{1,0:T(8,128)(2,1)} %get-tuple-element.39), channel_id=1, source_target_pairs={{0,3},{1,2},{2,1},{3,0},{4,7},{5,6},{6,5},{7,4},{8,11},{9,10},{10,... | collective-permute-start | bytes 49160 | tf_op jit(solution)/shard_map/ppermute | solution.py:77
  4.2 3.9 %collective-permute-start.1 = (bf16[16,512]{1,0:T(8,128)(2,1)}, bf16[16,512]{1,0:T(8,128)(2,1)S(1)}, u32[]{:S(2)}, u32[]{:S(2)}) collective-permute-start(bf16[16,512]{1,0:T(8,128)(2,1)} %get-tuple-element.39), channel_id=1, source_target_pairs={{0,2},{1,3},{2,0},{3,1},{4,6},{5,7},{6,4},{7,5},{8,10},{9,11},{10,... | collective-permute-start | bytes 49160 | tf_op jit(solution)/shard_map/ppermute | solution.py:77
  4.8 3.4 %collective-permute-start = (bf16[16,512]{1,0:T(8,128)(2,1)}, bf16[16,512]{1,0:T(8,128)(2,1)S(1)}, u32[]{:S(2)}, u32[]{:S(2)}) collective-permute-start(bf16[16,512]{1,0:T(8,128)(2,1)} %get-tuple-element.39), channel_id=1, source_target_pairs={{0,1},{1,0},{2,3},{3,2},{4,5},{5,4},{6,7},{7,6},{8,9},{9,8},{10,11... | collective-permute-start | bytes 49160 | tf_op jit(solution)/shard_map/ppermute | solution.py:77
  4.9 4.0 %collective-permute-start.3 = (bf16[128,512]{1,0:T(8,128)(2,1)}, bf16[128,512]{1,0:T(8,128)(2,1)S(1)}, u32[]{:S(2)}, u32[]{:S(2)}) collective-permute-start(bf16[128,512]{1,0:T(8,128)(2,1)} %get-tuple-element.40.local), channel_id=1, source_target_pairs={{0,1},{1,2},{2,3},{3,4},{4,5},{5,6},{6,7},{7,8},{8,9},{9,10},{10,1... | collective-permute-start | bytes 393224 | tf_op jit(solution)/shard_map/ppermute | solution.py:400
  8.9 13.0 %copy-start.12 = (bf16[128,512]{1,0:T(8,128)(2,1)}, bf16[128,512]{1,0:T(8,128)(2,1)S(1)}, u32[]{:S(2)}) copy-start(bf16[128,512]{1,0:T(8,128)(2,1)S(1)} %collective-permute-done.3.halo) | copy-start | bytes 393220
  8.9 48.7 %collective-permute-start.8 = (bf16[1440,2880]{1,0:T(8,128)(2,1)}, bf16[1440,2880]{1,0:T(8,128)(2,1)}, u32[]{:S(2)}, u32[]{:S(2)}) collective-permute-start(bf16[1440,2880]{1,0:T(8,128)(2,1)} %bitcast.13), channel_id=1, source_target_pairs={{0,1},{1,0},{2,3},{3,2},{4,5},{5,4},{6,7},{7,6},{8,9},{9,8},{10,11... | collective-permute-start | bytes 24883208 | tf_op jit(solution)/shard_map/ppermute | solution.py:408
  10.9 46.7 %collective-permute-start.9 = (bf16[720,2880]{1,0:T(8,128)(2,1)}, bf16[720,2880]{1,0:T(8,128)(2,1)}, u32[]{:S(2)}, u32[]{:S(2)}) collective-permute-start(bf16[720,2880]{1,0:T(8,128)(2,1)} %bitcast.18), channel_id=1, source_target_pairs={{0,1},{1,0},{2,3},{3,2},{4,5},{5,4},{6,7},{7,6},{8,9},{9,8},{10,11... | collective-permute-start | bytes 12441608 | tf_op jit(solution)/shard_map/ppermute | solution.py:409
  10.9 9.5 %collective-permute-start.6 = (bf16[16,512]{1,0:T(8,128)(2,1)S(1)}, bf16[16,512]{1,0:T(8,128)(2,1)S(1)}, u32[]{:S(2)}, u32[]{:S(2)}) collective-permute-start(bf16[16,512]{1,0:T(8,128)(2,1)S(1)} %add_add_fusion.1), channel_id=1, source_target_pairs={{0,12},{1,13},{2,14},{3,15},{4,8},{5,9},{6,10},{7,11},{8,4},{9,5},... | collective-permute-start | bytes 49160 | tf_op jit(solution)/shard_map/ppermute | solution.py:77
  16.6 4.6 %collective-permute-start.5 = (bf16[16,512]{1,0:T(8,128)(2,1)S(1)}, bf16[16,512]{1,0:T(8,128)(2,1)S(1)}, u32[]{:S(2)}, u32[]{:S(2)}) collective-permute-start(bf16[16,512]{1,0:T(8,128)(2,1)S(1)} %add_add_fusion.1), channel_id=1, source_target_pairs={{0,8},{1,9},{2,10},{3,11},{4,12},{5,13},{6,14},{7,15},{8,0},{9,1},... | collective-permute-start | bytes 49160 | tf_op jit(solution)/shard_map/ppermute | solution.py:77
  16.6 4.6 %collective-permute-start.4 = (bf16[16,512]{1,0:T(8,128)(2,1)S(1)}, bf16[16,512]{1,0:T(8,128)(2,1)S(1)}, u32[]{:S(2)}, u32[]{:S(2)}) collective-permute-start(bf16[16,512]{1,0:T(8,128)(2,1)S(1)} %add_add_fusion.1), channel_id=1, source_target_pairs={{0,4},{1,5},{2,6},{3,7},{4,0},{5,1},{6,2},{7,3},{8,12},{9,13},{10,... | collective-permute-start | bytes 49160 | tf_op jit(solution)/shard_map/ppermute | solution.py:77
  31.5 18.3 %collective-permute-start.10 = (bf16[2896,128]{1,0:T(8,128)(2,1)}, bf16[2896,128]{1,0:T(8,128)(2,1)S(1)}, u32[]{:S(2)}, u32[]{:S(2)}) collective-permute-start(bf16[2896,128]{1,0:T(8,128)(2,1)} %get-tuple-element.46.x_ref), channel_id=1, source_target_pairs={{0,4},{1,5},{2,6},{3,7},{4,8},{5,9},{6,10},{7,11},{8,12},{9,13},{1... | collective-permute-start | bytes 2224136 | tf_op jit(solution)/shard_map/ppermute | solution.py:359
  34.1 19.8 %collective-permute-start.11 = (bf16[2896,128]{1,0:T(8,128)(2,1)}, bf16[2896,128]{1,0:T(8,128)(2,1)S(1)}, u32[]{:S(2)}, u32[]{:S(2)}) collective-permute-start(bf16[2896,128]{1,0:T(8,128)(2,1)} %get-tuple-element.46.x_ref), channel_id=1, source_target_pairs={{4,0},{5,1},{6,2},{7,3},{8,4},{9,5},{10,6},{11,7},{12,8},{13,9},{1... | collective-permute-start | bytes 2224136 | tf_op jit(solution)/shard_map/ppermute | solution.py:360
  35.4 18.6 %collective-permute-start.7 = (bf16[2896,128]{1,0:T(8,128)(2,1)}, bf16[2896,128]{1,0:T(8,128)(2,1)S(1)}, u32[]{:S(2)}, u32[]{:S(2)}) collective-permute-start(bf16[2896,128]{1,0:T(8,128)(2,1)} %get-tuple-element.46.x_ref), channel_id=1, source_target_pairs={{0,2},{1,3},{2,0},{3,1},{4,6},{5,7},{6,4},{7,5},{8,10},{9,11},{10,... | collective-permute-start | bytes 2224136 | tf_op jit(solution)/shard_map/ppermute | solution.py:434
  54.0 17.8 %copy-start = (bf16[2896,128]{1,0:T(8,128)(2,1)}, bf16[2896,128]{1,0:T(8,128)(2,1)S(1)}, u32[]{:S(2)}) copy-start(bf16[2896,128]{1,0:T(8,128)(2,1)S(1)} %broadcast_select_fusion.2.x_ref) | copy-start | bytes 2224132
  54.0 3.5 %copy-start.7 = (bf16[2896,128]{1,0:T(8,128)(2,1)}, bf16[2896,128]{1,0:T(8,128)(2,1)S(1)}, u32[]{:S(2)}) copy-start(bf16[2896,128]{1,0:T(8,128)(2,1)S(1)} %collective-permute-done.7.y_ref) | copy-start | bytes 2224132
  54.0 17.8 %collective-permute-start.12 = (bf16[2896,128]{1,0:T(8,128)(2,1)S(1)}, bf16[2896,128]{1,0:T(8,128)(2,1)}, u32[]{:S(2)}, u32[]{:S(2)}) collective-permute-start(bf16[2896,128]{1,0:T(8,128)(2,1)S(1)} %broadcast_select_fusion.2.x_ref), channel_id=1, source_target_pairs={{0,2},{1,3},{2,0},{3,1},{4,6},{5,7},{6,4},{7,5},{8,10},{9,11},{10,... | collective-permute-start | bytes 2224136 | tf_op jit(solution)/shard_map/ppermute | solution.py:440
  54.7 17.1 %collective-permute-start.13 = (bf16[2896,128]{1,0:T(8,128)(2,1)S(1)}, bf16[2896,128]{1,0:T(8,128)(2,1)}, u32[]{:S(2)}, u32[]{:S(2)}) collective-permute-start(bf16[2896,128]{1,0:T(8,128)(2,1)S(1)} %collective-permute-done.10), channel_id=1, source_target_pairs={{4,8},{5,9},{6,10},{7,11},{8,12},{9,13},{10,14},{11,15},{20,24},{2... | collective-permute-start | bytes 2224136 | tf_op jit(solution)/shard_map/ppermute | solution.py:359
  56.2 20.5 %collective-permute-start.14 = (bf16[2896,128]{1,0:T(8,128)(2,1)S(1)}, bf16[2896,128]{1,0:T(8,128)(2,1)}, u32[]{:S(2)}, u32[]{:S(2)}) collective-permute-start(bf16[2896,128]{1,0:T(8,128)(2,1)S(1)} %collective-permute-done.11), channel_id=1, source_target_pairs={{4,0},{5,1},{6,2},{7,3},{8,4},{9,5},{10,6},{11,7},{20,16},{21,17},... | collective-permute-start | bytes 2224136 | tf_op jit(solution)/shard_map/ppermute | solution.py:360
  78.2 16.7 %copy-start.2 = (bf16[2896,128]{1,0:T(8,128)(2,1)}, bf16[2896,128]{1,0:T(8,128)(2,1)S(1)}, u32[]{:S(2)}) copy-start(bf16[2896,128]{1,0:T(8,128)(2,1)S(1)} %get-tuple-element.56.x_ref) | copy-start | bytes 2224132
  78.2 16.7 %collective-permute-start.15 = (bf16[2896,128]{1,0:T(8,128)(2,1)S(1)}, bf16[2896,128]{1,0:T(8,128)(2,1)S(1)}, u32[]{:S(2)}, u32[]{:S(2)}) collective-permute-start(bf16[2896,128]{1,0:T(8,128)(2,1)S(1)} %get-tuple-element.56.x_ref), channel_id=1, source_target_pairs={{0,2},{1,3},{2,0},{3,1},{4,6},{5,7},{6,4},{7,5},{8,10},{9,11},{10,... | collective-permute-start | bytes 2224136 | tf_op jit(solution)/shard_map/ppermute | solution.py:440
  79.7 16.8 %collective-permute-start.16 = (bf16[2896,128]{1,0:T(8,128)(2,1)S(1)}, bf16[2896,128]{1,0:T(8,128)(2,1)S(1)}, u32[]{:S(2)}, u32[]{:S(2)}) collective-permute-start(bf16[2896,128]{1,0:T(8,128)(2,1)S(1)} %get-tuple-element.57), channel_id=1, source_target_pairs={{8,12},{9,13},{10,14},{11,15},{4,0},{5,1},{6,2},{7,3},{24,28},{25,... | collective-permute-start | bytes 2224136 | tf_op jit(solution)/shard_map/ppermute | solution.py:356
  94.9 10.2 %copy-start.8 = (bf16[2896,128]{1,0:T(8,128)(2,1)}, bf16[2896,128]{1,0:T(8,128)(2,1)S(1)}, u32[]{:S(2)}) copy-start(bf16[2896,128]{1,0:T(8,128)(2,1)S(1)} %collective-permute-done.15.y_ref) | copy-start | bytes 2224132
  96.6 22.5 %copy-start.1 = (bf16[2896,128]{1,0:T(8,128)(2,1)}, bf16[2896,128]{1,0:T(8,128)(2,1)S(1)}, u32[]{:S(2)}) copy-start(bf16[2896,128]{1,0:T(8,128)(2,1)S(1)} %broadcast_select_fusion.x_ref) | copy-start | bytes 2224132
  96.6 22.5 %collective-permute-start.19 = (bf16[2896,128]{1,0:T(8,128)(2,1)S(1)}, bf16[2896,128]{1,0:T(8,128)(2,1)S(1)}, u32[]{:S(2)}, u32[]{:S(2)}) collective-permute-start(bf16[2896,128]{1,0:T(8,128)(2,1)S(1)} %broadcast_select_fusion.x_ref), channel_id=1, source_target_pairs={{0,2},{1,3},{2,0},{3,1},{4,6},{5,7},{6,4},{7,5},{8,10},{9,11},{10,... | collective-permute-start | bytes 2224136 | tf_op jit(solution)/shard_map/ppermute | solution.py:440
  97.3 21.8 %collective-permute-start.17 = (bf16[2880,128]{1,0:T(8,128)(2,1)}, bf16[2880,128]{1,0:T(8,128)(2,1)S(1)}, u32[]{:S(2)}, u32[]{:S(2)}) collective-permute-start(bf16[2880,128]{1,0:T(8,128)(2,1)} %get-tuple-element.58), channel_id=1, source_target_pairs={{0,4},{1,5},{2,6},{3,7},{4,8},{5,9},{6,10},{7,11},{16,20},{17,21},... | collective-permute-start | bytes 2211848 | tf_op jit(solution)/shard_map/ppermute | solution.py:463
  100.3 18.8 %collective-permute-start.18 = (bf16[2880,128]{1,0:T(8,128)(2,1)}, bf16[2880,128]{1,0:T(8,128)(2,1)S(1)}, u32[]{:S(2)}, u32[]{:S(2)}) collective-permute-start(bf16[2880,128]{1,0:T(8,128)(2,1)} %get-tuple-element.58), channel_id=1, source_target_pairs={{8,4},{9,5},{10,6},{11,7},{12,8},{13,9},{14,10},{15,11},{24,20},{2... | collective-permute-start | bytes 2211848 | tf_op jit(solution)/shard_map/ppermute | solution.py:463
  101.0 33.6 %collective-permute-start.23 = (bf16[2880,128]{1,0:T(8,128)(2,1)}, bf16[2880,128]{1,0:T(8,128)(2,1)S(1)}, u32[]{:S(2)}, u32[]{:S(2)}) collective-permute-start(bf16[2880,128]{1,0:T(8,128)(2,1)} %get-tuple-element.67), channel_id=1, source_target_pairs={{8,4},{9,5},{10,6},{11,7},{12,8},{13,9},{14,10},{15,11},{24,20},{2... | collective-permute-start | bytes 2211848 | tf_op jit(solution)/shard_map/ppermute | solution.py:463
  101.8 32.8 %collective-permute-start.22 = (bf16[2880,128]{1,0:T(8,128)(2,1)}, bf16[2880,128]{1,0:T(8,128)(2,1)S(1)}, u32[]{:S(2)}, u32[]{:S(2)}) collective-permute-start(bf16[2880,128]{1,0:T(8,128)(2,1)} %get-tuple-element.67), channel_id=1, source_target_pairs={{0,4},{1,5},{2,6},{3,7},{4,8},{5,9},{6,10},{7,11},{16,20},{17,21},... | collective-permute-start | bytes 2211848 | tf_op jit(solution)/shard_map/ppermute | solution.py:463
  119.1 1.5 copy-start.9
  119.2 17.0 %copy-start.6 = (f32[2880,128]{1,0:T(8,128)S(1)}, f32[2880,128]{1,0:T(8,128)}, u32[]{:S(2)}) copy-start(f32[2880,128]{1,0:T(8,128)} %get-tuple-element.59) | copy-start | bytes 4423684
  119.2 15.4 %collective-permute-start.20 = (bf16[2880,128]{1,0:T(8,128)(2,1)}, bf16[2880,128]{1,0:T(8,128)(2,1)S(1)}, u32[]{:S(2)}, u32[]{:S(2)}) collective-permute-start(bf16[2880,128]{1,0:T(8,128)(2,1)} %get-tuple-element.63), channel_id=1, source_target_pairs={{0,2},{1,3},{2,0},{3,1},{4,6},{5,7},{6,4},{7,5},{8,10},{9,11},{10,... | collective-permute-start | bytes 2211848 | tf_op jit(solution)/shard_map/ppermute | solution.py:482
  134.6 16.9 %collective-permute-start.24 = (bf16[2880,128]{1,0:T(8,128)(2,1)}, bf16[2880,128]{1,0:T(8,128)(2,1)S(1)}, u32[]{:S(2)}, u32[]{:S(2)}) collective-permute-start(bf16[2880,128]{1,0:T(8,128)(2,1)} %get-tuple-element.70), channel_id=1, source_target_pairs={{0,2},{1,3},{2,0},{3,1},{4,6},{5,7},{6,4},{7,5},{8,10},{9,11},{10,... | collective-permute-start | bytes 2211848 | tf_op jit(solution)/shard_map/ppermute | solution.py:482
  136.1 2.3 %copy-start.4 = (f32[2880,128]{1,0:T(8,128)S(1)}, f32[2880,128]{1,0:T(8,128)}, u32[]{:S(2)}) copy-start(f32[2880,128]{1,0:T(8,128)} %get-tuple-element.71) | copy-start | bytes 4423684
  136.3 24.5 %collective-permute-start.21 = (bf16[2880,128]{1,0:T(8,128)(2,1)S(1)}, bf16[2880,128]{1,0:T(8,128)(2,1)S(1)}, u32[]{:S(2)}, u32[]{:S(2)}) collective-permute-start(bf16[2880,128]{1,0:T(8,128)(2,1)S(1)} %add_convert_fusion.3), channel_id=1, source_target_pairs={{0,8},{1,9},{2,10},{3,11},{4,0},{5,1},{6,2},{7,3},{8,12},{9,13},{1... | collective-permute-start | bytes 2211848 | tf_op jit(solution)/shard_map/ppermute | solution.py:492
  138.4 14.6 %copy-start.5 = (f32[2880,128]{1,0:T(8,128)S(1)}, f32[2880,128]{1,0:T(8,128)}, u32[]{:S(2)}) copy-start(f32[2880,128]{1,0:T(8,128)} %get-tuple-element.64) | copy-start | bytes 4423684
  138.7 46.0 %copy-start.3 = (f32[2880,128]{1,0:T(8,128)S(1)}, f32[2880,128]{1,0:T(8,128)}, u32[]{:S(2)}) copy-start(f32[2880,128]{1,0:T(8,128)} %get-tuple-element.49) | copy-start | bytes 4423684
  138.7 46.0 %copy-start.10 = (bf16[2880,128]{1,0:T(8,128)(2,1)S(1)}, bf16[2880,128]{1,0:T(8,128)(2,1)}, u32[]{:S(2)}) copy-start(bf16[2880,128]{1,0:T(8,128)(2,1)} %get-tuple-element.45) | copy-start | bytes 2211844
  151.6 13.9 %collective-permute-start.27 = (bf16[2880,128]{1,0:T(8,128)(2,1)S(1)}, bf16[2880,128]{1,0:T(8,128)(2,1)S(1)}, u32[]{:S(2)}, u32[]{:S(2)}) collective-permute-start(bf16[2880,128]{1,0:T(8,128)(2,1)S(1)} %add_convert_fusion.1), channel_id=1, source_target_pairs={{0,2},{1,3},{2,0},{3,1},{4,6},{5,7},{6,4},{7,5},{8,10},{9,11},{10,... | collective-permute-start | bytes 2211848 | tf_op jit(solution)/shard_map/ppermute | solution.py:496
  153.1 15.9 %collective-permute-start.26 = (bf16[2880,128]{1,0:T(8,128)(2,1)S(1)}, bf16[2880,128]{1,0:T(8,128)(2,1)S(1)}, u32[]{:S(2)}, u32[]{:S(2)}) collective-permute-start(bf16[2880,128]{1,0:T(8,128)(2,1)S(1)} %add_convert_fusion.2), channel_id=1, source_target_pairs={{4,12},{5,13},{6,14},{7,15},{12,0},{13,1},{14,2},{15,3},{20,28},{2... | collective-permute-start | bytes 2211848 | tf_op jit(solution)/shard_map/ppermute | solution.py:499
  154.4 30.3 %collective-permute-start.25 = (bf16[2880,128]{1,0:T(8,128)(2,1)S(1)}, bf16[2880,128]{1,0:T(8,128)(2,1)S(1)}, u32[]{:S(2)}, u32[]{:S(2)}) collective-permute-start(bf16[2880,128]{1,0:T(8,128)(2,1)S(1)} %add_convert_fusion.2), channel_id=1, source_target_pairs={{0,12},{1,13},{2,14},{3,15},{8,0},{9,1},{10,2},{11,3},{16,28},{17,... | collective-permute-start | bytes 2211848 | tf_op jit(solution)/shard_map/ppermute | solution.py:499

commit v7 on v6

--- a/solution.py
+++ b/solution.py
@@ -495,7 +495,7 @@
         ready = (returned, *slow)
     crossing = lax.ppermute(after(cross_sum.astype(half), *ready), "seq", across)
     k, both = pending
-    for moves in rounds([(p, o[k - 1]) for p, o in enumerate(order)]):
+    for moves in reversed(rounds([(p, o[k - 1]) for p, o in enumerate(order)])):
         back = lax.ppermute(both, "seq", line_pairs(moves))
         column_sum = column_sum + back.astype(jnp.float32)
     return (column_sum + crossing.astype(jnp.float32)).astype(half).T

time: 187 us -> 187 us (level)
  transfers between devices with their start and end apart: 28 -> 28, of which waited for: 10 -> 9; matrix products, arithmetic and copies ran while one was open for 3% -> 3% of each run, Pallas kernels for 35% -> 35%
where the time goes in v7:
time: 187 us; the launch traced here: 186 us
  Pallas kernels  67.3 us (36%)
  waiting for transfers between devices  64.7 us (35%)
  starting transfers between devices  45.6 us (24%)
  other arithmetic  5.1 us (3%)
  local copies, waits for them, and re-layouts  3.3 us (2%)
    pallas_call x4, Pallas kernels, expert_rows(): pl.pallas_call(functools.partial(expert_kernel, experts), out_shape=[jax....  55.8 us
    ppermute x3, waiting for transfers between devices, on_device(): back = lax.ppermute(both, 'seq', line_pairs(moves))  19.3 us
    ppermute x2, waiting for transfers between devices, next_blocks(): lax.ppermute(below, 'seq', line_pairs(up))  13.7 us
    ppermute x2, waiting for transfers between devices, on_device(): returned = lax.ppermute(theirs, 'seq', across)  12.8 us
    pallas_call x1, Pallas kernels, attended_rows(): pl.pallas_call(functools.partial(attention_kernel, experts), out_shape=(j...  9.7 us
    ppermute x6, starting transfers between devices, summed(): lax.ppermute(block, axis, [(i, i ^ step * m) for i in range(shards)])  9.36 us
    ppermute x2, waiting for transfers between devices, next_blocks(): lax.ppermute(above, 'seq', line_pairs(down))  9.02 us
    ppermute x3, starting transfers between devices, on_device(): back = lax.ppermute(both, 'seq', line_pairs(moves))  7.98 us
  transfers between devices with their start and end apart: 28, of which 9 were waited for; matrix products, arithmetic and copies ran while one was open for 3% of the time, Pallas kernels for 35%

profile of v7, /device:TPU:0, one launch (start us, length us, event | category | flops | bytes accessed | tf_op | source)
XLA Modules:
  0.0 186.3 jit_solution(16335002351413929273)
XLA Ops:
  0.0 1.8 shard_map.109
  1.8 2.4 %collective-permute-start.2 = (bf16[16,512]{1,0:T(8,128)(2,1)}, bf16[16,512]{1,0:T(8,128)(2,1)S(1)}, u32[]{:S(2)}, u32[]{:S(2)}) collective-permute-start(bf16[16,512]{1,0:T(8,128)(2,1)} %get-tuple-element.39), channel_id=1, source_target_pairs={{0,3},{1,2},{2,1},{3,0},{4,7},{5,6},{6,5},{7,4},{8,11},{9,10},{10,... | collective-permute-start | bytes 49160 | tf_op jit(solution)/shard_map/ppermute | solution.py:77
  4.2 0.6 collective-permute-start.1
  4.9 2.3 %collective-permute-start.3 = (bf16[128,512]{1,0:T(8,128)(2,1)}, bf16[128,512]{1,0:T(8,128)(2,1)S(1)}, u32[]{:S(2)}, u32[]{:S(2)}) collective-permute-start(bf16[128,512]{1,0:T(8,128)(2,1)} %get-tuple-element.40.local), channel_id=1, source_target_pairs={{0,1},{1,2},{2,3},{3,4},{4,5},{5,6},{6,7},{7,8},{8,9},{9,10},{10,1... | collective-permute-start | bytes 393224 | tf_op jit(solution)/shard_map/ppermute | solution.py:400
  7.2 0.9 collective-permute-done.1
  8.1 0.7 add_add_fusion.1
  8.9 2.0 %collective-permute-start.8 = (bf16[1440,2880]{1,0:T(8,128)(2,1)}, bf16[1440,2880]{1,0:T(8,128)(2,1)}, u32[]{:S(2)}, u32[]{:S(2)}) collective-permute-start(bf16[1440,2880]{1,0:T(8,128)(2,1)} %bitcast.13), channel_id=1, source_target_pairs={{0,1},{1,0},{2,3},{3,2},{4,5},{5,4},{6,7},{7,6},{8,9},{9,8},{10,11... | collective-permute-start | bytes 24883208 | tf_op jit(solution)/shard_map/ppermute | solution.py:408
  10.9 5.7 %collective-permute-start.6 = (bf16[16,512]{1,0:T(8,128)(2,1)S(1)}, bf16[16,512]{1,0:T(8,128)(2,1)S(1)}, u32[]{:S(2)}, u32[]{:S(2)}) collective-permute-start(bf16[16,512]{1,0:T(8,128)(2,1)S(1)} %add_add_fusion.1), channel_id=1, source_target_pairs={{0,12},{1,13},{2,14},{3,15},{4,8},{5,9},{6,10},{7,11},{8,4},{9,5},... | collective-permute-start | bytes 49160 | tf_op jit(solution)/shard_map/ppermute | solution.py:77
  16.6 0.6 collective-permute-start.4
  17.1 2.2 %broadcast_in_dim.4.gain = f32[2880,1]{1,0:T(8,128)} reshape(f32[2880]{0:T(1024)} %param.17) | data formatting | bytes 23040 | tf_op jit(solution)/shard_map/broadcast_in_dim | solution.py:419
  19.4 1.0 copy.13
  20.4 0.8 collective-permute-done.5
  21.2 0.6 add_add_fusion.sinks
  21.8 9.7 %shard_map.110 = (bf16[2880,128]{1,0:T(8,128)(2,1)}, bf16[2896,128]{1,0:T(8,128)(2,1)}) custom-call(bf16[2048,128]{1,0:T(8,128)(2,1)} %bitcast.24, bf16[128,512]{1,0:T(8,128)(2,1)} %copy-done.12, bf16[128,512]{1,0:T(8,128)(2,1)} %get-tuple-element.40.local, bf16[16,512]{1,0:T(8,128)(2,1)} %add_add_fusion.sinks, f32[272,128]{1,0:T(8,128)} %get-tuple-element.44.bias, ...), custom_call_target="tpu_custom_call" | custom-call | flops 1509949440 | bytes 11796480 | tf_op jit(solution)/shard_map/pallas_call | solution.py:209
  31.5 2.6 %collective-permute-start.10 = (bf16[2896,128]{1,0:T(8,128)(2,1)}, bf16[2896,128]{1,0:T(8,128)(2,1)S(1)}, u32[]{:S(2)}, u32[]{:S(2)}) collective-permute-start(bf16[2896,128]{1,0:T(8,128)(2,1)} %get-tuple-element.46.x_ref), channel_id=1, source_target_pairs={{0,4},{1,5},{2,6},{3,7},{4,8},{5,9},{6,10},{7,11},{8,12},{9,13},{1... | collective-permute-start | bytes 2224136 | tf_op jit(solution)/shard_map/ppermute | solution.py:359
  34.1 1.3 collective-permute-start.11
  35.4 0.7 collective-permute-start.7
  36.1 13.7 %collective-permute-done.10 = bf16[2896,128]{1,0:T(8,128)(2,1)S(1)} collective-permute-done((bf16[2896,128]{1,0:T(8,128)(2,1)}, bf16[2896,128]{1,0:T(8,128)(2,1)S(1)}, u32[]{:S(2)}, u32[]{:S(2)}) %collective-permute-start.10) | collective-permute-done | bytes 741408 | tf_op jit(solution)/shard_map/ppermute | solution.py:359
  49.8 4.1 %collective-permute-done.11 = bf16[2896,128]{1,0:T(8,128)(2,1)S(1)} collective-permute-done((bf16[2896,128]{1,0:T(8,128)(2,1)}, bf16[2896,128]{1,0:T(8,128)(2,1)S(1)}, u32[]{:S(2)}, u32[]{:S(2)}) %collective-permute-start.11) | collective-permute-done | bytes 741408 | tf_op jit(solution)/shard_map/ppermute | solution.py:360
  54.0 0.7 collective-permute-start.12
  54.7 1.5 collective-permute-start.13
  56.2 1.3 collective-permute-start.14
  57.6 14.2 %shard_map.111 = (f32[2880,128]{1,0:T(8,128)}, f32[2880,128]{1,0:T(8,128)}) custom-call(s32[1]{0:T(128)} %bitcast.6.me_ref, bf16[2896,128]{1,0:T(8,128)(2,1)} %get-tuple-element.46.x_ref, bf16[2896,128]{1,0:T(8,128)(2,1)} %copy-done.7, bf16[1440,2880]{1,0:T(8,128)(2,1)} %bitcast.14, bf16[1440,2880]{1,0:T(8,128)(2,1)} %collective-permute-done.8.gu1, ...), custom_call_target="tpu_custom_call" | custom-call | flops 6370099200 | bytes 24883200 | tf_op jit(solution)/shard_map/pallas_call | solution.py:300
  71.8 5.0 %collective-permute-done.14 = bf16[2896,128]{1,0:T(8,128)(2,1)} collective-permute-done((bf16[2896,128]{1,0:T(8,128)(2,1)S(1)}, bf16[2896,128]{1,0:T(8,128)(2,1)}, u32[]{:S(2)}, u32[]{:S(2)}) %collective-permute-start.14) | collective-permute-done | bytes 741408 | tf_op jit(solution)/shard_map/ppermute | solution.py:360
  76.8 1.4 select_select_fusion
  78.2 1.5 collective-permute-start.15
  79.7 1.5 collective-permute-start.16
  81.1 13.7 %shard_map.112 = (bf16[2880,128]{1,0:T(8,128)(2,1)}, bf16[2880,128]{1,0:T(8,128)(2,1)}) custom-call(s32[1]{0:T(128)} %bitcast.6.me_ref, bf16[2896,128]{1,0:T(8,128)(2,1)} %copy-done, bf16[2896,128]{1,0:T(8,128)(2,1)} %collective-permute-done.12.y_ref, bf16[1440,2880]{1,0:T(8,128)(2,1)} %bitcast.15, bf16[1440,2880]{1,0:T(8,128)(2,1)} %collective-permute-done.8.gu1, ...), custom_call_target="tpu_custom_call" | custom-call | flops 6370099200 | bytes 24883200 | tf_op jit(solution)/shard_map/pallas_call | solution.py:300
  94.9 1.6 collective-permute-done.16
  96.6 0.7 collective-permute-start.19
  97.3 3.0 %collective-permute-start.17 = (bf16[2880,128]{1,0:T(8,128)(2,1)}, bf16[2880,128]{1,0:T(8,128)(2,1)S(1)}, u32[]{:S(2)}, u32[]{:S(2)}) collective-permute-start(bf16[2880,128]{1,0:T(8,128)(2,1)} %get-tuple-element.58), channel_id=1, source_target_pairs={{0,4},{1,5},{2,6},{3,7},{4,8},{5,9},{6,10},{7,11},{16,20},{17,21},... | collective-permute-start | bytes 2211848 | tf_op jit(solution)/shard_map/ppermute | solution.py:463
  100.3 0.7 collective-permute-start.18
  101.0 0.7 collective-permute-start.23
  101.8 3.4 %collective-permute-start.22 = (bf16[2880,128]{1,0:T(8,128)(2,1)}, bf16[2880,128]{1,0:T(8,128)(2,1)S(1)}, u32[]{:S(2)}, u32[]{:S(2)}) collective-permute-start(bf16[2880,128]{1,0:T(8,128)(2,1)} %get-tuple-element.67), channel_id=1, source_target_pairs={{0,4},{1,5},{2,6},{3,7},{4,8},{5,9},{6,10},{7,11},{16,20},{17,21},... | collective-permute-start | bytes 2211848 | tf_op jit(solution)/shard_map/ppermute | solution.py:463
  105.1 14.0 %shard_map.113 = (f32[2880,128]{1,0:T(8,128)}, bf16[2880,128]{1,0:T(8,128)(2,1)}) custom-call(s32[1]{0:T(128)} %bitcast.6.me_ref, bf16[2896,128]{1,0:T(8,128)(2,1)} %copy-done.2, bf16[2896,128]{1,0:T(8,128)(2,1)} %copy-done.8, bf16[1440,2880]{1,0:T(8,128)(2,1)} %bitcast.16, bf16[1440,2880]{1,0:T(8,128)(2,1)} %collective-permute-done.8.gu1, ...), custom_call_target="tpu_custom_call" | custom-call | flops 6370099200 | bytes 24883200 | tf_op jit(solution)/shard_map/pallas_call | solution.py:300
  119.2 1.5 collective-permute-start.20
  120.6 13.9 %shard_map.114 = (f32[2880,128]{1,0:T(8,128)}, bf16[2880,128]{1,0:T(8,128)(2,1)}) custom-call(s32[1]{0:T(128)} %bitcast.6.me_ref, bf16[2896,128]{1,0:T(8,128)(2,1)} %copy-done.1, bf16[2896,128]{1,0:T(8,128)(2,1)} %copy-done.9, bf16[1440,2880]{1,0:T(8,128)(2,1)} %bitcast.17, bf16[1440,2880]{1,0:T(8,128)(2,1)} %collective-permute-done.8.gu1, ...), custom_call_target="tpu_custom_call" | custom-call | flops 6370099200 | bytes 24883200 | tf_op jit(solution)/shard_map/pallas_call | solution.py:300
  134.6 1.5 collective-permute-start.24
  136.1 0.2 add_convert_fusion.3
  136.3 2.1 %collective-permute-start.21 = (bf16[2880,128]{1,0:T(8,128)(2,1)S(1)}, bf16[2880,128]{1,0:T(8,128)(2,1)S(1)}, u32[]{:S(2)}, u32[]{:S(2)}) collective-permute-start(bf16[2880,128]{1,0:T(8,128)(2,1)S(1)} %add_convert_fusion.3), channel_id=1, source_target_pairs={{0,8},{1,9},{2,10},{3,11},{4,0},{5,1},{6,2},{7,3},{8,12},{9,13},{1... | collective-permute-start | bytes 2211848 | tf_op jit(solution)/shard_map/ppermute | solution.py:492
  138.4 0.2 add_convert_fusion.1
  138.7 12.8 %collective-permute-done.24 = bf16[2880,128]{1,0:T(8,128)(2,1)S(1)} collective-permute-done((bf16[2880,128]{1,0:T(8,128)(2,1)}, bf16[2880,128]{1,0:T(8,128)(2,1)S(1)}, u32[]{:S(2)}, u32[]{:S(2)}) %collective-permute-start.24) | collective-permute-done | bytes 737312 | tf_op jit(solution)/shard_map/ppermute | solution.py:482
  151.6 1.4 collective-permute-start.27
  153.1 4.6 %collective-permute-start.26 = (bf16[2880,128]{1,0:T(8,128)(2,1)S(1)}, bf16[2880,128]{1,0:T(8,128)(2,1)S(1)}, u32[]{:S(2)}, u32[]{:S(2)}) collective-permute-start(bf16[2880,128]{1,0:T(8,128)(2,1)S(1)} %add_convert_fusion.2), channel_id=1, source_target_pairs={{0,12},{1,13},{2,14},{3,15},{8,0},{9,1},{10,2},{11,3},{16,28},{17,... | collective-permute-start | bytes 2211848 | tf_op jit(solution)/shard_map/ppermute | solution.py:499
  157.7 1.3 collective-permute-start.25
  159.1 6.4 %collective-permute-done.27 = bf16[2880,128]{1,0:T(8,128)(2,1)S(1)} collective-permute-done((bf16[2880,128]{1,0:T(8,128)(2,1)S(1)}, bf16[2880,128]{1,0:T(8,128)(2,1)S(1)}, u32[]{:S(2)}, u32[]{:S(2)}) %collective-permute-start.27) | collective-permute-done | bytes 737312 | tf_op jit(solution)/shard_map/ppermute | solution.py:496
  165.4 19.3 %collective-permute-done.26 = bf16[2880,128]{1,0:T(8,128)(2,1)S(1)} collective-permute-done((bf16[2880,128]{1,0:T(8,128)(2,1)S(1)}, bf16[2880,128]{1,0:T(8,128)(2,1)S(1)}, u32[]{:S(2)}, u32[]{:S(2)}) %collective-permute-start.26) | collective-permute-done | bytes 737312 | tf_op jit(solution)/shard_map/ppermute | solution.py:499
  184.7 1.6 fusion
  (51 shorter events, 0.5 us)
Async XLA Ops:
  0.0 19.4 %copy-start.11 = (bf16[128,2048]{1,0:T(8,128)(2,1)S(1)}, bf16[128,2048]{1,0:T(8,128)(2,1)}, u32[]{:S(2)}) copy-start(bf16[128,2048]{1,0:T(8,128)(2,1)} %param.11) | copy-start | bytes 1572868
  1.8 5.4 %collective-permute-start.2 = (bf16[16,512]{1,0:T(8,128)(2,1)}, bf16[16,512]{1,0:T(8,128)(2,1)S(1)}, u32[]{:S(2)}, u32[]{:S(2)}) collective-permute-start(bf16[16,512]{1,0:T(8,128)(2,1)} %get-tuple-element.39), channel_id=1, source_target_pairs={{0,3},{1,2},{2,1},{3,0},{4,7},{5,6},{6,5},{7,4},{8,11},{9,10},{10,... | collective-permute-start | bytes 49160 | tf_op jit(solution)/shard_map/ppermute | solution.py:77
  4.2 3.9 %collective-permute-start.1 = (bf16[16,512]{1,0:T(8,128)(2,1)}, bf16[16,512]{1,0:T(8,128)(2,1)S(1)}, u32[]{:S(2)}, u32[]{:S(2)}) collective-permute-start(bf16[16,512]{1,0:T(8,128)(2,1)} %get-tuple-element.39), channel_id=1, source_target_pairs={{0,2},{1,3},{2,0},{3,1},{4,6},{5,7},{6,4},{7,5},{8,10},{9,11},{10,... | collective-permute-start | bytes 49160 | tf_op jit(solution)/shard_map/ppermute | solution.py:77
  4.8 3.4 %collective-permute-start = (bf16[16,512]{1,0:T(8,128)(2,1)}, bf16[16,512]{1,0:T(8,128)(2,1)S(1)}, u32[]{:S(2)}, u32[]{:S(2)}) collective-permute-start(bf16[16,512]{1,0:T(8,128)(2,1)} %get-tuple-element.39), channel_id=1, source_target_pairs={{0,1},{1,0},{2,3},{3,2},{4,5},{5,4},{6,7},{7,6},{8,9},{9,8},{10,11... | collective-permute-start | bytes 49160 | tf_op jit(solution)/shard_map/ppermute | solution.py:77
  4.9 4.0 %collective-permute-start.3 = (bf16[128,512]{1,0:T(8,128)(2,1)}, bf16[128,512]{1,0:T(8,128)(2,1)S(1)}, u32[]{:S(2)}, u32[]{:S(2)}) collective-permute-start(bf16[128,512]{1,0:T(8,128)(2,1)} %get-tuple-element.40.local), channel_id=1, source_target_pairs={{0,1},{1,2},{2,3},{3,4},{4,5},{5,6},{6,7},{7,8},{8,9},{9,10},{10,1... | collective-permute-start | bytes 393224 | tf_op jit(solution)/shard_map/ppermute | solution.py:400
  8.9 13.0 %copy-start.12 = (bf16[128,512]{1,0:T(8,128)(2,1)}, bf16[128,512]{1,0:T(8,128)(2,1)S(1)}, u32[]{:S(2)}) copy-start(bf16[128,512]{1,0:T(8,128)(2,1)S(1)} %collective-permute-done.3.halo) | copy-start | bytes 393220
  8.9 48.7 %collective-permute-start.8 = (bf16[1440,2880]{1,0:T(8,128)(2,1)}, bf16[1440,2880]{1,0:T(8,128)(2,1)}, u32[]{:S(2)}, u32[]{:S(2)}) collective-permute-start(bf16[1440,2880]{1,0:T(8,128)(2,1)} %bitcast.13), channel_id=1, source_target_pairs={{0,1},{1,0},{2,3},{3,2},{4,5},{5,4},{6,7},{7,6},{8,9},{9,8},{10,11... | collective-permute-start | bytes 24883208 | tf_op jit(solution)/shard_map/ppermute | solution.py:408
  10.9 46.7 %collective-permute-start.9 = (bf16[720,2880]{1,0:T(8,128)(2,1)}, bf16[720,2880]{1,0:T(8,128)(2,1)}, u32[]{:S(2)}, u32[]{:S(2)}) collective-permute-start(bf16[720,2880]{1,0:T(8,128)(2,1)} %bitcast.18), channel_id=1, source_target_pairs={{0,1},{1,0},{2,3},{3,2},{4,5},{5,4},{6,7},{7,6},{8,9},{9,8},{10,11... | collective-permute-start | bytes 12441608 | tf_op jit(solution)/shard_map/ppermute | solution.py:409
  10.9 9.5 %collective-permute-start.6 = (bf16[16,512]{1,0:T(8,128)(2,1)S(1)}, bf16[16,512]{1,0:T(8,128)(2,1)S(1)}, u32[]{:S(2)}, u32[]{:S(2)}) collective-permute-start(bf16[16,512]{1,0:T(8,128)(2,1)S(1)} %add_add_fusion.1), channel_id=1, source_target_pairs={{0,12},{1,13},{2,14},{3,15},{4,8},{5,9},{6,10},{7,11},{8,4},{9,5},... | collective-permute-start | bytes 49160 | tf_op jit(solution)/shard_map/ppermute | solution.py:77
  16.6 4.6 %collective-permute-start.5 = (bf16[16,512]{1,0:T(8,128)(2,1)S(1)}, bf16[16,512]{1,0:T(8,128)(2,1)S(1)}, u32[]{:S(2)}, u32[]{:S(2)}) collective-permute-start(bf16[16,512]{1,0:T(8,128)(2,1)S(1)} %add_add_fusion.1), channel_id=1, source_target_pairs={{0,8},{1,9},{2,10},{3,11},{4,12},{5,13},{6,14},{7,15},{8,0},{9,1},... | collective-permute-start | bytes 49160 | tf_op jit(solution)/shard_map/ppermute | solution.py:77
  16.6 4.6 %collective-permute-start.4 = (bf16[16,512]{1,0:T(8,128)(2,1)S(1)}, bf16[16,512]{1,0:T(8,128)(2,1)S(1)}, u32[]{:S(2)}, u32[]{:S(2)}) collective-permute-start(bf16[16,512]{1,0:T(8,128)(2,1)S(1)} %add_add_fusion.1), channel_id=1, source_target_pairs={{0,4},{1,5},{2,6},{3,7},{4,0},{5,1},{6,2},{7,3},{8,12},{9,13},{10,... | collective-permute-start | bytes 49160 | tf_op jit(solution)/shard_map/ppermute | solution.py:77
  31.5 18.3 %collective-permute-start.10 = (bf16[2896,128]{1,0:T(8,128)(2,1)}, bf16[2896,128]{1,0:T(8,128)(2,1)S(1)}, u32[]{:S(2)}, u32[]{:S(2)}) collective-permute-start(bf16[2896,128]{1,0:T(8,128)(2,1)} %get-tuple-element.46.x_ref), channel_id=1, source_target_pairs={{0,4},{1,5},{2,6},{3,7},{4,8},{5,9},{6,10},{7,11},{8,12},{9,13},{1... | collective-permute-start | bytes 2224136 | tf_op jit(solution)/shard_map/ppermute | solution.py:359
  34.1 19.8 %collective-permute-start.11 = (bf16[2896,128]{1,0:T(8,128)(2,1)}, bf16[2896,128]{1,0:T(8,128)(2,1)S(1)}, u32[]{:S(2)}, u32[]{:S(2)}) collective-permute-start(bf16[2896,128]{1,0:T(8,128)(2,1)} %get-tuple-element.46.x_ref), channel_id=1, source_target_pairs={{4,0},{5,1},{6,2},{7,3},{8,4},{9,5},{10,6},{11,7},{12,8},{13,9},{1... | collective-permute-start | bytes 2224136 | tf_op jit(solution)/shard_map/ppermute | solution.py:360
  35.4 18.6 %collective-permute-start.7 = (bf16[2896,128]{1,0:T(8,128)(2,1)}, bf16[2896,128]{1,0:T(8,128)(2,1)S(1)}, u32[]{:S(2)}, u32[]{:S(2)}) collective-permute-start(bf16[2896,128]{1,0:T(8,128)(2,1)} %get-tuple-element.46.x_ref), channel_id=1, source_target_pairs={{0,2},{1,3},{2,0},{3,1},{4,6},{5,7},{6,4},{7,5},{8,10},{9,11},{10,... | collective-permute-start | bytes 2224136 | tf_op jit(solution)/shard_map/ppermute | solution.py:434
  54.0 17.8 %copy-start = (bf16[2896,128]{1,0:T(8,128)(2,1)}, bf16[2896,128]{1,0:T(8,128)(2,1)S(1)}, u32[]{:S(2)}) copy-start(bf16[2896,128]{1,0:T(8,128)(2,1)S(1)} %broadcast_select_fusion.2.x_ref) | copy-start | bytes 2224132
  54.0 3.5 %copy-start.7 = (bf16[2896,128]{1,0:T(8,128)(2,1)}, bf16[2896,128]{1,0:T(8,128)(2,1)S(1)}, u32[]{:S(2)}) copy-start(bf16[2896,128]{1,0:T(8,128)(2,1)S(1)} %collective-permute-done.7.y_ref) | copy-start | bytes 2224132
  54.0 17.8 %collective-permute-start.12 = (bf16[2896,128]{1,0:T(8,128)(2,1)S(1)}, bf16[2896,128]{1,0:T(8,128)(2,1)}, u32[]{:S(2)}, u32[]{:S(2)}) collective-permute-start(bf16[2896,128]{1,0:T(8,128)(2,1)S(1)} %broadcast_select_fusion.2.x_ref), channel_id=1, source_target_pairs={{0,2},{1,3},{2,0},{3,1},{4,6},{5,7},{6,4},{7,5},{8,10},{9,11},{10,... | collective-permute-start | bytes 2224136 | tf_op jit(solution)/shard_map/ppermute | solution.py:440
  54.7 17.1 %collective-permute-start.13 = (bf16[2896,128]{1,0:T(8,128)(2,1)S(1)}, bf16[2896,128]{1,0:T(8,128)(2,1)}, u32[]{:S(2)}, u32[]{:S(2)}) collective-permute-start(bf16[2896,128]{1,0:T(8,128)(2,1)S(1)} %collective-permute-done.10), channel_id=1, source_target_pairs={{4,8},{5,9},{6,10},{7,11},{8,12},{9,13},{10,14},{11,15},{20,24},{2... | collective-permute-start | bytes 2224136 | tf_op jit(solution)/shard_map/ppermute | solution.py:359
  56.2 20.5 %collective-permute-start.14 = (bf16[2896,128]{1,0:T(8,128)(2,1)S(1)}, bf16[2896,128]{1,0:T(8,128)(2,1)}, u32[]{:S(2)}, u32[]{:S(2)}) collective-permute-start(bf16[2896,128]{1,0:T(8,128)(2,1)S(1)} %collective-permute-done.11), channel_id=1, source_target_pairs={{4,0},{5,1},{6,2},{7,3},{8,4},{9,5},{10,6},{11,7},{20,16},{21,17},... | collective-permute-start | bytes 2224136 | tf_op jit(solution)/shard_map/ppermute | solution.py:360
  78.2 16.7 %copy-start.2 = (bf16[2896,128]{1,0:T(8,128)(2,1)}, bf16[2896,128]{1,0:T(8,128)(2,1)S(1)}, u32[]{:S(2)}) copy-start(bf16[2896,128]{1,0:T(8,128)(2,1)S(1)} %get-tuple-element.56.x_ref) | copy-start | bytes 2224132
  78.2 16.7 %collective-permute-start.15 = (bf16[2896,128]{1,0:T(8,128)(2,1)S(1)}, bf16[2896,128]{1,0:T(8,128)(2,1)S(1)}, u32[]{:S(2)}, u32[]{:S(2)}) collective-permute-start(bf16[2896,128]{1,0:T(8,128)(2,1)S(1)} %get-tuple-element.56.x_ref), channel_id=1, source_target_pairs={{0,2},{1,3},{2,0},{3,1},{4,6},{5,7},{6,4},{7,5},{8,10},{9,11},{10,... | collective-permute-start | bytes 2224136 | tf_op jit(solution)/shard_map/ppermute | solution.py:440
  79.7 16.8 %collective-permute-start.16 = (bf16[2896,128]{1,0:T(8,128)(2,1)S(1)}, bf16[2896,128]{1,0:T(8,128)(2,1)S(1)}, u32[]{:S(2)}, u32[]{:S(2)}) collective-permute-start(bf16[2896,128]{1,0:T(8,128)(2,1)S(1)} %get-tuple-element.57), channel_id=1, source_target_pairs={{8,12},{9,13},{10,14},{11,15},{4,0},{5,1},{6,2},{7,3},{24,28},{25,... | collective-permute-start | bytes 2224136 | tf_op jit(solution)/shard_map/ppermute | solution.py:356
  94.9 10.2 %copy-start.8 = (bf16[2896,128]{1,0:T(8,128)(2,1)}, bf16[2896,128]{1,0:T(8,128)(2,1)S(1)}, u32[]{:S(2)}) copy-start(bf16[2896,128]{1,0:T(8,128)(2,1)S(1)} %collective-permute-done.15.y_ref) | copy-start | bytes 2224132
  96.6 22.5 %copy-start.1 = (bf16[2896,128]{1,0:T(8,128)(2,1)}, bf16[2896,128]{1,0:T(8,128)(2,1)S(1)}, u32[]{:S(2)}) copy-start(bf16[2896,128]{1,0:T(8,128)(2,1)S(1)} %broadcast_select_fusion.x_ref) | copy-start | bytes 2224132
  96.6 22.5 %collective-permute-start.19 = (bf16[2896,128]{1,0:T(8,128)(2,1)S(1)}, bf16[2896,128]{1,0:T(8,128)(2,1)S(1)}, u32[]{:S(2)}, u32[]{:S(2)}) collective-permute-start(bf16[2896,128]{1,0:T(8,128)(2,1)S(1)} %broadcast_select_fusion.x_ref), channel_id=1, source_target_pairs={{0,2},{1,3},{2,0},{3,1},{4,6},{5,7},{6,4},{7,5},{8,10},{9,11},{10,... | collective-permute-start | bytes 2224136 | tf_op jit(solution)/shard_map/ppermute | solution.py:440
  97.3 21.8 %collective-permute-start.17 = (bf16[2880,128]{1,0:T(8,128)(2,1)}, bf16[2880,128]{1,0:T(8,128)(2,1)S(1)}, u32[]{:S(2)}, u32[]{:S(2)}) collective-permute-start(bf16[2880,128]{1,0:T(8,128)(2,1)} %get-tuple-element.58), channel_id=1, source_target_pairs={{0,4},{1,5},{2,6},{3,7},{4,8},{5,9},{6,10},{7,11},{16,20},{17,21},... | collective-permute-start | bytes 2211848 | tf_op jit(solution)/shard_map/ppermute | solution.py:463
  100.3 18.8 %collective-permute-start.18 = (bf16[2880,128]{1,0:T(8,128)(2,1)}, bf16[2880,128]{1,0:T(8,128)(2,1)S(1)}, u32[]{:S(2)}, u32[]{:S(2)}) collective-permute-start(bf16[2880,128]{1,0:T(8,128)(2,1)} %get-tuple-element.58), channel_id=1, source_target_pairs={{8,4},{9,5},{10,6},{11,7},{12,8},{13,9},{14,10},{15,11},{24,20},{2... | collective-permute-start | bytes 2211848 | tf_op jit(solution)/shard_map/ppermute | solution.py:463
  101.0 33.6 %collective-permute-start.23 = (bf16[2880,128]{1,0:T(8,128)(2,1)}, bf16[2880,128]{1,0:T(8,128)(2,1)S(1)}, u32[]{:S(2)}, u32[]{:S(2)}) collective-permute-start(bf16[2880,128]{1,0:T(8,128)(2,1)} %get-tuple-element.67), channel_id=1, source_target_pairs={{8,4},{9,5},{10,6},{11,7},{12,8},{13,9},{14,10},{15,11},{24,20},{2... | collective-permute-start | bytes 2211848 | tf_op jit(solution)/shard_map/ppermute | solution.py:463
  101.8 32.8 %collective-permute-start.22 = (bf16[2880,128]{1,0:T(8,128)(2,1)}, bf16[2880,128]{1,0:T(8,128)(2,1)S(1)}, u32[]{:S(2)}, u32[]{:S(2)}) collective-permute-start(bf16[2880,128]{1,0:T(8,128)(2,1)} %get-tuple-element.67), channel_id=1, source_target_pairs={{0,4},{1,5},{2,6},{3,7},{4,8},{5,9},{6,10},{7,11},{16,20},{17,21},... | collective-permute-start | bytes 2211848 | tf_op jit(solution)/shard_map/ppermute | solution.py:463
  119.1 1.5 copy-start.9
  119.2 17.0 %copy-start.6 = (f32[2880,128]{1,0:T(8,128)S(1)}, f32[2880,128]{1,0:T(8,128)}, u32[]{:S(2)}) copy-start(f32[2880,128]{1,0:T(8,128)} %get-tuple-element.59) | copy-start | bytes 4423684
  119.2 15.4 %collective-permute-start.20 = (bf16[2880,128]{1,0:T(8,128)(2,1)}, bf16[2880,128]{1,0:T(8,128)(2,1)S(1)}, u32[]{:S(2)}, u32[]{:S(2)}) collective-permute-start(bf16[2880,128]{1,0:T(8,128)(2,1)} %get-tuple-element.63), channel_id=1, source_target_pairs={{0,2},{1,3},{2,0},{3,1},{4,6},{5,7},{6,4},{7,5},{8,10},{9,11},{10,... | collective-permute-start | bytes 2211848 | tf_op jit(solution)/shard_map/ppermute | solution.py:482
  134.6 16.9 %collective-permute-start.24 = (bf16[2880,128]{1,0:T(8,128)(2,1)}, bf16[2880,128]{1,0:T(8,128)(2,1)S(1)}, u32[]{:S(2)}, u32[]{:S(2)}) collective-permute-start(bf16[2880,128]{1,0:T(8,128)(2,1)} %get-tuple-element.70), channel_id=1, source_target_pairs={{0,2},{1,3},{2,0},{3,1},{4,6},{5,7},{6,4},{7,5},{8,10},{9,11},{10,... | collective-permute-start | bytes 2211848 | tf_op jit(solution)/shard_map/ppermute | solution.py:482
  136.1 2.3 %copy-start.4 = (f32[2880,128]{1,0:T(8,128)S(1)}, f32[2880,128]{1,0:T(8,128)}, u32[]{:S(2)}) copy-start(f32[2880,128]{1,0:T(8,128)} %get-tuple-element.71) | copy-start | bytes 4423684
  136.3 22.7 %collective-permute-start.21 = (bf16[2880,128]{1,0:T(8,128)(2,1)S(1)}, bf16[2880,128]{1,0:T(8,128)(2,1)S(1)}, u32[]{:S(2)}, u32[]{:S(2)}) collective-permute-start(bf16[2880,128]{1,0:T(8,128)(2,1)S(1)} %add_convert_fusion.3), channel_id=1, source_target_pairs={{0,8},{1,9},{2,10},{3,11},{4,0},{5,1},{6,2},{7,3},{8,12},{9,13},{1... | collective-permute-start | bytes 2211848 | tf_op jit(solution)/shard_map/ppermute | solution.py:492
  138.4 14.6 %copy-start.5 = (f32[2880,128]{1,0:T(8,128)S(1)}, f32[2880,128]{1,0:T(8,128)}, u32[]{:S(2)}) copy-start(f32[2880,128]{1,0:T(8,128)} %get-tuple-element.64) | copy-start | bytes 4423684
  138.7 46.0 %copy-start.3 = (f32[2880,128]{1,0:T(8,128)S(1)}, f32[2880,128]{1,0:T(8,128)}, u32[]{:S(2)}) copy-start(f32[2880,128]{1,0:T(8,128)} %get-tuple-element.49) | copy-start | bytes 4423684
  138.7 46.0 %copy-start.10 = (bf16[2880,128]{1,0:T(8,128)(2,1)S(1)}, bf16[2880,128]{1,0:T(8,128)(2,1)}, u32[]{:S(2)}) copy-start(bf16[2880,128]{1,0:T(8,128)(2,1)} %get-tuple-element.45) | copy-start | bytes 2211844
  151.6 13.9 %collective-permute-start.27 = (bf16[2880,128]{1,0:T(8,128)(2,1)S(1)}, bf16[2880,128]{1,0:T(8,128)(2,1)S(1)}, u32[]{:S(2)}, u32[]{:S(2)}) collective-permute-start(bf16[2880,128]{1,0:T(8,128)(2,1)S(1)} %add_convert_fusion.1), channel_id=1, source_target_pairs={{0,2},{1,3},{2,0},{3,1},{4,6},{5,7},{6,4},{7,5},{8,10},{9,11},{10,... | collective-permute-start | bytes 2211848 | tf_op jit(solution)/shard_map/ppermute | solution.py:496
  153.1 31.6 %collective-permute-start.26 = (bf16[2880,128]{1,0:T(8,128)(2,1)S(1)}, bf16[2880,128]{1,0:T(8,128)(2,1)S(1)}, u32[]{:S(2)}, u32[]{:S(2)}) collective-permute-start(bf16[2880,128]{1,0:T(8,128)(2,1)S(1)} %add_convert_fusion.2), channel_id=1, source_target_pairs={{0,12},{1,13},{2,14},{3,15},{8,0},{9,1},{10,2},{11,3},{16,28},{17,... | collective-permute-start | bytes 2211848 | tf_op jit(solution)/shard_map/ppermute | solution.py:499
  157.7 27.0 %collective-permute-start.25 = (bf16[2880,128]{1,0:T(8,128)(2,1)S(1)}, bf16[2880,128]{1,0:T(8,128)(2,1)S(1)}, u32[]{:S(2)}, u32[]{:S(2)}) collective-permute-start(bf16[2880,128]{1,0:T(8,128)(2,1)S(1)} %add_convert_fusion.2), channel_id=1, source_target_pairs={{4,12},{5,13},{6,14},{7,15},{12,0},{13,1},{14,2},{15,3},{20,28},{2... | collective-permute-start | bytes 2211848 | tf_op jit(solution)/shard_map/ppermute | solution.py:499
